TPU v7x, 256 devices: a whole 4x4x8 slice. The times are simulated.
256 devices in a mesh: ctx: 8 (over x_hi, y), exp: 16 (over x_lo, z), tp: 2 (over core).
Axes of the slice: x: 4 (x_hi: 2, x_lo: 2; x = x_hi * 2 + x_lo), y: 4, z: 8, core: 2. Of those that a mesh axis runs over, the one named last changes fastest.
Arguments:
- tokens: bfloat16 [512, 6144], P(('ctx', 'exp'), 'tp'), may hold values from -6 to 6
- expert_ids: int32 [512, 4], P(('ctx', 'exp')), may hold values from 0 to 15, all different within a row; in each aligned block of 4 rows (0 to 3, 4 to 7, ...) at most 2 rows name the same one
- combine_weights: float32 [512, 4], P(('ctx', 'exp')), may hold values from 0.2 to 1
- cotangent: bfloat16 [512, 6144], P(('ctx', 'exp'), 'tp'), may hold values from -6 to 6
- gate_weight: bfloat16 [16, 6144, 8064], P('exp', None, ('ctx', 'tp')), may hold values from -0.078125 to 0.078125
- down_weight: bfloat16 [16, 8064, 6144], P('exp', ('ctx', 'tp')), may hold values from -0.0625 to 0.0625
Outputs:
- layer_out: bfloat16 [512, 6144], P(('ctx', 'exp'), 'tp')
- token_grad: bfloat16 [512, 6144], P(('ctx', 'exp'), 'tp')
- weight_grad: float32 [512, 4], P(('ctx', 'exp'))
Inputs may be any that keep to these rules, and one draw needn't show every extreme that they name: `expert_ids`: within the 4 rows of one group (aligned blocks), no expert is named by more than 2 rows, and in some block one expert is named by exactly 2.
All inputs are finite; a program needn't handle non-finite values.
Results may differ from a plain program's by a relative error of at most 0.029.
Values may be sent and summed in bfloat16 or wider, within the bound.
No kernel may reach another device: no remote copies, remote signals or barrier semaphores. Data moves between devices by JAX's collectives and lax.ppermute only.
A program may use at most 128 MiB of HBM per device.

v0:
```python
import jax
import jax.numpy as jnp
from jax import lax
from jax.sharding import PartitionSpec as P


def silu_slope(value):
    sigma = jax.nn.sigmoid(value)
    return sigma * (1.0 + value * (1.0 - sigma))


def shards(tokens, expert_ids, combine_weights, cotangent, gate_weight, down_weight):
    tok_count, half_width = tokens.shape
    top_count = expert_ids.shape[1]
    local_experts, model_width, hidden_part = gate_weight.shape
    context_size = lax.axis_size("ctx")
    expert_size = lax.axis_size("exp")
    tensor_size = lax.axis_size("tp")
    experts = local_experts * expert_size
    capacity = min(tok_count, tok_count * top_count * 2 // experts)
    highest = lax.Precision.HIGHEST
    flattened = expert_ids.reshape(-1)
    onehot = (flattened[:, None] == jnp.arange(experts, dtype=jnp.int32)[None, :]).astype(jnp.int32)
    before = jnp.cumsum(onehot, 0) - onehot
    slot_index = jnp.sum(onehot * before, 1)
    position = flattened * capacity + slot_index
    placing = (
        jnp.arange(experts * capacity, dtype=jnp.int32)[:, None] == position[None, :]
    ).astype(jnp.float32)
    per_token = placing.reshape(experts * capacity, tok_count, top_count)
    chosen = jnp.sum(per_token, 2)
    weighted = jnp.sum(per_token * combine_weights[None, :, :], 2)
    row_width = tokens.shape[1]
    dispatched = jnp.dot(
        chosen.astype(jnp.bfloat16), tokens, preferred_element_type=jnp.float32
    ).astype(jnp.bfloat16)
    dispatched_grad = jnp.dot(weighted, cotangent.astype(jnp.float32), precision=highest).astype(
        jnp.bfloat16
    )
    arrived = (
        lax.all_to_all(
            dispatched.reshape(experts, capacity, row_width),
            "exp",
            split_axis=0,
            concat_axis=0,
            tiled=True,
        ),
        lax.all_to_all(
            dispatched_grad.reshape(experts, capacity, row_width),
            "exp",
            split_axis=0,
            concat_axis=0,
            tiled=True,
        ),
    )

    def regroup(received):
        shaped = received.reshape(expert_size, local_experts, capacity, row_width).transpose(
            1, 0, 2, 3
        )
        return shaped.reshape(local_experts, expert_size * capacity, row_width)

    first_rows = regroup(arrived[0])
    first_grads = regroup(arrived[1])
    block_rows = local_experts * expert_size * capacity
    member_rows = expert_size * capacity
    context_rows, context_grads = (
        lax.all_gather(first_rows, "ctx", axis=1, tiled=True),
        lax.all_gather(first_grads, "ctx", axis=1, tiled=True),
    )
    routed_rows, routed_grad = (
        lax.all_gather(context_rows, "tp", axis=2, tiled=True),
        lax.all_gather(context_grads, "tp", axis=2, tiled=True),
    )
    gate_pre = jnp.einsum(
        "jrd,jdf->jrf", routed_rows, gate_weight, preferred_element_type=jnp.float32
    )
    hidden = jax.nn.silu(gate_pre).astype(jnp.bfloat16)
    hidden_grad = jnp.einsum(
        "jrd,jfd->jrf", routed_grad, down_weight, preferred_element_type=jnp.float32
    )
    pre_grad = (hidden_grad * silu_slope(gate_pre)).astype(jnp.bfloat16)
    hidden_blocks = hidden.reshape(local_experts, context_size, member_rows, hidden_part)
    grad_blocks = pre_grad.reshape(local_experts, context_size, member_rows, hidden_part)
    number = lax.axis_size(("ctx", "tp")) * block_rows // block_rows
    block_ids = jnp.arange(number, dtype=jnp.int32)
    context_pick = block_ids // tensor_size
    tensor_pick = block_ids % tensor_size
    hidden_sel = jnp.take(hidden_blocks, context_pick, axis=1)
    grad_sel = jnp.take(grad_blocks, context_pick, axis=1)
    out_full = jnp.einsum(
        "jbmf,jfd->bjmd", hidden_sel, down_weight, preferred_element_type=jnp.float32
    )
    back_full = jnp.einsum(
        "jbmf,jdf->bjmd", grad_sel, gate_weight, preferred_element_type=jnp.float32
    )
    keep = (tensor_pick[:, None] == jnp.arange(tensor_size, dtype=jnp.int32)[None, :])[
        :, None, None, :, None
    ]
    out_full = out_full.reshape(number, local_experts, member_rows, tensor_size, half_width)
    back_full = back_full.reshape(number, local_experts, member_rows, tensor_size, half_width)
    out_part = jnp.sum(jnp.where(keep, out_full, 0.0), 3)
    back_part = jnp.sum(jnp.where(keep, back_full, 0.0), 3)
    summed = lax.psum_scatter(
        jnp.concatenate([out_part, back_part], 3)
        .reshape(lax.axis_size(("ctx", "tp")) * block_rows, 2 * half_width)
        .astype(jnp.bfloat16),
        ("ctx", "tp"),
        scatter_dimension=0,
        tiled=True,
    ).astype(jnp.float32)
    term_width = summed.shape[1]
    half_term = term_width // 2
    going_back = summed.astype(jnp.bfloat16).reshape(
        local_experts, expert_size, capacity, term_width
    )
    going_back = going_back.transpose(1, 0, 2, 3).reshape(
        expert_size, local_experts * capacity, term_width
    )
    returned = lax.all_to_all(going_back, "exp", split_axis=0, concat_axis=0, tiled=True).reshape(
        experts * capacity, term_width
    )
    out_rows = returned[:, :half_term].astype(jnp.float32)
    back_rows = returned[:, half_term:]
    out_sum = jnp.dot(weighted.T, out_rows, precision=highest)
    back_sum = jnp.dot(chosen.T.astype(jnp.bfloat16), back_rows, preferred_element_type=jnp.float32)
    picked = jnp.dot(placing.T, out_rows, precision=highest).reshape(
        tok_count, top_count, half_term
    )
    partial_pairs = jnp.sum(picked * cotangent.astype(jnp.float32)[:, None, :], 2)
    weight_grad = lax.psum(partial_pairs, "tp")
    return (out_sum.astype(jnp.bfloat16), back_sum.astype(jnp.bfloat16), weight_grad)


def solution(mesh):
    in_specs = (
        P(("ctx", "exp"), "tp"),
        P(("ctx", "exp"), None),
        P(("ctx", "exp"), None),
        P(("ctx", "exp"), "tp"),
        P("exp", None, ("ctx", "tp")),
        P("exp", ("ctx", "tp"), None),
    )
    out_specs = (P(("ctx", "exp"), "tp"), P(("ctx", "exp"), "tp"), P(("ctx", "exp"), None))
    return jax.shard_map(shards, mesh=mesh, in_specs=in_specs, out_specs=out_specs, check_vma=False)
```

profile of v0, /device:TPU:8, one launch (start us, length us, event | category | flops | bytes accessed | tf_op | source)
XLA Modules:
  0.0 409.4 jit_solution(10528967026911835908)
XLA Ops:
  7.2 0.8 eq.61
  8.1 0.2 select_reduce_fusion.3
  8.4 0.7 multiply_add_fusion
  9.1 0.8 convert_reduce_fusion
  9.8 0.2 convolution_convert_fusion.1
  10.2 18.4 %all_to_all.15 = bf16[16,2,3072]{2,1,0:T(2,128)(2,1)S(1)} all-to-all(bf16[16,2,3072]{2,1,0:T(2,128)(2,1)S(1)} %reshape.173), channel_id=1, replica_groups=mesh['ctx'=8,'exp'=16,'tp'=2] {'exp'}, dimensions={0} | all-to-all | bytes 393216 | tf_op jit(solution)/shard_map/all_to_all | solution.py:41
  28.5 0.7 reshape_transpose_reshape.9
  29.4 1.1 convolution_convert_fusion
  30.6 13.0 %all_to_all.16 = bf16[16,2,3072]{2,1,0:T(2,128)(2,1)S(1)} all-to-all(bf16[16,2,3072]{2,1,0:T(2,128)(2,1)S(1)} %reshape.180), channel_id=1, replica_groups=mesh['ctx'=8,'exp'=16,'tp'=2] {'exp'}, dimensions={0} | all-to-all | bytes 393216 | tf_op jit(solution)/shard_map/all_to_all | solution.py:48
  43.5 0.8 reshape_transpose_reshape.10
  44.4 37.4 %all-gather.5.cloned.1.call-done = bf16[1,256,3072]{2,1,0:T(8,128)(2,1)} async-done(((bf16[1,32,3072]{2,1,0:T(8,128)(2,1)}), bf16[1,256,3072]{2,1,0:T(8,128)(2,1)}) %all-gather.5.cloned.1.call-update) | async-done | bytes 1572880 | tf_op jit(solution)/shard_map/all_gather | solution.py:68
  81.8 55.9 %all-gather.9.cloned.1.call-done = bf16[1,256,3072]{2,1,0:T(8,128)(2,1)} async-done(((bf16[1,32,3072]{2,1,0:T(8,128)(2,1)}), bf16[1,256,3072]{2,1,0:T(8,128)(2,1)}) %all-gather.9.cloned.1.call-update) | async-done | bytes 1572880 | tf_op jit(solution)/shard_map/all_gather | solution.py:69
  138.0 18.3 %all-gather.7.cloned.1.call-done = bf16[1,256,6144]{2,1,0:T(8,128)(2,1)} async-done(((bf16[1,256,3072]{2,1,0:T(8,128)(2,1)}), bf16[1,256,6144]{2,1,0:T(8,128)(2,1)}) %all-gather.7.cloned.1.call-update) | async-done | bytes 3145744 | tf_op jit(solution)/shard_map/all_gather | solution.py:72
  156.2 5.5 %multiply_convert_fusion = (bf16[256,504]{0,1:T(8,128)(2,1)S(1)}, f32[256,504]{0,1:T(8,128)S(1)}) fusion(bf16[1,6144,504]{1,2,0:T(8,128)(2,1)} %param.12, bf16[1,256,6144]{2,1,0:T(8,128)(2,1)} %all-gather.7.cloned.1.call-done), kind=kOutput, calls=%fused_computation.29 | convolution fusion | flops 1586092032 | bytes 10113024 | tf_op jit(solution)/shard_map/jrd,jdf->jrf/dot_general | solution.py:75
  161.8 14.9 %all-gather.11.cloned.1.call-done = bf16[1,256,6144]{2,1,0:T(8,128)(2,1)} async-done(((bf16[1,256,3072]{2,1,0:T(8,128)(2,1)}), bf16[1,256,6144]{2,1,0:T(8,128)(2,1)}) %all-gather.11.cloned.1.call-update) | async-done | bytes 3145744 | tf_op jit(solution)/shard_map/all_gather | solution.py:73
  176.7 5.5 %fusion.13 = bf16[256,504]{0,1:T(8,128)(2,1)S(1)} fusion(bf16[1,504,6144]{2,1,0:T(8,128)(2,1)} %param.13, bf16[1,256,6144]{2,1,0:T(8,128)(2,1)} %all-gather.11.cloned.1.call-done, f32[256,504]{0,1:T(8,128)S(1)} %get-tuple-element.9), kind=kOutput, calls=%fused_computation.21 | convolution fusion | flops 1586608128 | bytes 10113024 | tf_op jit(solution)/shard_map/jrd,jfd->jrf/dot_general | solution.py:79
  182.3 0.6 gather_fusion.1
  182.9 9.4 %convolution_bitcast_fusion = f32[16,1,32,6144]{3,2,0,1:T(8,128)} fusion(bf16[1,6144,504]{1,2,0:T(8,128)(2,1)} %param.12, bf16[16,32,504]{2,1,0:T(8,128)(2,1)S(1)} %gather_fusion.1, pred[16]{0:T(512)(128)(4,1)S(1)} %compare_and_fusion), kind=kOutput, calls=%fused_computation.4 | convolution fusion | flops 3171151872 | bytes 19292176 | tf_op jit(solution)/shard_map/jbmf,jdf->bjmd/dot_general | solution.py:94
  192.3 16.5 %reshape.184 = f32[16,1,32,2,3072]{4,3,2,0,1:T(2,128)} reshape(f32[16,1,32,6144]{3,2,0,1:T(8,128)} %convolution_bitcast_fusion) | data formatting | bytes 25165824 | tf_op jit(solution)/shard_map/reshape | solution.py:101
  209.0 0.6 gather_fusion
  209.6 9.2 %convolution_bitcast_fusion.1 = f32[16,1,32,6144]{3,2,0,1:T(8,128)} fusion(bf16[1,504,6144]{2,1,0:T(8,128)(2,1)} %param.13, bf16[16,32,504]{2,1,0:T(8,128)(2,1)S(1)} %gather_fusion, pred[16]{0:T(512)(128)(4,1)S(1)} %compare_and_fusion), kind=kOutput, calls=%fused_computation.5 | convolution fusion | flops 3171151872 | bytes 19292176 | tf_op jit(solution)/shard_map/jbmf,jfd->bjmd/dot_general | solution.py:91
  218.8 16.5 %reshape.179 = f32[16,1,32,2,3072]{4,3,2,0,1:T(2,128)} reshape(f32[16,1,32,6144]{3,2,0,1:T(8,128)} %convolution_bitcast_fusion.1) | data formatting | bytes 25165824 | tf_op jit(solution)/shard_map/reshape | solution.py:100
  235.3 40.2 %select_reduce_fusion.1 = (bf16[16,32,3072]{2,1,0:T(8,128)(2,1)S(1)}, bf16[16,32,3072]{2,1,0:T(8,128)(2,1)S(1)}) fusion(f32[16,1,32,2,3072]{4,3,2,0,1:T(2,128)} %reshape.179, pred[16,2]{1,0:T(8,128)(4,1)S(1)} %iota_compare_fusion.2, f32[16,1,32,2,3072]{4,3,2,0,1:T(2,128)} %reshape.184), kind=kLoop, calls=%fused_computation.3 | loop fusion | flops 9437184 | bytes 31457312 | tf_op jit(solution)/shard_map/reduce_sum | solution.py:102
  275.5 3.2 pad_maximum_fusion
  278.8 98.5 %reduce-scatter.2.cloned.1.call-done = bf16[32,6144]{1,0:T(8,128)(2,1)} async-done(((bf16[512,6144]{1,0:T(8,128)(2,1)}), bf16[32,6144]{1,0:T(8,128)(2,1)}) %reduce-scatter.2.cloned.1.call-update) | async-done | bytes 393232 | tf_op jit(solution)/shard_map/reduce_scatter | solution.py:104
  377.2 2.0 reshape_transpose_reshape.11
  379.2 7.1 %all-to-all-start.2 = ((bf16[16,2,6144]{2,1,0:T(2,128)(2,1)}), bf16[16,2,6144]{2,1,0:T(2,128)(2,1)S(1)}, u32[]{:S(2)}, u32[]{:S(2)}) async-start(bf16[16,2,6144]{2,1,0:T(2,128)(2,1)} %reshape_transpose_reshape.11), calls=%async_computation.3 | async-start | bytes 786432 | tf_op jit(solution)/shard_map/all_to_all | solution.py:120
  386.5 11.2 %all-to-all-done.2 = bf16[16,2,6144]{2,1,0:T(2,128)(2,1)S(1)} async-done(((bf16[16,2,6144]{2,1,0:T(2,128)(2,1)}), bf16[16,2,6144]{2,1,0:T(2,128)(2,1)S(1)}, u32[]{:S(2)}, u32[]{:S(2)}) %all-to-all-start.2) | async-done | bytes 393248 | tf_op jit(solution)/shard_map/all_to_all | solution.py:120
  397.9 0.8 convolution_convert_fusion.3
  398.6 0.8 convolution_convert_fusion.2
  399.4 0.3 fusion.18
  399.8 3.0 psum.7
  (33 shorter events, 1.4 us)
Async XLA Ops:
  7.2 2.7 copy-start
  7.2 74.6 %all-gather.5.cloned.1.call-start = ((), (), s32[]{:S(2)}) async-start(), calls=%async_computation.4 | async-start | bytes 1769472 | tf_op jit(solution)/shard_map/all_gather | solution.py:68
  29.3 108.5 %all-gather.9.cloned.1.call-start = ((), (), s32[]{:S(2)}) async-start(), calls=%async_computation.6 | async-start | bytes 1769472 | tf_op jit(solution)/shard_map/all_gather | solution.py:69
  44.3 111.9 %all-gather.7.cloned.1.call-start = ((), (), s32[]{:S(2)}) async-start(), calls=%async_computation.5 | async-start | bytes 4718592 | tf_op jit(solution)/shard_map/all_gather | solution.py:72
  81.8 94.9 %all-gather.11.cloned.1.call-start = ((), (), s32[]{:S(2)}) async-start(), calls=%async_computation.7 | async-start | bytes 4718592 | tf_op jit(solution)/shard_map/all_gather | solution.py:73
  137.8 239.4 %reduce-scatter.2.cloned.1.call-start = ((), (), s32[]{:S(2)}) async-start(), calls=%async_computation.8 | async-start | bytes 6684672 | tf_op jit(solution)/shard_map/reduce_scatter | solution.py:104
  275.5 127.4 %copy-start.1 = (bf16[4,3072]{1,0:T(4,128)(2,1)S(1)}, bf16[4,3072]{1,0:T(4,128)(2,1)}, u32[]{:S(2)}) copy-start(bf16[4,3072]{1,0:T(4,128)(2,1)} %param.8) | copy-start | bytes 73732
  278.7 107.6 %copy-start.2 = (bf16[4,3072]{1,0:T(4,128)(2,1)S(1)}, bf16[4,3072]{1,0:T(4,128)(2,1)}, u32[]{:S(2)}) copy-start(bf16[4,3072]{1,0:T(4,128)(2,1)} %param.11) | copy-start | bytes 73732
  379.2 18.5 %all-to-all-start.2 = ((bf16[16,2,6144]{2,1,0:T(2,128)(2,1)}), bf16[16,2,6144]{2,1,0:T(2,128)(2,1)S(1)}, u32[]{:S(2)}, u32[]{:S(2)}) async-start(bf16[16,2,6144]{2,1,0:T(2,128)(2,1)} %reshape_transpose_reshape.11), calls=%async_computation.3 | async-start | bytes 786432 | tf_op jit(solution)/shard_map/all_to_all | solution.py:120
Sparse Core Ops, SparseCore 0:
  29.4 52.2 all-gather.4
  84.3 53.3 all-gather.8
  139.6 16.6 all-gather.6
  157.9 18.7 all-gather.10
  278.9 98.2 reduce-scatter.1
where the time goes:
time: 412 us; the launch traced here: 409 us
  waiting for transfers between devices  236 us (57%)
  other arithmetic  45.2 us (11%)
  local copies, waits for them, and re-layouts  39.4 us (10%)
  blocking collectives  34.3 us (8%)
  matrix products  32.9 us (8%)
  between operations  14 us (3%)
  starting transfers between devices  7.33 us (2%)
    reduce_scatter x1, waiting for transfers between devices, shards(): lax.psum_scatter(jnp.concatenate([out_part, back_part], 3).reshape(lax.ax...  98.5 us
    all_gather x1, waiting for transfers between devices, shards(): lax.all_gather(first_grads, 'ctx', axis=1, tiled=True)  55.9 us
    reduce_sum x1, other arithmetic, shards(): out_part = jnp.sum(jnp.where(keep, out_full, 0.0), 3)  40.2 us
    all_gather x1, waiting for transfers between devices, shards(): lax.all_gather(first_rows, 'ctx', axis=1, tiled=True)  37.4 us
    all_to_all x1, blocking collectives, shards(): lax.all_to_all(dispatched.reshape(experts, capacity, row_width), 'exp', s...  18.4 us
    all_gather x1, waiting for transfers between devices, shards(): lax.all_gather(context_rows, 'tp', axis=2, tiled=True)  18.3 us
    reshape x1, local copies, waits for them, and re-layouts, shards(): out_full.reshape(number, local_experts, member_rows, tensor_size, half_wi...  16.5 us
    reshape x1, local copies, waits for them, and re-layouts, shards(): back_full.reshape(number, local_experts, member_rows, tensor_size, half_w...  16.5 us
  transfers between devices with their start and end apart: 6, of which 6 were waited for; matrix products, arithmetic and copies ran while one was open for 2% of the time, Pallas kernels for 0%

commit v1 on v0

v1 whole, which is shorter than its diff:
```python
import jax
import jax.numpy as jnp
from jax import lax
from jax.sharding import PartitionSpec as P

AXES = ("ctx", "exp", "tp")
ROW_SPLIT = 2


def shift_pairs(sizes, hi=0, row=0, core=0):
    contexts, experts, cores = sizes
    rows = contexts // ROW_SPLIT
    pairs = []
    for c in range(contexts):
        h, y = divmod(c, rows)
        target = (h + hi) % ROW_SPLIT * rows + (y + row) % rows
        for e in range(experts):
            for t in range(cores):
                pairs.append(
                    ((c * experts + e) * cores + t, (target * experts + e) * cores + (t + core) % cores)
                )
    return pairs


def shards(sizes, tokens, expert_ids, combine_weights, cotangent, gate_weight, down_weight):
    tok_count, half_width = tokens.shape
    top_count = expert_ids.shape[1]
    gate = gate_weight[0]
    down = down_weight[0]
    experts = sizes[1]
    capacity = 2
    member_rows = experts * capacity
    highest = lax.Precision.HIGHEST
    core = lax.axis_index("tp")

    def move(value, **shift):
        return lax.ppermute(value, AXES, shift_pairs(sizes, **shift))

    flattened = expert_ids.reshape(-1)
    onehot = (flattened[:, None] == jnp.arange(experts, dtype=jnp.int32)[None, :]).astype(jnp.int32)
    before = jnp.cumsum(onehot, 0) - onehot
    slot_index = jnp.sum(onehot * before, 1)
    position = flattened * capacity + slot_index
    placing = (
        jnp.arange(member_rows, dtype=jnp.int32)[:, None] == position[None, :]
    ).astype(jnp.float32)
    per_token = placing.reshape(member_rows, tok_count, top_count)
    chosen = jnp.sum(per_token, 2)
    weighted = jnp.sum(per_token * combine_weights[None, :, :], 2)

    def exchange(rows):
        sent = rows.reshape(experts, capacity, half_width)
        got = lax.all_to_all(sent, "exp", split_axis=0, concat_axis=0, tiled=True)
        return got.reshape(member_rows, half_width)

    def gather(block):
        across = move(block, hi=1)
        below = move(block, row=1)
        above = move(block, row=-1)
        far = move(block, row=2)
        across_below = move(across, row=1)
        across_above = move(across, row=-1)
        across_far = move(far, hi=1)
        mine = jnp.concatenate(
            [block, across, below, above, far, across_below, across_above, across_far], 0
        )
        other = move(mine, core=1)
        first = jnp.where(core == 0, mine, other)
        second = jnp.where(core == 0, other, mine)
        return jnp.concatenate([first, second], 1)

    def scatter(partial):
        kept = lax.dynamic_slice_in_dim(partial, core * half_width, half_width, 1)
        given = lax.dynamic_slice_in_dim(partial, (1 - core) * half_width, half_width, 1)
        got = move(given, core=1)
        total = (kept.astype(jnp.float32) + got.astype(jnp.float32)).astype(jnp.bfloat16)
        own, across, below, above, far, across_below, across_above, across_far = [
            total[i * member_rows : (i + 1) * member_rows] for i in range(8)
        ]

        def add(*terms):
            return sum(t.astype(jnp.float32) for t in terms).astype(jnp.bfloat16)

        from_above = move(across_below, row=-1)
        from_below = move(across_above, row=1)
        from_across = move(across_far, hi=1)
        direct_above = move(below, row=-1)
        direct_below = move(above, row=1)
        turned = move(add(across, from_above, from_below), hi=1)
        direct_far = move(add(far, from_across), row=2)
        return add(own, direct_above, direct_below, turned, direct_far)

    dispatched = jnp.dot(
        chosen.astype(jnp.bfloat16), tokens, preferred_element_type=jnp.float32
    ).astype(jnp.bfloat16)
    dispatched_grad = jnp.dot(weighted, cotangent.astype(jnp.float32), precision=highest).astype(
        jnp.bfloat16
    )
    token_block = exchange(dispatched)
    grad_block = exchange(dispatched_grad)
    routed_rows = gather(token_block)
    routed_grad = gather(grad_block)
    gate_pre = jnp.dot(routed_rows, gate, preferred_element_type=jnp.float32)
    sigma = jax.nn.sigmoid(gate_pre)
    hidden = (gate_pre * sigma).astype(jnp.bfloat16)
    out_partial = jnp.dot(hidden, down, preferred_element_type=jnp.float32).astype(jnp.bfloat16)
    hidden_grad = lax.dot_general(
        routed_grad, down, (((1,), (1,)), ((), ())), preferred_element_type=jnp.float32
    )
    pre_grad = (hidden_grad * sigma * (1.0 + gate_pre * (1.0 - sigma))).astype(jnp.bfloat16)
    back_partial = lax.dot_general(
        pre_grad, gate, (((1,), (1,)), ((), ())), preferred_element_type=jnp.float32
    ).astype(jnp.bfloat16)
    out_rows = exchange(scatter(out_partial))
    back_rows = exchange(scatter(back_partial))

    out_sum = jnp.dot(weighted.T, out_rows.astype(jnp.float32), precision=highest)
    back_sum = jnp.dot(chosen.T.astype(jnp.bfloat16), back_rows, preferred_element_type=jnp.float32)
    products = lax.dot_general(
        cotangent, out_rows, (((1,), (1,)), ((), ())), preferred_element_type=jnp.float32
    )
    partial_pairs = jnp.einsum("nj,jnk->nk", products, per_token, precision=highest)
    weight_grad = lax.psum(partial_pairs, "tp")
    return (out_sum.astype(jnp.bfloat16), back_sum.astype(jnp.bfloat16), weight_grad)


def solution(mesh):
    sizes = tuple(mesh.shape[name] for name in AXES)

    def block(*args):
        return shards(sizes, *args)

    in_specs = (
        P(("ctx", "exp"), "tp"),
        P(("ctx", "exp"), None),
        P(("ctx", "exp"), None),
        P(("ctx", "exp"), "tp"),
        P("exp", None, ("ctx", "tp")),
        P("exp", ("ctx", "tp"), None),
    )
    out_specs = (P(("ctx", "exp"), "tp"), P(("ctx", "exp"), "tp"), P(("ctx", "exp"), None))
    return jax.shard_map(block, mesh=mesh, in_specs=in_specs, out_specs=out_specs, check_vma=False)
```

time: 412 us -> 160 us (0.39)
  waiting for transfers between devices: 236 us -> 37.1 us
  starting transfers between devices: 7.33 us -> 75.6 us
  other arithmetic: 45.2 us -> 8.54 us
  blocking collectives: 34.3 us -> 3.03 us
  local copies, waits for them, and re-layouts: 39.4 us -> 9.31 us
  between operations: 14 us -> 1.06 us
  matrix products: 32.9 us -> 24.4 us
    all_gather x4 -> x0, waiting for transfers between devices: 126 us -> none  [the longest x1 55.9 us: shards(): lax.all_gather(first_grads, 'ctx', axis=1, tiled=True)]
    reduce_scatter x1 -> x0, waiting for transfers between devices: 98.5 us -> none  [shards(): lax.psum_scatter(jnp.concatenate([out_part, back_part], 3).reshape(lax.ax...]
    ppermute x0 -> x32, starting transfers between devices: none -> 51.3 us  [move(): return lax.ppermute(value, AXES, shift_pairs(sizes, **shift))]
    reduce_sum x1 -> x0, other arithmetic: 40.2 us -> none  [shards(): out_part = jnp.sum(jnp.where(keep, out_full, 0.0), 3)]
    all_to_all x2 -> x0, blocking collectives: 31.3 us -> none  [the longest x1 18.4 us: shards(): lax.all_to_all(dispatched.reshape(experts, capacity, row_width), 'exp', s...]
    reshape x5 -> x8, local copies, waits for them, and re-layouts: 33.4 us -> 3.31 us  [the longest x4 3.01 us: exchange(): sent = rows.reshape(experts, capacity, half_width)]
    all_to_all x1 -> x4, starting transfers between devices: 7.13 us -> 24.3 us  [exchange(): got = lax.all_to_all(sent, 'exp', split_axis=0, concat_axis=0, tiled=True)]
    all_to_all x1 -> x4, waiting for transfers between devices: 11.2 us -> 24.9 us  [exchange(): got = lax.all_to_all(sent, 'exp', split_axis=0, concat_axis=0, tiled=True)]
  transfers between devices with their start and end apart: 6 -> 36, of which waited for: 6 -> 9; matrix products, arithmetic and copies ran while one was open for 2% -> 23% of each run, Pallas kernels for 0% -> 0%
where the time goes in v1:
time: 160 us; the launch traced here: 159 us
  starting transfers between devices  75.6 us (47%)
  waiting for transfers between devices  37.1 us (23%)
  matrix products  24.4 us (15%)
  local copies, waits for them, and re-layouts  9.31 us (6%)
  other arithmetic  8.54 us (5%)
  blocking collectives  3.03 us (2%)
    ppermute x32, starting transfers between devices, move(): return lax.ppermute(value, AXES, shift_pairs(sizes, **shift))  51.3 us
    all_to_all x4, waiting for transfers between devices, exchange(): got = lax.all_to_all(sent, 'exp', split_axis=0, concat_axis=0, tiled=True)  24.9 us
    all_to_all x4, starting transfers between devices, exchange(): got = lax.all_to_all(sent, 'exp', split_axis=0, concat_axis=0, tiled=True)  24.3 us
    dot_general x1, matrix products, shards(): lax.dot_general(pre_grad, gate, (((1,), (1,)), ((), ())), preferred_eleme...  14 us
    ppermute x32, waiting for transfers between devices, move(): return lax.ppermute(value, AXES, shift_pairs(sizes, **shift))  12.3 us
    dot_general x1, matrix products, shards(): gate_pre = jnp.dot(routed_rows, gate, preferred_element_type=jnp.float32)  4.87 us
    dynamic_slice x2, local copies, waits for them, and re-layouts, scatter(): lax.dynamic_slice_in_dim(partial, (1 - core) * half_width, half_width, 1)  4.01 us
    convert_element_type x2, other arithmetic, scatter(): (kept.astype(jnp.float32) + got.astype(jnp.float32)).astype(jnp.bfloat16)  3.97 us
  transfers between devices with their start and end apart: 36, of which 9 were waited for; matrix products, arithmetic and copies ran while one was open for 23% of the time, Pallas kernels for 0%

profile of v1, /device:TPU:8, one launch (start us, length us, event | category | flops | bytes accessed | tf_op | source)
XLA Modules:
  0.0 159.2 jit_solution(15676989963327463962)
XLA Ops:
  5.0 9.5 %all-to-all-start = ((bf16[16,2,3072]{2,1,0:T(2,128)(2,1)}), bf16[16,2,3072]{2,1,0:T(2,128)(2,1)S(1)}, u32[]{:S(2)}, u32[]{:S(2)}) async-start(bf16[16,2,3072]{2,1,0:T(2,128)(2,1)} %reshape.58), calls=%async_computation | async-start | bytes 393216 | tf_op jit(solution)/shard_map/all_to_all | solution.py:53
  15.7 7.9 %all-to-all-done = bf16[16,2,3072]{2,1,0:T(2,128)(2,1)S(1)} async-done(((bf16[16,2,3072]{2,1,0:T(2,128)(2,1)}), bf16[16,2,3072]{2,1,0:T(2,128)(2,1)S(1)}, u32[]{:S(2)}, u32[]{:S(2)}) %all-to-all-start) | async-done | bytes 196640 | tf_op jit(solution)/shard_map/all_to_all | solution.py:53
  23.6 4.2 %all-to-all-start.2 = ((bf16[16,2,3072]{2,1,0:T(2,128)(2,1)}), bf16[16,2,3072]{2,1,0:T(2,128)(2,1)S(1)}, u32[]{:S(2)}, u32[]{:S(2)}) async-start(bf16[16,2,3072]{2,1,0:T(2,128)(2,1)} %reshape.62), calls=%async_computation.2 | async-start | bytes 393216 | tf_op jit(solution)/shard_map/all_to_all | solution.py:53
  27.8 2.8 %collective-permute-start = (bf16[32,3072]{1,0:T(8,128)(2,1)S(1)}, bf16[32,3072]{1,0:T(8,128)(2,1)S(1)}, u32[]{:S(2)}, u32[]{:S(2)}) collective-permute-start(bf16[32,3072]{1,0:T(8,128)(2,1)S(1)} %reshape.59), channel_id=1, source_target_pairs={{0,128},{1,129},{2,130},{3,131},{4,132},{5,133},{6,134},{7,135},{8... | collective-permute-start | bytes 589832 | tf_op jit(solution)/shard_map/ppermute | solution.py:37
  32.7 2.3 %collective-permute-start.3 = (bf16[32,3072]{1,0:T(8,128)(2,1)S(1)}, bf16[32,3072]{1,0:T(8,128)(2,1)S(1)}, u32[]{:S(2)}, u32[]{:S(2)}) collective-permute-start(bf16[32,3072]{1,0:T(8,128)(2,1)S(1)} %reshape.59), channel_id=1, source_target_pairs={{0,64},{1,65},{2,66},{3,67},{4,68},{5,69},{6,70},{7,71},{8,72},{9,... | collective-permute-start | bytes 589832 | tf_op jit(solution)/shard_map/ppermute | solution.py:37
  36.8 2.8 %collective-permute-start.16 = (bf16[32,3072]{1,0:T(8,128)(2,1)S(1)}, bf16[32,3072]{1,0:T(8,128)(2,1)S(1)}, u32[]{:S(2)}, u32[]{:S(2)}) collective-permute-start(bf16[32,3072]{1,0:T(8,128)(2,1)S(1)} %reshape.63), channel_id=1, source_target_pairs={{0,128},{1,129},{2,130},{3,131},{4,132},{5,133},{6,134},{7,135},{8... | collective-permute-start | bytes 589832 | tf_op jit(solution)/shard_map/ppermute | solution.py:37
  41.9 2.4 %collective-permute-start.19 = (bf16[32,3072]{1,0:T(8,128)(2,1)S(1)}, bf16[32,3072]{1,0:T(8,128)(2,1)S(1)}, u32[]{:S(2)}, u32[]{:S(2)}) collective-permute-start(bf16[32,3072]{1,0:T(8,128)(2,1)S(1)} %reshape.63), channel_id=1, source_target_pairs={{0,64},{1,65},{2,66},{3,67},{4,68},{5,69},{6,70},{7,71},{8,72},{9,... | collective-permute-start | bytes 589832 | tf_op jit(solution)/shard_map/ppermute | solution.py:37
  46.5 3.3 %collective-permute-done.17 = bf16[32,3072]{1,0:T(8,128)(2,1)S(1)} collective-permute-done((bf16[32,3072]{1,0:T(8,128)(2,1)S(1)}, bf16[32,3072]{1,0:T(8,128)(2,1)S(1)}, u32[]{:S(2)}, u32[]{:S(2)}) %collective-permute-start.17) | collective-permute-done | bytes 196640 | tf_op jit(solution)/shard_map/ppermute | solution.py:37
  50.6 2.8 %collective-permute-done.4 = bf16[32,3072]{1,0:T(8,128)(2,1)S(1)} collective-permute-done((bf16[32,3072]{1,0:T(8,128)(2,1)S(1)}, bf16[32,3072]{1,0:T(8,128)(2,1)S(1)}, u32[]{:S(2)}, u32[]{:S(2)}) %collective-permute-start.4) | collective-permute-done | bytes 196640 | tf_op jit(solution)/shard_map/ppermute | solution.py:37
  57.2 2.5 %collective-permute-done.20 = bf16[32,3072]{1,0:T(8,128)(2,1)S(1)} collective-permute-done((bf16[32,3072]{1,0:T(8,128)(2,1)S(1)}, bf16[32,3072]{1,0:T(8,128)(2,1)S(1)}, u32[]{:S(2)}, u32[]{:S(2)}) %collective-permute-start.20) | collective-permute-done | bytes 196640 | tf_op jit(solution)/shard_map/ppermute | solution.py:37
  60.7 2.6 %collective-permute-done.22 = bf16[32,3072]{1,0:T(8,128)(2,1)S(1)} collective-permute-done((bf16[32,3072]{1,0:T(8,128)(2,1)S(1)}, bf16[32,3072]{1,0:T(8,128)(2,1)S(1)}, u32[]{:S(2)}, u32[]{:S(2)}) %collective-permute-start.22) | collective-permute-done | bytes 196640 | tf_op jit(solution)/shard_map/ppermute | solution.py:37
  64.0 4.9 %fusion.4 = f32[256,504]{0,1:T(8,128)S(1)} fusion(bf16[1,6144,504]{1,2,0:T(8,128)(2,1)} %param.10, bf16[256,3072]{1,0:T(8,128)(2,1)S(1)} %get-tuple-element.8, bf16[256,3072]{1,0:T(8,128)(2,1)S(1)} %get-tuple-element.7), kind=kOutput, calls=%fused_computation.6 | convolution fusion | flops 1591738368 | bytes 9854976 | tf_op jit(solution)/shard_map/dot_general | solution.py:103
  68.9 2.2 %convolution_convert_fusion.1 = bf16[256,6144]{1,0:T(8,128)(2,1)S(1)} fusion(bf16[1,504,6144]{2,1,0:T(8,128)(2,1)S(1)} %bitcast.36, f32[256,504]{0,1:T(8,128)S(1)} %fusion.4), kind=kOutput, calls=%fused_computation.1 | convolution fusion | flops 1587664896 | bytes 9854976 | tf_op jit(solution)/shard_map/dot_general | solution.py:106
  72.9 1.9 %broadcast_select_fusion.1 = (bf16[256,3072]{1,0:T(8,128)(2,1)}, bf16[256,3072]{1,0:T(8,128)(2,1)}) fusion(bf16[256,3072]{1,0:T(8,128)(2,1)S(1)} %constant_dynamic-update-slice_fusion.8, bf16[256,3072]{1,0:T(8,128)(2,1)S(1)} %collective-permute-done.23, pred[]{:T(512)S(6)} %eq.43), kind=kLoop, calls=%fused_computation.21 | loop fusion | flops 1572864 | bytes 6291457 | tf_op jit(solution)/shard_map/jit(_where)/select_n | solution.py:68
  74.8 14.0 %convolution_convert_fusion = bf16[256,6144]{1,0:T(8,128)(2,1)} fusion(bf16[1,6144,504]{1,2,0:T(8,128)(2,1)} %param.10, bf16[1,504,6144]{2,1,0:T(8,128)(2,1)} %param.11, bf16[256,3072]{1,0:T(8,128)(2,1)} %get-tuple-element.6, bf16[256,3072]{1,0:T(8,128)(2,1)} %get-tuple-element.5, f32[256,504]{0,1:T(8,128)} %copy-done.2), kind=kOutput, calls=%fused_computation | convolution fusion | flops 3179919360 | bytes 19193856 | tf_op jit(solution)/shard_map/dot_general | solution.py:111
  88.8 2.7 %constant_dynamic-slice_fusion.1 = bf16[256,3072]{1,0:T(8,128)(2,1)} fusion(bf16[256,6144]{1,0:T(8,128)(2,1)} %convolution_convert_fusion, s32[]{:T(128)S(6)} %select_n.32), kind=kLoop, calls=%fused_computation.67 | loop fusion | bytes 3145732 | tf_op jit(solution)/shard_map/dynamic_slice | solution.py:74
  91.6 2.1 %add_convert_fusion.1 = bf16[256,3072]{1,0:T(8,128)(2,1)S(1)} fusion(bf16[256,3072]{1,0:T(8,128)(2,1)} %collective-permute-done.8, bf16[256,6144]{1,0:T(8,128)(2,1)S(1)} %convolution_convert_fusion.1, s32[]{:T(128)S(6)} %select_n.31), kind=kLoop, calls=%fused_computation.19 | loop fusion | flops 3145728 | bytes 4718596 | tf_op jit(solution)/shard_map/convert_element_type | solution.py:76
  93.8 3.3 %collective-permute-start.11 = (bf16[32,3072]{1,0:T(8,128)(2,1)S(1)}, bf16[32,3072]{1,0:T(8,128)(2,1)S(1)}, u32[]{:S(2)}, u32[]{:S(2)}) collective-permute-start(bf16[32,3072]{1,0:T(8,128)(2,1)S(1)} %get-tuple-element.19), channel_id=1, source_target_pairs={{0,96},{1,97},{2,98},{3,99},{4,100},{5,101},{6,102},{7,103},{8,104... | collective-permute-start | bytes 589832 | tf_op jit(solution)/shard_map/ppermute | solution.py:37
  97.9 1.8 %add_convert_fusion = bf16[256,3072]{1,0:T(8,128)(2,1)S(1)} fusion(bf16[256,3072]{1,0:T(8,128)(2,1)} %collective-permute-done.24, bf16[256,6144]{1,0:T(8,128)(2,1)S(1)} %copy-done.1, s32[]{:T(128)S(6)} %select_n.31), kind=kLoop, calls=%fused_computation.18 | loop fusion | flops 3145728 | bytes 4718596 | tf_op jit(solution)/shard_map/convert_element_type | solution.py:76
  100.5 2.0 %collective-permute-start.27 = (bf16[32,3072]{1,0:T(8,128)(2,1)S(1)}, bf16[32,3072]{1,0:T(8,128)(2,1)S(1)}, u32[]{:S(2)}, u32[]{:S(2)}) collective-permute-start(bf16[32,3072]{1,0:T(8,128)(2,1)S(1)} %get-tuple-element.12), channel_id=1, source_target_pairs={{0,96},{1,97},{2,98},{3,99},{4,100},{5,101},{6,102},{7,103},{8,104... | collective-permute-start | bytes 589832 | tf_op jit(solution)/shard_map/ppermute | solution.py:37
  102.6 2.7 %collective-permute-start.30 = (bf16[32,3072]{1,0:T(8,128)(2,1)S(1)}, bf16[32,3072]{1,0:T(8,128)(2,1)S(1)}, u32[]{:S(2)}, u32[]{:S(2)}) collective-permute-start(bf16[32,3072]{1,0:T(8,128)(2,1)S(1)} %get-tuple-element.10), channel_id=1, source_target_pairs={{0,128},{1,129},{2,130},{3,131},{4,132},{5,133},{6,134},{7,135},{8... | collective-permute-start | bytes 589832 | tf_op jit(solution)/shard_map/ppermute | solution.py:37
  105.3 2.0 %collective-permute-start.25 = (bf16[32,3072]{1,0:T(8,128)(2,1)}, bf16[32,3072]{1,0:T(8,128)(2,1)S(1)}, u32[]{:S(2)}, u32[]{:S(2)}) collective-permute-start(bf16[32,3072]{1,0:T(8,128)(2,1)} %get-tuple-element.9), channel_id=1, source_target_pairs={{0,96},{1,97},{2,98},{3,99},{4,100},{5,101},{6,102},{7,103},{8,104... | collective-permute-start | bytes 589832 | tf_op jit(solution)/shard_map/ppermute | solution.py:37
  107.5 2.8 %collective-permute-start.9 = (bf16[32,3072]{1,0:T(8,128)(2,1)S(1)}, bf16[32,3072]{1,0:T(8,128)(2,1)S(1)}, u32[]{:S(2)}, u32[]{:S(2)}) collective-permute-start(bf16[32,3072]{1,0:T(8,128)(2,1)S(1)} %get-tuple-element.16), channel_id=1, source_target_pairs={{0,96},{1,97},{2,98},{3,99},{4,100},{5,101},{6,102},{7,103},{8,104... | collective-permute-start | bytes 589832 | tf_op jit(solution)/shard_map/ppermute | solution.py:37
  110.3 2.8 %collective-permute-start.13 = (bf16[32,3072]{1,0:T(8,128)(2,1)S(1)}, bf16[32,3072]{1,0:T(8,128)(2,1)S(1)}, u32[]{:S(2)}, u32[]{:S(2)}) collective-permute-start(bf16[32,3072]{1,0:T(8,128)(2,1)S(1)} %get-tuple-element.21), channel_id=1, source_target_pairs={{0,128},{1,129},{2,130},{3,131},{4,132},{5,133},{6,134},{7,135},{8... | collective-permute-start | bytes 589832 | tf_op jit(solution)/shard_map/ppermute | solution.py:37
  114.4 2.7 %collective-permute-start.26 = (bf16[32,3072]{1,0:T(8,128)(2,1)S(1)}, bf16[32,3072]{1,0:T(8,128)(2,1)S(1)}, u32[]{:S(2)}, u32[]{:S(2)}) collective-permute-start(bf16[32,3072]{1,0:T(8,128)(2,1)S(1)} %get-tuple-element.13), channel_id=1, source_target_pairs={{0,32},{1,33},{2,34},{3,35},{4,36},{5,37},{6,38},{7,39},{8,40},{9,... | collective-permute-start | bytes 589832 | tf_op jit(solution)/shard_map/ppermute | solution.py:37
  117.1 1.9 %collective-permute-start.29 = (bf16[32,3072]{1,0:T(8,128)(2,1)S(1)}, bf16[32,3072]{1,0:T(8,128)(2,1)S(1)}, u32[]{:S(2)}, u32[]{:S(2)}) collective-permute-start(bf16[32,3072]{1,0:T(8,128)(2,1)S(1)} %get-tuple-element.14), channel_id=1, source_target_pairs={{0,128},{1,129},{2,130},{3,131},{4,132},{5,133},{6,134},{7,135},{8... | collective-permute-start | bytes 589832 | tf_op jit(solution)/shard_map/ppermute | solution.py:37
  119.1 7.2 %collective-permute-start.31 = (bf16[32,3072]{1,0:T(8,128)(2,1)S(1)}, bf16[32,3072]{1,0:T(8,128)(2,1)S(1)}, u32[]{:S(2)}, u32[]{:S(2)}) collective-permute-start(bf16[32,3072]{1,0:T(8,128)(2,1)S(1)} %get-tuple-element.15), channel_id=1, source_target_pairs={{0,64},{1,65},{2,66},{3,67},{4,68},{5,69},{6,70},{7,71},{8,72},{9,... | collective-permute-start | bytes 589832 | tf_op jit(solution)/shard_map/ppermute | solution.py:37
  127.1 6.8 %all-to-all-start.1 = ((bf16[16,2,3072]{2,1,0:T(2,128)(2,1)}), bf16[16,2,3072]{2,1,0:T(2,128)(2,1)S(1)}, u32[]{:S(2)}, u32[]{:S(2)}) async-start(bf16[16,2,3072]{2,1,0:T(2,128)(2,1)} %reshape.60), calls=%async_computation.1 | async-start | bytes 393216 | tf_op jit(solution)/shard_map/all_to_all | solution.py:53
  134.8 7.7 %all-to-all-done.1 = bf16[16,2,3072]{2,1,0:T(2,128)(2,1)S(1)} async-done(((bf16[16,2,3072]{2,1,0:T(2,128)(2,1)}), bf16[16,2,3072]{2,1,0:T(2,128)(2,1)S(1)}, u32[]{:S(2)}, u32[]{:S(2)}) %all-to-all-start.1) | async-done | bytes 196640 | tf_op jit(solution)/shard_map/all_to_all | solution.py:53
  142.5 3.9 %all-to-all-start.3 = ((bf16[16,2,3072]{2,1,0:T(2,128)(2,1)}), bf16[16,2,3072]{2,1,0:T(2,128)(2,1)S(1)}, u32[]{:S(2)}, u32[]{:S(2)}) async-start(bf16[16,2,3072]{2,1,0:T(2,128)(2,1)} %reshape.64), calls=%async_computation.3 | async-start | bytes 393216 | tf_op jit(solution)/shard_map/all_to_all | solution.py:53
  147.5 7.5 %all-to-all-done.3 = bf16[16,2,3072]{2,1,0:T(2,128)(2,1)S(1)} async-done(((bf16[16,2,3072]{2,1,0:T(2,128)(2,1)}), bf16[16,2,3072]{2,1,0:T(2,128)(2,1)S(1)}, u32[]{:S(2)}, u32[]{:S(2)}) %all-to-all-start.3) | async-done | bytes 196640 | tf_op jit(solution)/shard_map/all_to_all | solution.py:53
  156.1 3.0 %psum.7 = f32[4,4]{1,0:T(4,128)} all-reduce(f32[4,4]{1,0:T(4,128)S(1)} %bitcast.37), channel_id=1, replica_groups=mesh['ctx'=8,'exp'=16,'tp'=2] {'tp'}, use_global_device_ids=true, to_apply=%region_4.5 | all-reduce | flops 16 | bytes 128 | tf_op jit(solution)/shard_map/psum | solution.py:123
  (105 shorter events, 28.9 us)
Async XLA Ops:
  5.0 18.6 %all-to-all-start = ((bf16[16,2,3072]{2,1,0:T(2,128)(2,1)}), bf16[16,2,3072]{2,1,0:T(2,128)(2,1)S(1)}, u32[]{:S(2)}, u32[]{:S(2)}) async-start(bf16[16,2,3072]{2,1,0:T(2,128)(2,1)} %reshape.58), calls=%async_computation | async-start | bytes 393216 | tf_op jit(solution)/shard_map/all_to_all | solution.py:53
  23.6 13.2 %all-to-all-start.2 = ((bf16[16,2,3072]{2,1,0:T(2,128)(2,1)}), bf16[16,2,3072]{2,1,0:T(2,128)(2,1)S(1)}, u32[]{:S(2)}, u32[]{:S(2)}) async-start(bf16[16,2,3072]{2,1,0:T(2,128)(2,1)} %reshape.62), calls=%async_computation.2 | async-start | bytes 393216 | tf_op jit(solution)/shard_map/all_to_all | solution.py:53
  27.8 11.8 %collective-permute-start = (bf16[32,3072]{1,0:T(8,128)(2,1)S(1)}, bf16[32,3072]{1,0:T(8,128)(2,1)S(1)}, u32[]{:S(2)}, u32[]{:S(2)}) collective-permute-start(bf16[32,3072]{1,0:T(8,128)(2,1)S(1)} %reshape.59), channel_id=1, source_target_pairs={{0,128},{1,129},{2,130},{3,131},{4,132},{5,133},{6,134},{7,135},{8... | collective-permute-start | bytes 589832 | tf_op jit(solution)/shard_map/ppermute | solution.py:37
  30.6 10.7 %collective-permute-start.1 = (bf16[32,3072]{1,0:T(8,128)(2,1)S(1)}, bf16[32,3072]{1,0:T(8,128)(2,1)S(1)}, u32[]{:S(2)}, u32[]{:S(2)}) collective-permute-start(bf16[32,3072]{1,0:T(8,128)(2,1)S(1)} %reshape.59), channel_id=1, source_target_pairs={{0,32},{1,33},{2,34},{3,35},{4,36},{5,37},{6,38},{7,39},{8,40},{9,... | collective-permute-start | bytes 589832 | tf_op jit(solution)/shard_map/ppermute | solution.py:37
  32.2 9.7 %collective-permute-start.2 = (bf16[32,3072]{1,0:T(8,128)(2,1)S(1)}, bf16[32,3072]{1,0:T(8,128)(2,1)S(1)}, u32[]{:S(2)}, u32[]{:S(2)}) collective-permute-start(bf16[32,3072]{1,0:T(8,128)(2,1)S(1)} %reshape.59), channel_id=1, source_target_pairs={{0,96},{1,97},{2,98},{3,99},{4,100},{5,101},{6,102},{7,103},{8,104... | collective-permute-start | bytes 589832 | tf_op jit(solution)/shard_map/ppermute | solution.py:37
  32.7 11.6 %collective-permute-start.3 = (bf16[32,3072]{1,0:T(8,128)(2,1)S(1)}, bf16[32,3072]{1,0:T(8,128)(2,1)S(1)}, u32[]{:S(2)}, u32[]{:S(2)}) collective-permute-start(bf16[32,3072]{1,0:T(8,128)(2,1)S(1)} %reshape.59), channel_id=1, source_target_pairs={{0,64},{1,65},{2,66},{3,67},{4,68},{5,69},{6,70},{7,71},{8,72},{9,... | collective-permute-start | bytes 589832 | tf_op jit(solution)/shard_map/ppermute | solution.py:37
  36.8 8.4 %collective-permute-start.16 = (bf16[32,3072]{1,0:T(8,128)(2,1)S(1)}, bf16[32,3072]{1,0:T(8,128)(2,1)S(1)}, u32[]{:S(2)}, u32[]{:S(2)}) collective-permute-start(bf16[32,3072]{1,0:T(8,128)(2,1)S(1)} %reshape.63), channel_id=1, source_target_pairs={{0,128},{1,129},{2,130},{3,131},{4,132},{5,133},{6,134},{7,135},{8... | collective-permute-start | bytes 589832 | tf_op jit(solution)/shard_map/ppermute | solution.py:37
  39.7 10.1 %collective-permute-start.17 = (bf16[32,3072]{1,0:T(8,128)(2,1)S(1)}, bf16[32,3072]{1,0:T(8,128)(2,1)S(1)}, u32[]{:S(2)}, u32[]{:S(2)}) collective-permute-start(bf16[32,3072]{1,0:T(8,128)(2,1)S(1)} %reshape.63), channel_id=1, source_target_pairs={{0,32},{1,33},{2,34},{3,35},{4,36},{5,37},{6,38},{7,39},{8,40},{9,... | collective-permute-start | bytes 589832 | tf_op jit(solution)/shard_map/ppermute | solution.py:37
  41.3 15.8 %collective-permute-start.18 = (bf16[32,3072]{1,0:T(8,128)(2,1)S(1)}, bf16[32,3072]{1,0:T(8,128)(2,1)S(1)}, u32[]{:S(2)}, u32[]{:S(2)}) collective-permute-start(bf16[32,3072]{1,0:T(8,128)(2,1)S(1)} %reshape.63), channel_id=1, source_target_pairs={{0,96},{1,97},{2,98},{3,99},{4,100},{5,101},{6,102},{7,103},{8,104... | collective-permute-start | bytes 589832 | tf_op jit(solution)/shard_map/ppermute | solution.py:37
  41.9 13.0 %collective-permute-start.19 = (bf16[32,3072]{1,0:T(8,128)(2,1)S(1)}, bf16[32,3072]{1,0:T(8,128)(2,1)S(1)}, u32[]{:S(2)}, u32[]{:S(2)}) collective-permute-start(bf16[32,3072]{1,0:T(8,128)(2,1)S(1)} %reshape.63), channel_id=1, source_target_pairs={{0,64},{1,65},{2,66},{3,67},{4,68},{5,69},{6,70},{7,71},{8,72},{9,... | collective-permute-start | bytes 589832 | tf_op jit(solution)/shard_map/ppermute | solution.py:37
  44.3 9.1 %collective-permute-start.4 = (bf16[32,3072]{1,0:T(8,128)(2,1)S(1)}, bf16[32,3072]{1,0:T(8,128)(2,1)S(1)}, u32[]{:S(2)}, u32[]{:S(2)}) collective-permute-start(bf16[32,3072]{1,0:T(8,128)(2,1)S(1)} %collective-permute-done), channel_id=1, source_target_pairs={{0,32},{1,33},{2,34},{3,35},{4,36},{5,37},{6,38},{7,39},{8,40},{9,... | collective-permute-start | bytes 589832 | tf_op jit(solution)/shard_map/ppermute | solution.py:37
  45.2 10.9 %collective-permute-start.5 = (bf16[32,3072]{1,0:T(8,128)(2,1)S(1)}, bf16[32,3072]{1,0:T(8,128)(2,1)S(1)}, u32[]{:S(2)}, u32[]{:S(2)}) collective-permute-start(bf16[32,3072]{1,0:T(8,128)(2,1)S(1)} %collective-permute-done), channel_id=1, source_target_pairs={{0,96},{1,97},{2,98},{3,99},{4,100},{5,101},{6,102},{7,103},{8,104... | collective-permute-start | bytes 589832 | tf_op jit(solution)/shard_map/ppermute | solution.py:37
  49.8 7.2 %collective-permute-start.6 = (bf16[32,3072]{1,0:T(8,128)(2,1)S(1)}, bf16[32,3072]{1,0:T(8,128)(2,1)S(1)}, u32[]{:S(2)}, u32[]{:S(2)}) collective-permute-start(bf16[32,3072]{1,0:T(8,128)(2,1)S(1)} %collective-permute-done.3), channel_id=1, source_target_pairs={{0,128},{1,129},{2,130},{3,131},{4,132},{5,133},{6,134},{7,135},{8... | collective-permute-start | bytes 589832 | tf_op jit(solution)/shard_map/ppermute | solution.py:37
  56.1 7.2 %collective-permute-start.22 = (bf16[32,3072]{1,0:T(8,128)(2,1)S(1)}, bf16[32,3072]{1,0:T(8,128)(2,1)S(1)}, u32[]{:S(2)}, u32[]{:S(2)}) collective-permute-start(bf16[32,3072]{1,0:T(8,128)(2,1)S(1)} %collective-permute-done.19), channel_id=1, source_target_pairs={{0,128},{1,129},{2,130},{3,131},{4,132},{5,133},{6,134},{7,135},{8... | collective-permute-start | bytes 589832 | tf_op jit(solution)/shard_map/ppermute | solution.py:37
  63.3 9.6 %collective-permute-start.23 = (bf16[256,3072]{1,0:T(8,128)(2,1)S(1)}, bf16[256,3072]{1,0:T(8,128)(2,1)S(1)}, u32[]{:S(2)}, u32[]{:S(2)}) collective-permute-start(bf16[256,3072]{1,0:T(8,128)(2,1)S(1)} %constant_dynamic-update-slice_fusion.8), channel_id=1, source_target_pairs={{0,1},{1,0},{2,3},{3,2},{4,5},{5,4},{6,7},{7,6},{8,9},{9,8},{10,11... | collective-permute-start | bytes 4718600 | tf_op jit(solution)/shard_map/ppermute | solution.py:37
  72.4 19.2 %collective-permute-start.8 = (bf16[256,3072]{1,0:T(8,128)(2,1)}, bf16[256,3072]{1,0:T(8,128)(2,1)}, u32[]{:S(2)}, u32[]{:S(2)}) collective-permute-start(bf16[256,3072]{1,0:T(8,128)(2,1)} %constant_dynamic-slice_fusion), channel_id=1, source_target_pairs={{0,1},{1,0},{2,3},{3,2},{4,5},{5,4},{6,7},{7,6},{8,9},{9,8},{10,11... | collective-permute-start | bytes 4718600 | tf_op jit(solution)/shard_map/ppermute | solution.py:37
  93.8 8.7 %collective-permute-start.11 = (bf16[32,3072]{1,0:T(8,128)(2,1)S(1)}, bf16[32,3072]{1,0:T(8,128)(2,1)S(1)}, u32[]{:S(2)}, u32[]{:S(2)}) collective-permute-start(bf16[32,3072]{1,0:T(8,128)(2,1)S(1)} %get-tuple-element.19), channel_id=1, source_target_pairs={{0,96},{1,97},{2,98},{3,99},{4,100},{5,101},{6,102},{7,103},{8,104... | collective-permute-start | bytes 589832 | tf_op jit(solution)/shard_map/ppermute | solution.py:37
  97.1 8.2 %collective-permute-start.12 = (bf16[32,3072]{1,0:T(8,128)(2,1)S(1)}, bf16[32,3072]{1,0:T(8,128)(2,1)S(1)}, u32[]{:S(2)}, u32[]{:S(2)}) collective-permute-start(bf16[32,3072]{1,0:T(8,128)(2,1)S(1)} %get-tuple-element.18), channel_id=1, source_target_pairs={{0,32},{1,33},{2,34},{3,35},{4,36},{5,37},{6,38},{7,39},{8,40},{9,... | collective-permute-start | bytes 589832 | tf_op jit(solution)/shard_map/ppermute | solution.py:37
  97.1 10.2 %collective-permute-start.14 = (bf16[32,3072]{1,0:T(8,128)(2,1)S(1)}, bf16[32,3072]{1,0:T(8,128)(2,1)S(1)}, u32[]{:S(2)}, u32[]{:S(2)}) collective-permute-start(bf16[32,3072]{1,0:T(8,128)(2,1)S(1)} %get-tuple-element.17), channel_id=1, source_target_pairs={{0,128},{1,129},{2,130},{3,131},{4,132},{5,133},{6,134},{7,135},{8... | collective-permute-start | bytes 589832 | tf_op jit(solution)/shard_map/ppermute | solution.py:37
  100.5 6.9 %collective-permute-start.27 = (bf16[32,3072]{1,0:T(8,128)(2,1)S(1)}, bf16[32,3072]{1,0:T(8,128)(2,1)S(1)}, u32[]{:S(2)}, u32[]{:S(2)}) collective-permute-start(bf16[32,3072]{1,0:T(8,128)(2,1)S(1)} %get-tuple-element.12), channel_id=1, source_target_pairs={{0,96},{1,97},{2,98},{3,99},{4,100},{5,101},{6,102},{7,103},{8,104... | collective-permute-start | bytes 589832 | tf_op jit(solution)/shard_map/ppermute | solution.py:37
  102.6 7.7 %collective-permute-start.28 = (bf16[32,3072]{1,0:T(8,128)(2,1)S(1)}, bf16[32,3072]{1,0:T(8,128)(2,1)S(1)}, u32[]{:S(2)}, u32[]{:S(2)}) collective-permute-start(bf16[32,3072]{1,0:T(8,128)(2,1)S(1)} %get-tuple-element.11), channel_id=1, source_target_pairs={{0,32},{1,33},{2,34},{3,35},{4,36},{5,37},{6,38},{7,39},{8,40},{9,... | collective-permute-start | bytes 589832 | tf_op jit(solution)/shard_map/ppermute | solution.py:37
  102.6 10.6 %collective-permute-start.30 = (bf16[32,3072]{1,0:T(8,128)(2,1)S(1)}, bf16[32,3072]{1,0:T(8,128)(2,1)S(1)}, u32[]{:S(2)}, u32[]{:S(2)}) collective-permute-start(bf16[32,3072]{1,0:T(8,128)(2,1)S(1)} %get-tuple-element.10), channel_id=1, source_target_pairs={{0,128},{1,129},{2,130},{3,131},{4,132},{5,133},{6,134},{7,135},{8... | collective-permute-start | bytes 589832 | tf_op jit(solution)/shard_map/ppermute | solution.py:37
  105.3 28.6 %collective-permute-start.25 = (bf16[32,3072]{1,0:T(8,128)(2,1)}, bf16[32,3072]{1,0:T(8,128)(2,1)S(1)}, u32[]{:S(2)}, u32[]{:S(2)}) collective-permute-start(bf16[32,3072]{1,0:T(8,128)(2,1)} %get-tuple-element.9), channel_id=1, source_target_pairs={{0,96},{1,97},{2,98},{3,99},{4,100},{5,101},{6,102},{7,103},{8,104... | collective-permute-start | bytes 589832 | tf_op jit(solution)/shard_map/ppermute | solution.py:37
  107.3 7.1 %collective-permute-start.10 = (bf16[32,3072]{1,0:T(8,128)(2,1)S(1)}, bf16[32,3072]{1,0:T(8,128)(2,1)S(1)}, u32[]{:S(2)}, u32[]{:S(2)}) collective-permute-start(bf16[32,3072]{1,0:T(8,128)(2,1)S(1)} %get-tuple-element.20), channel_id=1, source_target_pairs={{0,32},{1,33},{2,34},{3,35},{4,36},{5,37},{6,38},{7,39},{8,40},{9,... | collective-permute-start | bytes 589832 | tf_op jit(solution)/shard_map/ppermute | solution.py:37
  107.5 9.7 %collective-permute-start.9 = (bf16[32,3072]{1,0:T(8,128)(2,1)S(1)}, bf16[32,3072]{1,0:T(8,128)(2,1)S(1)}, u32[]{:S(2)}, u32[]{:S(2)}) collective-permute-start(bf16[32,3072]{1,0:T(8,128)(2,1)S(1)} %get-tuple-element.16), channel_id=1, source_target_pairs={{0,96},{1,97},{2,98},{3,99},{4,100},{5,101},{6,102},{7,103},{8,104... | collective-permute-start | bytes 589832 | tf_op jit(solution)/shard_map/ppermute | solution.py:37
  110.3 8.8 %collective-permute-start.13 = (bf16[32,3072]{1,0:T(8,128)(2,1)S(1)}, bf16[32,3072]{1,0:T(8,128)(2,1)S(1)}, u32[]{:S(2)}, u32[]{:S(2)}) collective-permute-start(bf16[32,3072]{1,0:T(8,128)(2,1)S(1)} %get-tuple-element.21), channel_id=1, source_target_pairs={{0,128},{1,129},{2,130},{3,131},{4,132},{5,133},{6,134},{7,135},{8... | collective-permute-start | bytes 589832 | tf_op jit(solution)/shard_map/ppermute | solution.py:37
  113.1 13.1 %collective-permute-start.15 = (bf16[32,3072]{1,0:T(8,128)(2,1)S(1)}, bf16[32,3072]{1,0:T(8,128)(2,1)S(1)}, u32[]{:S(2)}, u32[]{:S(2)}) collective-permute-start(bf16[32,3072]{1,0:T(8,128)(2,1)S(1)} %get-tuple-element.22), channel_id=1, source_target_pairs={{0,64},{1,65},{2,66},{3,67},{4,68},{5,69},{6,70},{7,71},{8,72},{9,... | collective-permute-start | bytes 589832 | tf_op jit(solution)/shard_map/ppermute | solution.py:37
  114.4 19.4 %collective-permute-start.26 = (bf16[32,3072]{1,0:T(8,128)(2,1)S(1)}, bf16[32,3072]{1,0:T(8,128)(2,1)S(1)}, u32[]{:S(2)}, u32[]{:S(2)}) collective-permute-start(bf16[32,3072]{1,0:T(8,128)(2,1)S(1)} %get-tuple-element.13), channel_id=1, source_target_pairs={{0,32},{1,33},{2,34},{3,35},{4,36},{5,37},{6,38},{7,39},{8,40},{9,... | collective-permute-start | bytes 589832 | tf_op jit(solution)/shard_map/ppermute | solution.py:37
  117.1 16.7 %collective-permute-start.29 = (bf16[32,3072]{1,0:T(8,128)(2,1)S(1)}, bf16[32,3072]{1,0:T(8,128)(2,1)S(1)}, u32[]{:S(2)}, u32[]{:S(2)}) collective-permute-start(bf16[32,3072]{1,0:T(8,128)(2,1)S(1)} %get-tuple-element.14), channel_id=1, source_target_pairs={{0,128},{1,129},{2,130},{3,131},{4,132},{5,133},{6,134},{7,135},{8... | collective-permute-start | bytes 589832 | tf_op jit(solution)/shard_map/ppermute | solution.py:37
  119.1 14.8 %collective-permute-start.31 = (bf16[32,3072]{1,0:T(8,128)(2,1)S(1)}, bf16[32,3072]{1,0:T(8,128)(2,1)S(1)}, u32[]{:S(2)}, u32[]{:S(2)}) collective-permute-start(bf16[32,3072]{1,0:T(8,128)(2,1)S(1)} %get-tuple-element.15), channel_id=1, source_target_pairs={{0,64},{1,65},{2,66},{3,67},{4,68},{5,69},{6,70},{7,71},{8,72},{9,... | collective-permute-start | bytes 589832 | tf_op jit(solution)/shard_map/ppermute | solution.py:37
  127.1 15.4 %all-to-all-start.1 = ((bf16[16,2,3072]{2,1,0:T(2,128)(2,1)}), bf16[16,2,3072]{2,1,0:T(2,128)(2,1)S(1)}, u32[]{:S(2)}, u32[]{:S(2)}) async-start(bf16[16,2,3072]{2,1,0:T(2,128)(2,1)} %reshape.60), calls=%async_computation.1 | async-start | bytes 393216 | tf_op jit(solution)/shard_map/all_to_all | solution.py:53
  142.5 12.5 %all-to-all-start.3 = ((bf16[16,2,3072]{2,1,0:T(2,128)(2,1)}), bf16[16,2,3072]{2,1,0:T(2,128)(2,1)S(1)}, u32[]{:S(2)}, u32[]{:S(2)}) async-start(bf16[16,2,3072]{2,1,0:T(2,128)(2,1)} %reshape.64), calls=%async_computation.3 | async-start | bytes 393216 | tf_op jit(solution)/shard_map/all_to_all | solution.py:53
  (9 other events, 57.6 us)

commit v2 on v1

v2 whole, which is shorter than its diff:
```python
import functools

import jax
import jax.numpy as jnp
from jax import lax
from jax.experimental import pallas as pl
from jax.experimental.pallas import tpu as pltpu
from jax.sharding import PartitionSpec as P

AXES = ("ctx", "exp", "tp")
ROW_SPLIT = 2


def shift_pairs(sizes, hi=0, row=0, core=0):
    contexts, experts, cores = sizes
    rows = contexts // ROW_SPLIT
    pairs = []
    for c in range(contexts):
        h, y = divmod(c, rows)
        target = (h + hi) % ROW_SPLIT * rows + (y + row) % rows
        for e in range(experts):
            for t in range(cores):
                pairs.append(
                    ((c * experts + e) * cores + t, (target * experts + e) * cores + (t + core) % cores)
                )
    return pairs


NT = (((1,), (1,)), ((), ()))
TILE = 512
WHOLE = pl.BlockSpec(memory_space=pltpu.VMEM)


def half_columns(core, width, start, size):
    return pl.ds(pl.multiple_of(core * width + start, TILE), size)


def wide_product(core, mine_ref, other_ref, weight_ref):
    width = mine_ref.shape[1]
    left = lax.dot_general(
        mine_ref[...],
        weight_ref[:, half_columns(core, width, 0, width)],
        NT,
        preferred_element_type=jnp.float32,
    )
    right = lax.dot_general(
        other_ref[...],
        weight_ref[:, half_columns(1 - core, width, 0, width)],
        NT,
        preferred_element_type=jnp.float32,
    )
    return left + right


def deep_product(core, left, weight_ref, kept_ref, given_ref):
    width = kept_ref.shape[1]
    for side, out_ref in ((1 - core, given_ref), (core, kept_ref)):
        for start in range(0, width, TILE):
            out_ref[:, start : start + TILE] = jnp.dot(
                left,
                weight_ref[:, half_columns(side, width, start, TILE)],
                preferred_element_type=jnp.float32,
            ).astype(jnp.bfloat16)


def forward_kernel(core_ref, mine_ref, other_ref, gate_ref, down_ref, pre_ref, kept_ref, given_ref):
    core = core_ref[0]
    pre = wide_product(core, mine_ref, other_ref, gate_ref)
    pre_ref[...] = pre
    hidden = (pre / (1.0 + jnp.exp(-pre))).astype(jnp.bfloat16)
    deep_product(core, hidden, down_ref, kept_ref, given_ref)


def backward_kernel(core_ref, mine_ref, other_ref, down_ref, gate_ref, pre_ref, kept_ref, given_ref):
    core = core_ref[0]
    grad = wide_product(core, mine_ref, other_ref, down_ref)
    pre = pre_ref[...]
    sigma = 1.0 / (1.0 + jnp.exp(-pre))
    pre_grad = (grad * (sigma * (1.0 + pre * (1.0 - sigma)))).astype(jnp.bfloat16)
    deep_product(core, pre_grad, gate_ref, kept_ref, given_ref)


def expert_call(kernel, core, mine, other, first, second, pre=None):
    rows, width = mine.shape
    units = first.shape[0]
    half = jax.ShapeDtypeStruct((rows, width), jnp.bfloat16)
    outs = [half, half]
    args = [core, mine, other, first, second]
    if pre is None:
        outs = [jax.ShapeDtypeStruct((rows, units), jnp.float32)] + outs
    else:
        args = args + [pre]
    return pl.pallas_call(
        kernel,
        out_shape=tuple(outs),
        in_specs=[pl.BlockSpec(memory_space=pltpu.SMEM)] + [WHOLE] * (len(args) - 1),
        out_specs=tuple([WHOLE] * len(outs)),
        compiler_params=pltpu.CompilerParams(vmem_limit_bytes=24 * 1024 * 1024),
        cost_estimate=pl.CostEstimate(
            flops=8 * rows * width * units, bytes_accessed=8 * units * width, transcendentals=rows * units
        ),
    )(*args)


def load_kernel(source, target, sem):
    copy = pltpu.make_async_copy(source, target, sem)
    copy.start()
    copy.wait()


def load_weights(*weights):
    return [
        pl.pallas_call(
            load_kernel,
            out_shape=jax.ShapeDtypeStruct(weight.shape, weight.dtype),
            in_specs=[pl.BlockSpec(memory_space=pl.ANY)],
            out_specs=WHOLE,
            scratch_shapes=[pltpu.SemaphoreType.DMA],
            compiler_params=pltpu.CompilerParams(vmem_limit_bytes=44 * 1024 * 1024),
        )(weight)
        for weight in weights
    ]


def slot_positions(ids_ref, tok_count, top_count, capacity):
    names = [ids_ref[n, k] for n in range(tok_count) for k in range(top_count)]
    positions = []
    for i, name in enumerate(names):
        slot = jnp.int32(0)
        for other in names[:i]:
            slot = slot + jnp.where(other == name, 1, 0)
        positions.append(name * capacity + slot)
    return positions


def dispatch_kernel(
    capacity, core_ref, ids_ref, weights_ref, tokens_ref, cotangent_ref, sent_ref, core_out
):
    core_out[0] = core_ref[0]
    tok_count, width = tokens_ref.shape
    top_count = ids_ref.shape[1]
    rows = sent_ref.shape[0]
    positions = slot_positions(ids_ref, tok_count, top_count, capacity)
    place = lax.broadcasted_iota(jnp.int32, (rows, 1), 0)
    chosen, weighted = [], []
    for n in range(tok_count):
        plain = jnp.zeros((rows, 1), jnp.float32)
        scaled = jnp.zeros((rows, 1), jnp.float32)
        for k in range(top_count):
            here = place == positions[n * top_count + k]
            plain = jnp.where(here, 1.0, plain)
            scaled = jnp.where(here, weights_ref[n, k], scaled)
        chosen.append(plain)
        weighted.append(scaled)
    for source_ref, masks, base in ((tokens_ref, chosen, 0), (cotangent_ref, weighted, width)):
        for start in range(0, width, 512):
            values = source_ref[:, start : start + 512].astype(jnp.float32)
            total = masks[0] * values[0:1]
            for n in range(1, tok_count):
                total = total + masks[n] * values[n : n + 1]
            sent_ref[:, base + start : base + start + 512] = total.astype(jnp.bfloat16)


def dispatch_rows(core, tokens, expert_ids, combine_weights, cotangent, experts, capacity):
    scalars = pl.BlockSpec(memory_space=pltpu.SMEM)
    return pl.pallas_call(
        functools.partial(dispatch_kernel, capacity),
        out_shape=(
            jax.ShapeDtypeStruct((experts * capacity, 2 * tokens.shape[1]), jnp.bfloat16),
            jax.ShapeDtypeStruct((1,), jnp.int32),
        ),
        in_specs=[scalars, scalars, scalars, WHOLE, WHOLE],
        out_specs=(WHOLE, scalars),
        compiler_params=pltpu.CompilerParams(vmem_limit_bytes=58 * 1024 * 1024),
    )(core.reshape(1), expert_ids, combine_weights, tokens, cotangent)


def combine_kernel(capacity, ids_ref, weights_ref, returned_ref, out_ref, back_ref, pairs_ref):
    tok_count, width = out_ref.shape
    top_count = ids_ref.shape[1]
    rows = returned_ref.shape[0]
    positions = slot_positions(ids_ref, tok_count, top_count, capacity)
    line = lax.broadcasted_iota(jnp.int32, (8, rows), 0)
    place = lax.broadcasted_iota(jnp.int32, (8, rows), 1)
    chosen = jnp.zeros((8, rows), jnp.float32)
    weighted = jnp.zeros((8, rows), jnp.float32)
    lane = lax.broadcasted_iota(jnp.int32, (1, 128), 1)
    pair_place = jnp.full((1, 128), -1, jnp.int32)
    pair_weight = jnp.ones((1, 128), jnp.float32)
    for i, position in enumerate(positions):
        n, k = divmod(i, top_count)
        here = (line == n) & (place == position)
        chosen = jnp.where(here, 1.0, chosen)
        weighted = jnp.where(here, weights_ref[n, k], weighted)
        pair_place = jnp.where(lane == i, position, pair_place)
        pair_weight = jnp.where(lane == i, weights_ref[n, k], pair_weight)
    high = weighted.astype(jnp.bfloat16)
    rest = weighted - high.astype(jnp.float32)
    middle = rest.astype(jnp.bfloat16)
    low = (rest - middle.astype(jnp.float32)).astype(jnp.bfloat16)
    plain = chosen.astype(jnp.bfloat16)
    for start in range(0, width, 512):
        values = returned_ref[:, start : start + 512]
        total = jnp.dot(high, values, preferred_element_type=jnp.float32)
        total = total + jnp.dot(middle, values, preferred_element_type=jnp.float32)
        total = total + jnp.dot(low, values, preferred_element_type=jnp.float32)
        out_ref[:, start : start + 512] = total[:tok_count].astype(jnp.bfloat16)
        values = returned_ref[:, width + start : width + start + 512]
        total = jnp.dot(plain, values, preferred_element_type=jnp.float32)
        back_ref[:, start : start + 512] = total[:tok_count].astype(jnp.bfloat16)
    extra = returned_ref[:, 2 * width : 2 * width + 128].astype(jnp.float32)
    row_values = jnp.sum(extra, 1, keepdims=True)
    match = lax.broadcasted_iota(jnp.int32, (rows, 128), 0) == pair_place
    pairs = jnp.sum(jnp.where(match, row_values, 0.0), 0, keepdims=True) / pair_weight
    for n in range(tok_count):
        pairs_ref[n : n + 1, :] = pairs[:, n * top_count : (n + 1) * top_count]


def combine_rows(expert_ids, combine_weights, returned, width, capacity):
    scalars = pl.BlockSpec(memory_space=pltpu.SMEM)
    tok_count = expert_ids.shape[0]
    half = jax.ShapeDtypeStruct((tok_count, width), jnp.bfloat16)
    return pl.pallas_call(
        functools.partial(combine_kernel, capacity),
        out_shape=(half, half, jax.ShapeDtypeStruct(expert_ids.shape, jnp.float32)),
        in_specs=[scalars, scalars, WHOLE],
        out_specs=(WHOLE, WHOLE, WHOLE),
        compiler_params=pltpu.CompilerParams(vmem_limit_bytes=8 * 1024 * 1024),
    )(expert_ids, combine_weights, returned)


def shards(sizes, tokens, expert_ids, combine_weights, cotangent, gate_weight, down_weight):
    half_width = tokens.shape[1]
    gate = gate_weight[0].T
    down = down_weight[0]
    experts = sizes[1]
    capacity = 2
    member_rows = experts * capacity

    def move(value, **shift):
        return lax.ppermute(value, AXES, shift_pairs(sizes, **shift))

    def exchange(rows):
        sent = rows.reshape(experts, capacity, rows.shape[1])
        got = lax.all_to_all(sent, "exp", split_axis=0, concat_axis=0, tiled=True)
        return got.reshape(rows.shape)

    def add(*terms):
        return sum(t.astype(jnp.float32) for t in terms).astype(jnp.bfloat16)

    def gather(blocks, weights):
        stacked = jnp.concatenate(blocks, 0)
        across, far, gate, down = lax.optimization_barrier(
            (move(stacked, hi=1), move(stacked, row=2), *weights)
        )
        results = []
        for i, block in enumerate(blocks):
            part = slice(i * member_rows, (i + 1) * member_rows)
            pair = jnp.concatenate([block, across[part]], 0)
            results.append([pair, move(pair, row=1), move(pair, row=-1), far[part]])
        across_far = move(far, hi=1)
        for i, pieces in enumerate(results):
            part = slice(i * member_rows, (i + 1) * member_rows)
            mine = jnp.concatenate(pieces + [across_far[part]], 0)
            results[i] = (mine, move(mine, core=1))
        return results, gate, down

    def scatter(kept, given):
        total = add(kept, move(given, core=1))
        own, across, below, above, far, across_far = jnp.split(
            total, [member_rows * i for i in (1, 2, 4, 6, 7)], 0
        )
        got_below = move(below, row=-1)
        got_above = move(above, row=1)
        far = add(far, move(across_far, hi=1))
        across = add(across, got_below[member_rows:], got_above[member_rows:])
        got_across = move(across, hi=1)
        got_far = move(far, row=2)
        return add(own, got_below[:member_rows], got_above[:member_rows], got_across, got_far)

    sent, core = dispatch_rows(
        lax.axis_index("tp"), tokens, expert_ids, combine_weights, cotangent, experts, capacity
    )
    arrived = exchange(sent)
    arrived, gate, down = lax.optimization_barrier((arrived, gate, down))
    gate, down = load_weights(gate, down)
    grad_block = arrived[:, half_width:]
    (routed_rows, routed_grad), gate, down = gather(
        (arrived[:, :half_width], grad_block), (gate, down)
    )
    pre, out_kept, out_given = expert_call(forward_kernel, core, *routed_rows, gate, down)
    back_kept, back_given = expert_call(backward_kernel, core, *routed_grad, down, gate, pre)
    out_block = scatter(out_kept, out_given)
    pair_half = jnp.sum(
        out_block.astype(jnp.float32) * grad_block.astype(jnp.float32), 1, keepdims=True
    )
    pair_value = pair_half + move(pair_half, core=1)
    pieces = []
    for _ in range(3):
        piece = pair_value.astype(jnp.bfloat16)
        pieces.append(piece)
        pair_value = pair_value - piece.astype(jnp.float32)
    back_block = scatter(back_kept, back_given)
    extra = jnp.concatenate(pieces + [jnp.zeros((member_rows, 125), jnp.bfloat16)], 1)
    returned = exchange(jnp.concatenate([out_block, back_block, extra], 1))

    return combine_rows(expert_ids, combine_weights, returned, half_width, capacity)


def solution(mesh):
    sizes = tuple(mesh.shape[name] for name in AXES)

    def block(*args):
        return shards(sizes, *args)

    in_specs = (
        P(("ctx", "exp"), "tp"),
        P(("ctx", "exp"), None),
        P(("ctx", "exp"), None),
        P(("ctx", "exp"), "tp"),
        P("exp", None, ("ctx", "tp")),
        P("exp", ("ctx", "tp"), None),
    )
    out_specs = (P(("ctx", "exp"), "tp"), P(("ctx", "exp"), "tp"), P(("ctx", "exp"), None))
    return jax.shard_map(block, mesh=mesh, in_specs=in_specs, out_specs=out_specs, check_vma=False)
```

time: 160 us -> 128 us (0.80)
  the two profiles are of different devices: /device:TPU:8 before, /device:TPU:4 now
where the time goes in v2:
time: 128 us
  blocking collectives  40.8 us (32%)
  starting transfers between devices  32.6 us (25%)
  waiting for transfers between devices  31.5 us (25%)
  Pallas kernels  17.5 us (14%)
  local copies, waits for them, and re-layouts  2.36 us (2%)
  other arithmetic  1.92 us (2%)
    all_to_all x2, blocking collectives, exchange(): got = lax.all_to_all(sent, 'exp', split_axis=0, concat_axis=0, tiled=True)  40.8 us
    ppermute x22, starting transfers between devices, move(): return lax.ppermute(value, AXES, shift_pairs(sizes, **shift))  32.6 us
    ppermute x22, waiting for transfers between devices, move(): return lax.ppermute(value, AXES, shift_pairs(sizes, **shift))  31.5 us
    pallas_call x2, Pallas kernels, expert_call(): pl.pallas_call(kernel, out_shape=tuple(outs), in_specs=[pl.BlockSpec(memo...  8.5 us
    pallas_call x2, Pallas kernels, load_weights(): pl.pallas_call(load_kernel, out_shape=jax.ShapeDtypeStruct(weight.shape,...  5.53 us
  transfers between devices with their start and end apart: 22, of which 11 were waited for; matrix products, arithmetic and copies ran while one was open for 2% of the time, Pallas kernels for 11%

profile of v2, /device:TPU:4, one launch (start us, length us, event | category | flops | bytes accessed | tf_op | source)
XLA Modules:
  0.0 127.6 jit_solution(16766021597861958524)
XLA Ops:
  0.6 1.9 %shard_map.85 = (bf16[32,6144]{1,0:T(8,128)(2,1)}, s32[1]{0:T(128)}) custom-call(s32[1]{0:T(128)} %bitcast.core_ref, s32[4,4]{1,0:T(4,128)} %ids_ref.3, f32[4,4]{1,0:T(4,128)} %weights_ref.3, bf16[4,3072]{1,0:T(4,128)(2,1)} %tokens_ref.1, bf16[4,3072]{1,0:T(4,128)(2,1)} %cotangent_ref.1), custom_call_target="tpu_custom_call" | custom-call | tf_op jit(solution)/shard_map/pallas_call | solution.py:166
  2.5 1.3 reshape.22
  3.8 21.6 %all_to_all.10 = bf16[16,2,6144]{2,1,0:T(2,128)(2,1)S(1)} all-to-all(bf16[16,2,6144]{2,1,0:T(2,128)(2,1)S(1)} %reshape.22), channel_id=1, replica_groups=mesh['ctx'=8,'exp'=16,'tp'=2] {'exp'}, dimensions={0} | all-to-all | bytes 786432 | tf_op jit(solution)/shard_map/all_to_all | solution.py:245
  25.7 0.9 collective-permute-start
  26.6 3.2 %collective-permute-start.1 = (bf16[64,3072]{1,0:T(8,128)(2,1)S(1)}, bf16[64,3072]{1,0:T(8,128)(2,1)S(1)}, u32[]{:S(2)}, u32[]{:S(2)}) collective-permute-start(bf16[64,3072]{1,0:T(8,128)(2,1)S(1)} %pad_maximum_fusion.1), channel_id=1, source_target_pairs={{0,64},{1,65},{2,66},{3,67},{4,68},{5,69},{6,70},{7,71},{8,72},{9,... | collective-permute-start | bytes 1179656 | tf_op jit(solution)/shard_map/ppermute | solution.py:241
  29.8 2.8 %shard_map.86.gate_ref = bf16[504,6144]{1,0:T(8,128)(2,1)S(1)} custom-call(bf16[504,6144]{1,0:T(8,128)(2,1)} %bitcast.7), custom_call_target="tpu_custom_call" | custom-call | tf_op jit(solution)/shard_map/pallas_call | solution.py:113
  32.5 2.8 %shard_map.87.down_ref = bf16[504,6144]{1,0:T(8,128)(2,1)S(1)} custom-call(bf16[504,6144]{1,0:T(8,128)(2,1)} %bitcast.8), custom_call_target="tpu_custom_call" | custom-call | tf_op jit(solution)/shard_map/pallas_call | solution.py:113
  35.3 0.9 collective-permute-done
  36.9 1.7 %collective-permute-start.2 = (bf16[64,3072]{1,0:T(8,128)(2,1)S(1)}, bf16[64,3072]{1,0:T(8,128)(2,1)S(1)}, u32[]{:S(2)}, u32[]{:S(2)}) collective-permute-start(bf16[64,3072]{1,0:T(8,128)(2,1)S(1)} %pad_maximum_fusion), channel_id=1, source_target_pairs={{0,32},{1,33},{2,34},{3,35},{4,36},{5,37},{6,38},{7,39},{8,40},{9,... | collective-permute-start | bytes 1179656 | tf_op jit(solution)/shard_map/ppermute | solution.py:241
  38.5 1.7 %collective-permute-start.3 = (bf16[64,3072]{1,0:T(8,128)(2,1)S(1)}, bf16[64,3072]{1,0:T(8,128)(2,1)S(1)}, u32[]{:S(2)}, u32[]{:S(2)}) collective-permute-start(bf16[64,3072]{1,0:T(8,128)(2,1)S(1)} %pad_maximum_fusion), channel_id=1, source_target_pairs={{0,96},{1,97},{2,98},{3,99},{4,100},{5,101},{6,102},{7,103},{8,104... | collective-permute-start | bytes 1179656 | tf_op jit(solution)/shard_map/ppermute | solution.py:241
  40.7 2.8 %collective-permute-start.13 = (bf16[64,3072]{1,0:T(8,128)(2,1)S(1)}, bf16[64,3072]{1,0:T(8,128)(2,1)S(1)}, u32[]{:S(2)}, u32[]{:S(2)}) collective-permute-start(bf16[64,3072]{1,0:T(8,128)(2,1)S(1)} %pad_maximum_fusion.2), channel_id=1, source_target_pairs={{0,96},{1,97},{2,98},{3,99},{4,100},{5,101},{6,102},{7,103},{8,104... | collective-permute-start | bytes 1179656 | tf_op jit(solution)/shard_map/ppermute | solution.py:241
  43.5 2.7 %collective-permute-start.4 = (bf16[64,3072]{1,0:T(8,128)(2,1)S(1)}, bf16[64,3072]{1,0:T(8,128)(2,1)S(1)}, u32[]{:S(2)}, u32[]{:S(2)}) collective-permute-start(bf16[64,3072]{1,0:T(8,128)(2,1)S(1)} %collective-permute-done.1), channel_id=1, source_target_pairs={{0,128},{1,129},{2,130},{3,131},{4,132},{5,133},{6,134},{7,135},{8... | collective-permute-start | bytes 1179656 | tf_op jit(solution)/shard_map/ppermute | solution.py:241
  46.3 4.0 %collective-permute-done.2 = bf16[64,3072]{1,0:T(8,128)(2,1)S(1)} collective-permute-done((bf16[64,3072]{1,0:T(8,128)(2,1)S(1)}, bf16[64,3072]{1,0:T(8,128)(2,1)S(1)}, u32[]{:S(2)}, u32[]{:S(2)}) %collective-permute-start.2) | collective-permute-done | bytes 393248 | tf_op jit(solution)/shard_map/ppermute | solution.py:241
  50.3 4.1 %collective-permute-done.12 = bf16[64,3072]{1,0:T(8,128)(2,1)S(1)} collective-permute-done((bf16[64,3072]{1,0:T(8,128)(2,1)S(1)}, bf16[64,3072]{1,0:T(8,128)(2,1)S(1)}, u32[]{:S(2)}, u32[]{:S(2)}) %collective-permute-start.12) | collective-permute-done | bytes 393248 | tf_op jit(solution)/shard_map/ppermute | solution.py:241
  55.2 2.9 %collective-permute-done.5.other_ref = bf16[256,3072]{1,0:T(8,128)(2,1)S(1)} collective-permute-done((bf16[256,3072]{1,0:T(8,128)(2,1)S(1)}, bf16[256,3072]{1,0:T(8,128)(2,1)S(1)}, u32[]{:S(2)}, u32[]{:S(2)}) %collective-permute-start.5) | collective-permute-done | bytes 1572896 | tf_op jit(solution)/shard_map/ppermute | solution.py:241
  58.1 4.3 %shard_map.88 = (f32[256,504]{1,0:T(8,128)S(1)}, bf16[256,3072]{1,0:T(8,128)(2,1)S(1)}, bf16[256,3072]{1,0:T(8,128)(2,1)S(1)}) custom-call(s32[1]{0:T(128)} %get-tuple-element.17.core_ref, bf16[256,3072]{1,0:T(8,128)(2,1)S(1)} %get-tuple-element.42.mine_ref, bf16[256,3072]{1,0:T(8,128)(2,1)S(1)} %collective-permute-done.5.other_ref, ...), custom_call_target="tpu_custom_call" | custom-call | flops 3170893824 | bytes 12386304 | tf_op jit(solution)/shard_map/pallas_call | solution.py:93
  62.8 4.2 %shard_map.89 = (bf16[256,3072]{1,0:T(8,128)(2,1)S(1)}, bf16[256,3072]{1,0:T(8,128)(2,1)S(1)}) custom-call(s32[1]{0:T(128)} %get-tuple-element.17.core_ref, bf16[256,3072]{1,0:T(8,128)(2,1)S(1)} %get-tuple-element.41.mine_ref, bf16[256,3072]{1,0:T(8,128)(2,1)S(1)} %collective-permute-done.14.other_ref, bf16[504,6144]{1,0:T(8,128)(2,1)S(1)} %shard_map.87.down_ref, ...), custom_call_target="tpu_custom_call" | custom-call | flops 3170893824 | bytes 12386304 | tf_op jit(solution)/shard_map/pallas_call | solution.py:93
  68.2 3.1 %collective-permute-start.7 = (bf16[64,3072]{1,0:T(8,128)(2,1)S(1)}, bf16[64,3072]{1,0:T(8,128)(2,1)S(1)}, u32[]{:S(2)}, u32[]{:S(2)}) collective-permute-start(bf16[64,3072]{1,0:T(8,128)(2,1)S(1)} %get-tuple-element.39), channel_id=1, source_target_pairs={{0,96},{1,97},{2,98},{3,99},{4,100},{5,101},{6,102},{7,103},{8,104... | collective-permute-start | bytes 1179656 | tf_op jit(solution)/shard_map/ppermute | solution.py:241
  71.2 2.7 %collective-permute-start.10 = (bf16[32,3072]{1,0:T(8,128)(2,1)S(1)}, bf16[32,3072]{1,0:T(8,128)(2,1)S(1)}, u32[]{:S(2)}, u32[]{:S(2)}) collective-permute-start(bf16[32,3072]{1,0:T(8,128)(2,1)S(1)} %split.53), channel_id=1, source_target_pairs={{0,128},{1,129},{2,130},{3,131},{4,132},{5,133},{6,134},{7,135},{8... | collective-permute-start | bytes 589832 | tf_op jit(solution)/shard_map/ppermute | solution.py:241
  74.0 0.6 add_convert_fusion
  74.6 3.3 %collective-permute-start.16 = (bf16[64,3072]{1,0:T(8,128)(2,1)S(1)}, bf16[64,3072]{1,0:T(8,128)(2,1)S(1)}, u32[]{:S(2)}, u32[]{:S(2)}) collective-permute-start(bf16[64,3072]{1,0:T(8,128)(2,1)S(1)} %get-tuple-element.35), channel_id=1, source_target_pairs={{0,96},{1,97},{2,98},{3,99},{4,100},{5,101},{6,102},{7,103},{8,104... | collective-permute-start | bytes 1179656 | tf_op jit(solution)/shard_map/ppermute | solution.py:241
  78.0 1.4 %collective-permute-done.10 = bf16[32,3072]{1,0:T(8,128)(2,1)S(1)} collective-permute-done((bf16[32,3072]{1,0:T(8,128)(2,1)S(1)}, bf16[32,3072]{1,0:T(8,128)(2,1)S(1)}, u32[]{:S(2)}, u32[]{:S(2)}) %collective-permute-start.10) | collective-permute-done | bytes 196640 | tf_op jit(solution)/shard_map/ppermute | solution.py:241
  79.4 2.7 %collective-permute-start.19 = (bf16[32,3072]{1,0:T(8,128)(2,1)S(1)}, bf16[32,3072]{1,0:T(8,128)(2,1)S(1)}, u32[]{:S(2)}, u32[]{:S(2)}) collective-permute-start(bf16[32,3072]{1,0:T(8,128)(2,1)S(1)} %split.59), channel_id=1, source_target_pairs={{0,128},{1,129},{2,130},{3,131},{4,132},{5,133},{6,134},{7,135},{8... | collective-permute-start | bytes 589832 | tf_op jit(solution)/shard_map/ppermute | solution.py:241
  82.1 2.3 %collective-permute-done.8 = bf16[64,3072]{1,0:T(8,128)(2,1)S(1)} collective-permute-done((bf16[64,3072]{1,0:T(8,128)(2,1)S(1)}, bf16[64,3072]{1,0:T(8,128)(2,1)S(1)}, u32[]{:S(2)}, u32[]{:S(2)}) %collective-permute-start.8) | collective-permute-done | bytes 393248 | tf_op jit(solution)/shard_map/ppermute | solution.py:241
  84.7 2.8 %collective-permute-start.9 = (bf16[32,3072]{1,0:T(8,128)(2,1)S(1)}, bf16[32,3072]{1,0:T(8,128)(2,1)S(1)}, u32[]{:S(2)}, u32[]{:S(2)}) collective-permute-start(bf16[32,3072]{1,0:T(8,128)(2,1)S(1)} %get-tuple-element.37), channel_id=1, source_target_pairs={{0,128},{1,129},{2,130},{3,131},{4,132},{5,133},{6,134},{7,135},{8... | collective-permute-start | bytes 589832 | tf_op jit(solution)/shard_map/ppermute | solution.py:241
  87.5 5.1 %collective-permute-done.16 = bf16[64,3072]{1,0:T(8,128)(2,1)S(1)} collective-permute-done((bf16[64,3072]{1,0:T(8,128)(2,1)S(1)}, bf16[64,3072]{1,0:T(8,128)(2,1)S(1)}, u32[]{:S(2)}, u32[]{:S(2)}) %collective-permute-start.16) | collective-permute-done | bytes 393248 | tf_op jit(solution)/shard_map/ppermute | solution.py:241
  92.5 3.4 %collective-permute-done.17 = bf16[64,3072]{1,0:T(8,128)(2,1)S(1)} collective-permute-done((bf16[64,3072]{1,0:T(8,128)(2,1)S(1)}, bf16[64,3072]{1,0:T(8,128)(2,1)S(1)}, u32[]{:S(2)}, u32[]{:S(2)}) %collective-permute-start.17) | collective-permute-done | bytes 393248 | tf_op jit(solution)/shard_map/ppermute | solution.py:241
  96.1 2.8 %collective-permute-start.18 = (bf16[32,3072]{1,0:T(8,128)(2,1)S(1)}, bf16[32,3072]{1,0:T(8,128)(2,1)S(1)}, u32[]{:S(2)}, u32[]{:S(2)}) collective-permute-start(bf16[32,3072]{1,0:T(8,128)(2,1)S(1)} %get-tuple-element.33), channel_id=1, source_target_pairs={{0,128},{1,129},{2,130},{3,131},{4,132},{5,133},{6,134},{7,135},{8... | collective-permute-start | bytes 589832 | tf_op jit(solution)/shard_map/ppermute | solution.py:241
  99.3 4.2 %collective-permute-done.18 = bf16[32,3072]{1,0:T(8,128)(2,1)S(1)} collective-permute-done((bf16[32,3072]{1,0:T(8,128)(2,1)S(1)}, bf16[32,3072]{1,0:T(8,128)(2,1)S(1)}, u32[]{:S(2)}, u32[]{:S(2)}) %collective-permute-start.18) | collective-permute-done | bytes 196640 | tf_op jit(solution)/shard_map/ppermute | solution.py:241
  103.5 2.6 %collective-permute-done.20 = bf16[32,3072]{1,0:T(8,128)(2,1)S(1)} collective-permute-done((bf16[32,3072]{1,0:T(8,128)(2,1)S(1)}, bf16[32,3072]{1,0:T(8,128)(2,1)S(1)}, u32[]{:S(2)}, u32[]{:S(2)}) %collective-permute-start.20) | collective-permute-done | bytes 196640 | tf_op jit(solution)/shard_map/ppermute | solution.py:241
  106.6 19.1 %all_to_all.11 = bf16[16,2,6272]{2,1,0:T(2,128)(2,1)S(1)} all-to-all(bf16[16,2,6272]{2,1,0:T(2,128)(2,1)S(1)} %reshape.24), channel_id=1, replica_groups=mesh['ctx'=8,'exp'=16,'tp'=2] {'exp'}, dimensions={0} | all-to-all | bytes 802816 | tf_op jit(solution)/shard_map/all_to_all | solution.py:245
  126.0 1.6 %shard_map.90 = (bf16[4,3072]{1,0:T(4,128)(2,1)}, bf16[4,3072]{1,0:T(4,128)(2,1)}, f32[4,4]{1,0:T(4,128)}) custom-call(s32[4,4]{1,0:T(4,128)S(1)} %copy-done, f32[4,4]{1,0:T(4,128)S(1)} %copy-done.1, bf16[32,6272]{1,0:T(8,128)(2,1)S(1)} %reshape.25.returned_ref), custom_call_target="tpu_custom_call" | custom-call | tf_op jit(solution)/shard_map/pallas_call | solution.py:223
  (54 shorter events, 5.1 us)
Async XLA Ops:
  25.7 10.6 %collective-permute-start = (bf16[64,3072]{1,0:T(8,128)(2,1)S(1)}, bf16[64,3072]{1,0:T(8,128)(2,1)S(1)}, u32[]{:S(2)}, u32[]{:S(2)}) collective-permute-start(bf16[64,3072]{1,0:T(8,128)(2,1)S(1)} %pad_maximum_fusion.1), channel_id=1, source_target_pairs={{0,128},{1,129},{2,130},{3,131},{4,132},{5,133},{6,134},{7,135},{8... | collective-permute-start | bytes 1179656 | tf_op jit(solution)/shard_map/ppermute | solution.py:241
  26.6 10.2 %collective-permute-start.1 = (bf16[64,3072]{1,0:T(8,128)(2,1)S(1)}, bf16[64,3072]{1,0:T(8,128)(2,1)S(1)}, u32[]{:S(2)}, u32[]{:S(2)}) collective-permute-start(bf16[64,3072]{1,0:T(8,128)(2,1)S(1)} %pad_maximum_fusion.1), channel_id=1, source_target_pairs={{0,64},{1,65},{2,66},{3,67},{4,68},{5,69},{6,70},{7,71},{8,72},{9,... | collective-permute-start | bytes 1179656 | tf_op jit(solution)/shard_map/ppermute | solution.py:241
  36.9 13.3 %collective-permute-start.2 = (bf16[64,3072]{1,0:T(8,128)(2,1)S(1)}, bf16[64,3072]{1,0:T(8,128)(2,1)S(1)}, u32[]{:S(2)}, u32[]{:S(2)}) collective-permute-start(bf16[64,3072]{1,0:T(8,128)(2,1)S(1)} %pad_maximum_fusion), channel_id=1, source_target_pairs={{0,32},{1,33},{2,34},{3,35},{4,36},{5,37},{6,38},{7,39},{8,40},{9,... | collective-permute-start | bytes 1179656 | tf_op jit(solution)/shard_map/ppermute | solution.py:241
  38.5 11.7 %collective-permute-start.3 = (bf16[64,3072]{1,0:T(8,128)(2,1)S(1)}, bf16[64,3072]{1,0:T(8,128)(2,1)S(1)}, u32[]{:S(2)}, u32[]{:S(2)}) collective-permute-start(bf16[64,3072]{1,0:T(8,128)(2,1)S(1)} %pad_maximum_fusion), channel_id=1, source_target_pairs={{0,96},{1,97},{2,98},{3,99},{4,100},{5,101},{6,102},{7,103},{8,104... | collective-permute-start | bytes 1179656 | tf_op jit(solution)/shard_map/ppermute | solution.py:241
  40.2 14.2 %collective-permute-start.12 = (bf16[64,3072]{1,0:T(8,128)(2,1)S(1)}, bf16[64,3072]{1,0:T(8,128)(2,1)S(1)}, u32[]{:S(2)}, u32[]{:S(2)}) collective-permute-start(bf16[64,3072]{1,0:T(8,128)(2,1)S(1)} %pad_maximum_fusion.2), channel_id=1, source_target_pairs={{0,32},{1,33},{2,34},{3,35},{4,36},{5,37},{6,38},{7,39},{8,40},{9,... | collective-permute-start | bytes 1179656 | tf_op jit(solution)/shard_map/ppermute | solution.py:241
  40.7 13.7 %collective-permute-start.13 = (bf16[64,3072]{1,0:T(8,128)(2,1)S(1)}, bf16[64,3072]{1,0:T(8,128)(2,1)S(1)}, u32[]{:S(2)}, u32[]{:S(2)}) collective-permute-start(bf16[64,3072]{1,0:T(8,128)(2,1)S(1)} %pad_maximum_fusion.2), channel_id=1, source_target_pairs={{0,96},{1,97},{2,98},{3,99},{4,100},{5,101},{6,102},{7,103},{8,104... | collective-permute-start | bytes 1179656 | tf_op jit(solution)/shard_map/ppermute | solution.py:241
  43.5 11.0 %collective-permute-start.4 = (bf16[64,3072]{1,0:T(8,128)(2,1)S(1)}, bf16[64,3072]{1,0:T(8,128)(2,1)S(1)}, u32[]{:S(2)}, u32[]{:S(2)}) collective-permute-start(bf16[64,3072]{1,0:T(8,128)(2,1)S(1)} %collective-permute-done.1), channel_id=1, source_target_pairs={{0,128},{1,129},{2,130},{3,131},{4,132},{5,133},{6,134},{7,135},{8... | collective-permute-start | bytes 1179656 | tf_op jit(solution)/shard_map/ppermute | solution.py:241
  54.6 3.5 %collective-permute-start.5 = (bf16[256,3072]{1,0:T(8,128)(2,1)S(1)}, bf16[256,3072]{1,0:T(8,128)(2,1)S(1)}, u32[]{:S(2)}, u32[]{:S(2)}) collective-permute-start(bf16[256,3072]{1,0:T(8,128)(2,1)S(1)} %get-tuple-element.42.mine_ref), channel_id=1, source_target_pairs={{0,1},{1,0},{2,3},{3,2},{4,5},{5,4},{6,7},{7,6},{8,9},{9,8},{10,11... | collective-permute-start | bytes 4718600 | tf_op jit(solution)/shard_map/ppermute | solution.py:241
  54.7 8.1 %collective-permute-start.14 = (bf16[256,3072]{1,0:T(8,128)(2,1)S(1)}, bf16[256,3072]{1,0:T(8,128)(2,1)S(1)}, u32[]{:S(2)}, u32[]{:S(2)}) collective-permute-start(bf16[256,3072]{1,0:T(8,128)(2,1)S(1)} %get-tuple-element.41.mine_ref), channel_id=1, source_target_pairs={{0,1},{1,0},{2,3},{3,2},{4,5},{5,4},{6,7},{7,6},{8,9},{9,8},{10,11... | collective-permute-start | bytes 4718600 | tf_op jit(solution)/shard_map/ppermute | solution.py:241
  62.4 5.1 %collective-permute-start.6 = (bf16[256,3072]{1,0:T(8,128)(2,1)S(1)}, bf16[256,3072]{1,0:T(8,128)(2,1)S(1)}, u32[]{:S(2)}, u32[]{:S(2)}) collective-permute-start(bf16[256,3072]{1,0:T(8,128)(2,1)S(1)} %get-tuple-element.27), channel_id=1, source_target_pairs={{0,1},{1,0},{2,3},{3,2},{4,5},{5,4},{6,7},{7,6},{8,9},{9,8},{10,11... | collective-permute-start | bytes 4718600 | tf_op jit(solution)/shard_map/ppermute | solution.py:241
  67.0 6.9 %collective-permute-start.15 = (bf16[256,3072]{1,0:T(8,128)(2,1)S(1)}, bf16[256,3072]{1,0:T(8,128)(2,1)S(1)}, u32[]{:S(2)}, u32[]{:S(2)}) collective-permute-start(bf16[256,3072]{1,0:T(8,128)(2,1)S(1)} %get-tuple-element.30), channel_id=1, source_target_pairs={{0,1},{1,0},{2,3},{3,2},{4,5},{5,4},{6,7},{7,6},{8,9},{9,8},{10,11... | collective-permute-start | bytes 4718600 | tf_op jit(solution)/shard_map/ppermute | solution.py:241
  68.2 14.0 %collective-permute-start.7 = (bf16[64,3072]{1,0:T(8,128)(2,1)S(1)}, bf16[64,3072]{1,0:T(8,128)(2,1)S(1)}, u32[]{:S(2)}, u32[]{:S(2)}) collective-permute-start(bf16[64,3072]{1,0:T(8,128)(2,1)S(1)} %get-tuple-element.39), channel_id=1, source_target_pairs={{0,96},{1,97},{2,98},{3,99},{4,100},{5,101},{6,102},{7,103},{8,104... | collective-permute-start | bytes 1179656 | tf_op jit(solution)/shard_map/ppermute | solution.py:241
  71.2 13.2 %collective-permute-start.8 = (bf16[64,3072]{1,0:T(8,128)(2,1)S(1)}, bf16[64,3072]{1,0:T(8,128)(2,1)S(1)}, u32[]{:S(2)}, u32[]{:S(2)}) collective-permute-start(bf16[64,3072]{1,0:T(8,128)(2,1)S(1)} %get-tuple-element.40), channel_id=1, source_target_pairs={{0,32},{1,33},{2,34},{3,35},{4,36},{5,37},{6,38},{7,39},{8,40},{9,... | collective-permute-start | bytes 1179656 | tf_op jit(solution)/shard_map/ppermute | solution.py:241
  71.2 8.2 %collective-permute-start.10 = (bf16[32,3072]{1,0:T(8,128)(2,1)S(1)}, bf16[32,3072]{1,0:T(8,128)(2,1)S(1)}, u32[]{:S(2)}, u32[]{:S(2)}) collective-permute-start(bf16[32,3072]{1,0:T(8,128)(2,1)S(1)} %split.53), channel_id=1, source_target_pairs={{0,128},{1,129},{2,130},{3,131},{4,132},{5,133},{6,134},{7,135},{8... | collective-permute-start | bytes 589832 | tf_op jit(solution)/shard_map/ppermute | solution.py:241
  74.6 17.9 %collective-permute-start.16 = (bf16[64,3072]{1,0:T(8,128)(2,1)S(1)}, bf16[64,3072]{1,0:T(8,128)(2,1)S(1)}, u32[]{:S(2)}, u32[]{:S(2)}) collective-permute-start(bf16[64,3072]{1,0:T(8,128)(2,1)S(1)} %get-tuple-element.35), channel_id=1, source_target_pairs={{0,96},{1,97},{2,98},{3,99},{4,100},{5,101},{6,102},{7,103},{8,104... | collective-permute-start | bytes 1179656 | tf_op jit(solution)/shard_map/ppermute | solution.py:241
  78.0 18.0 %collective-permute-start.17 = (bf16[64,3072]{1,0:T(8,128)(2,1)S(1)}, bf16[64,3072]{1,0:T(8,128)(2,1)S(1)}, u32[]{:S(2)}, u32[]{:S(2)}) collective-permute-start(bf16[64,3072]{1,0:T(8,128)(2,1)S(1)} %get-tuple-element.36), channel_id=1, source_target_pairs={{0,32},{1,33},{2,34},{3,35},{4,36},{5,37},{6,38},{7,39},{8,40},{9,... | collective-permute-start | bytes 1179656 | tf_op jit(solution)/shard_map/ppermute | solution.py:241
  79.4 8.1 %collective-permute-start.19 = (bf16[32,3072]{1,0:T(8,128)(2,1)S(1)}, bf16[32,3072]{1,0:T(8,128)(2,1)S(1)}, u32[]{:S(2)}, u32[]{:S(2)}) collective-permute-start(bf16[32,3072]{1,0:T(8,128)(2,1)S(1)} %split.59), channel_id=1, source_target_pairs={{0,128},{1,129},{2,130},{3,131},{4,132},{5,133},{6,134},{7,135},{8... | collective-permute-start | bytes 589832 | tf_op jit(solution)/shard_map/ppermute | solution.py:241
  84.6 14.3 %collective-permute-start.11 = (bf16[32,3072]{1,0:T(8,128)(2,1)S(1)}, bf16[32,3072]{1,0:T(8,128)(2,1)S(1)}, u32[]{:S(2)}, u32[]{:S(2)}) collective-permute-start(bf16[32,3072]{1,0:T(8,128)(2,1)S(1)} %get-tuple-element.38), channel_id=1, source_target_pairs={{0,64},{1,65},{2,66},{3,67},{4,68},{5,69},{6,70},{7,71},{8,72},{9,... | collective-permute-start | bytes 589832 | tf_op jit(solution)/shard_map/ppermute | solution.py:241
  84.7 14.2 %collective-permute-start.9 = (bf16[32,3072]{1,0:T(8,128)(2,1)S(1)}, bf16[32,3072]{1,0:T(8,128)(2,1)S(1)}, u32[]{:S(2)}, u32[]{:S(2)}) collective-permute-start(bf16[32,3072]{1,0:T(8,128)(2,1)S(1)} %get-tuple-element.37), channel_id=1, source_target_pairs={{0,128},{1,129},{2,130},{3,131},{4,132},{5,133},{6,134},{7,135},{8... | collective-permute-start | bytes 589832 | tf_op jit(solution)/shard_map/ppermute | solution.py:241
  96.1 7.4 %collective-permute-start.18 = (bf16[32,3072]{1,0:T(8,128)(2,1)S(1)}, bf16[32,3072]{1,0:T(8,128)(2,1)S(1)}, u32[]{:S(2)}, u32[]{:S(2)}) collective-permute-start(bf16[32,3072]{1,0:T(8,128)(2,1)S(1)} %get-tuple-element.33), channel_id=1, source_target_pairs={{0,128},{1,129},{2,130},{3,131},{4,132},{5,133},{6,134},{7,135},{8... | collective-permute-start | bytes 589832 | tf_op jit(solution)/shard_map/ppermute | solution.py:241
  98.9 7.2 %collective-permute-start.20 = (bf16[32,3072]{1,0:T(8,128)(2,1)S(1)}, bf16[32,3072]{1,0:T(8,128)(2,1)S(1)}, u32[]{:S(2)}, u32[]{:S(2)}) collective-permute-start(bf16[32,3072]{1,0:T(8,128)(2,1)S(1)} %get-tuple-element.34), channel_id=1, source_target_pairs={{0,64},{1,65},{2,66},{3,67},{4,68},{5,69},{6,70},{7,71},{8,72},{9,... | collective-permute-start | bytes 589832 | tf_op jit(solution)/shard_map/ppermute | solution.py:241
  99.2 7.0 %collective-permute-start.21 = (f32[32,1]{0,1:T(1,128)S(1)}, f32[32,1]{0,1:T(1,128)S(1)}, u32[]{:S(2)}, u32[]{:S(2)}) collective-permute-start(f32[32,1]{0,1:T(1,128)S(1)} %bitcast.9), channel_id=1, source_target_pairs={{0,1},{1,0},{2,3},{3,2},{4,5},{5,4},{6,7},{7,6},{8,9},{9,8},{10,11... | collective-permute-start | bytes 392 | tf_op jit(solution)/shard_map/ppermute | solution.py:241
  106.3 19.6 %copy-start = (s32[4,4]{1,0:T(4,128)S(1)}, s32[4,4]{1,0:T(4,128)}, u32[]{:S(2)}) copy-start(s32[4,4]{1,0:T(4,128)} %ids_ref.3) | copy-start | bytes 196
  106.4 19.6 %copy-start.1 = (f32[4,4]{1,0:T(4,128)S(1)}, f32[4,4]{1,0:T(4,128)}, u32[]{:S(2)}) copy-start(f32[4,4]{1,0:T(4,128)} %weights_ref.3) | copy-start | bytes 196

commit v3 on v2

--- a/solution.py
+++ b/solution.py
@@ -35,21 +35,14 @@
     return pl.ds(pl.multiple_of(core * width + start, TILE), size)
 
 
-def wide_product(core, mine_ref, other_ref, weight_ref):
-    width = mine_ref.shape[1]
-    left = lax.dot_general(
-        mine_ref[...],
+def wide_product(core, rows_ref, weight_ref):
+    width = rows_ref.shape[1]
+    return lax.dot_general(
+        rows_ref[...],
         weight_ref[:, half_columns(core, width, 0, width)],
         NT,
         preferred_element_type=jnp.float32,
     )
-    right = lax.dot_general(
-        other_ref[...],
-        weight_ref[:, half_columns(1 - core, width, 0, width)],
-        NT,
-        preferred_element_type=jnp.float32,
-    )
-    return left + right
 
 
 def deep_product(core, left, weight_ref, kept_ref, given_ref):
@@ -63,41 +56,49 @@
             ).astype(jnp.bfloat16)
 
 
-def forward_kernel(core_ref, mine_ref, other_ref, gate_ref, down_ref, pre_ref, kept_ref, given_ref):
+def first_kernel(core_ref, rows_ref, grads_ref, gate_ref, down_ref, pre_ref, grad_ref):
+    pre_ref[...] = wide_product(core_ref[0], rows_ref, gate_ref)
+    grad_ref[...] = wide_product(core_ref[0], grads_ref, down_ref)
+
+
+def forward_kernel(
+    core_ref, partial_ref, other_ref, gate_ref, down_ref, pre_ref, kept_ref, given_ref
+):
     core = core_ref[0]
-    pre = wide_product(core, mine_ref, other_ref, gate_ref)
+    pre = partial_ref[...] + wide_product(1 - core, other_ref, gate_ref)
     pre_ref[...] = pre
     hidden = (pre / (1.0 + jnp.exp(-pre))).astype(jnp.bfloat16)
     deep_product(core, hidden, down_ref, kept_ref, given_ref)
 
 
-def backward_kernel(core_ref, mine_ref, other_ref, down_ref, gate_ref, pre_ref, kept_ref, given_ref):
+def backward_kernel(
+    core_ref, partial_ref, other_ref, down_ref, gate_ref, pre_ref, kept_ref, given_ref
+):
     core = core_ref[0]
-    grad = wide_product(core, mine_ref, other_ref, down_ref)
+    grad = partial_ref[...] + wide_product(1 - core, other_ref, down_ref)
     pre = pre_ref[...]
     sigma = 1.0 / (1.0 + jnp.exp(-pre))
     pre_grad = (grad * (sigma * (1.0 + pre * (1.0 - sigma)))).astype(jnp.bfloat16)
     deep_product(core, pre_grad, gate_ref, kept_ref, given_ref)
 
 
-def expert_call(kernel, core, mine, other, first, second, pre=None):
-    rows, width = mine.shape
-    units = first.shape[0]
-    half = jax.ShapeDtypeStruct((rows, width), jnp.bfloat16)
-    outs = [half, half]
-    args = [core, mine, other, first, second]
-    if pre is None:
-        outs = [jax.ShapeDtypeStruct((rows, units), jnp.float32)] + outs
-    else:
-        args = args + [pre]
+def expert_call(kernel, outs, args, products):
+    rows, width = args[2].shape
+    units = args[3].shape[0]
+    shapes = {
+        "units": jax.ShapeDtypeStruct((rows, units), jnp.float32),
+        "half": jax.ShapeDtypeStruct((rows, width), jnp.bfloat16),
+    }
     return pl.pallas_call(
         kernel,
-        out_shape=tuple(outs),
+        out_shape=tuple(shapes[name] for name in outs),
         in_specs=[pl.BlockSpec(memory_space=pltpu.SMEM)] + [WHOLE] * (len(args) - 1),
         out_specs=tuple([WHOLE] * len(outs)),
         compiler_params=pltpu.CompilerParams(vmem_limit_bytes=24 * 1024 * 1024),
         cost_estimate=pl.CostEstimate(
-            flops=8 * rows * width * units, bytes_accessed=8 * units * width, transcendentals=rows * units
+            flops=2 * products * rows * width * units,
+            bytes_accessed=products * units * width,
+            transcendentals=0,
         ),
     )(*args)
 
@@ -122,6 +123,59 @@
     ]
 
 
+def total_kernel(kept_ref, got_ref, *out_refs):
+    at = 0
+    for out_ref in out_refs:
+        size = out_ref.shape[0]
+        kept = kept_ref[at : at + size, :].astype(jnp.float32)
+        out_ref[...] = (kept + got_ref[at : at + size, :].astype(jnp.float32)).astype(jnp.bfloat16)
+        at = at + size
+
+
+def total_blocks(kept, got, sizes):
+    width = kept.shape[1]
+    return pl.pallas_call(
+        total_kernel,
+        out_shape=tuple(jax.ShapeDtypeStruct((size, width), jnp.bfloat16) for size in sizes),
+        in_specs=[WHOLE, WHOLE],
+        out_specs=tuple([WHOLE] * len(sizes)),
+        compiler_params=pltpu.CompilerParams(vmem_limit_bytes=12 * 1024 * 1024),
+        cost_estimate=pl.CostEstimate(
+            flops=kept.size, bytes_accessed=1 << 20, transcendentals=0
+        ),
+    )(kept, got)
+
+
+def payload_kernel(out_ref, own, below, above, across, straight, pair_ref, moved_ref, sent_ref):
+    rows, width = out_ref.shape
+    for start in range(0, width, TILE):
+        cols = slice(start, start + TILE)
+        sent_ref[:, cols] = out_ref[:, cols]
+        total = own[:, cols].astype(jnp.float32)
+        for ref in (below, above, across, straight):
+            total = total + ref[:rows, cols].astype(jnp.float32)
+        sent_ref[:, width + start : width + start + TILE] = total.astype(jnp.bfloat16)
+    value = pair_ref[...] + moved_ref[...]
+    lane = lax.broadcasted_iota(jnp.int32, (rows, 128), 1)
+    extra = jnp.zeros((rows, 128), jnp.float32)
+    for i in range(3):
+        piece = value.astype(jnp.bfloat16).astype(jnp.float32)
+        extra = jnp.where(lane == i, piece, extra)
+        value = value - piece
+    sent_ref[:, 2 * width :] = extra.astype(jnp.bfloat16)
+
+
+def return_payload(out_block, back_parts, pair_half, moved):
+    rows, width = out_block.shape
+    return pl.pallas_call(
+        payload_kernel,
+        out_shape=jax.ShapeDtypeStruct((rows, 2 * width + 128), jnp.bfloat16),
+        in_specs=[WHOLE] * 8,
+        out_specs=WHOLE,
+        compiler_params=pltpu.CompilerParams(vmem_limit_bytes=8 * 1024 * 1024),
+    )(out_block, *back_parts, pair_half, moved)
+
+
 def slot_positions(ids_ref, tok_count, top_count, capacity):
     names = [ids_ref[n, k] for n in range(tok_count) for k in range(top_count)]
     positions = []
@@ -139,7 +193,7 @@
     core_out[0] = core_ref[0]
     tok_count, width = tokens_ref.shape
     top_count = ids_ref.shape[1]
-    rows = sent_ref.shape[0]
+    rows = sent_ref.shape[0] * sent_ref.shape[1]
     positions = slot_positions(ids_ref, tok_count, top_count, capacity)
     place = lax.broadcasted_iota(jnp.int32, (rows, 1), 0)
     chosen, weighted = [], []
@@ -158,7 +212,8 @@
             total = masks[0] * values[0:1]
             for n in range(1, tok_count):
                 total = total + masks[n] * values[n : n + 1]
-            sent_ref[:, base + start : base + start + 512] = total.astype(jnp.bfloat16)
+            shaped = total.astype(jnp.bfloat16).reshape(rows // capacity, capacity, 512)
+            sent_ref[:, :, base + start : base + start + 512] = shaped
 
 
 def dispatch_rows(core, tokens, expert_ids, combine_weights, cotangent, experts, capacity):
@@ -166,7 +221,7 @@
     return pl.pallas_call(
         functools.partial(dispatch_kernel, capacity),
         out_shape=(
-            jax.ShapeDtypeStruct((experts * capacity, 2 * tokens.shape[1]), jnp.bfloat16),
+            jax.ShapeDtypeStruct((experts, capacity, 2 * tokens.shape[1]), jnp.bfloat16),
             jax.ShapeDtypeStruct((1,), jnp.int32),
         ),
         in_specs=[scalars, scalars, scalars, WHOLE, WHOLE],
@@ -198,12 +253,12 @@
     rest = weighted - high.astype(jnp.float32)
     middle = rest.astype(jnp.bfloat16)
     low = (rest - middle.astype(jnp.float32)).astype(jnp.bfloat16)
+    terms = jnp.concatenate([high, middle, low], 0)
     plain = chosen.astype(jnp.bfloat16)
     for start in range(0, width, 512):
         values = returned_ref[:, start : start + 512]
-        total = jnp.dot(high, values, preferred_element_type=jnp.float32)
-        total = total + jnp.dot(middle, values, preferred_element_type=jnp.float32)
-        total = total + jnp.dot(low, values, preferred_element_type=jnp.float32)
+        total = jnp.dot(terms, values, preferred_element_type=jnp.float32)
+        total = total[0:8] + total[8:16] + total[16:24]
         out_ref[:, start : start + 512] = total[:tok_count].astype(jnp.bfloat16)
         values = returned_ref[:, width + start : width + start + 512]
         total = jnp.dot(plain, values, preferred_element_type=jnp.float32)
@@ -241,9 +296,9 @@
         return lax.ppermute(value, AXES, shift_pairs(sizes, **shift))
 
     def exchange(rows):
-        sent = rows.reshape(experts, capacity, rows.shape[1])
+        sent = rows.reshape(experts, capacity, rows.shape[-1])
         got = lax.all_to_all(sent, "exp", split_axis=0, concat_axis=0, tiled=True)
-        return got.reshape(rows.shape)
+        return got.reshape(member_rows, rows.shape[-1])
 
     def add(*terms):
         return sum(t.astype(jnp.float32) for t in terms).astype(jnp.bfloat16)
@@ -265,18 +320,28 @@
             results[i] = (mine, move(mine, core=1))
         return results, gate, down
 
-    def scatter(kept, given):
-        total = add(kept, move(given, core=1))
-        own, across, below, above, far, across_far = jnp.split(
-            total, [member_rows * i for i in (1, 2, 4, 6, 7)], 0
-        )
-        got_below = move(below, row=-1)
-        got_above = move(above, row=1)
-        far = add(far, move(across_far, hi=1))
-        across = add(across, got_below[member_rows:], got_above[member_rows:])
-        got_across = move(across, hi=1)
-        got_far = move(far, row=2)
-        return add(own, got_below[:member_rows], got_above[:member_rows], got_across, got_far)
+    def scatter_all(*halves):
+        r = member_rows
+        sizes_of = [r * i for i in (1, 1, 2, 2, 1, 1)]
+        (kept, given), (back_kept, back_given) = halves
+        first = total_blocks(kept, move(given, core=1), sizes_of)
+        first_near = (move(first[2], row=-1), move(first[3], row=1))
+        first_got = move(first[5], hi=1)
+        back_other = move(back_given, core=1)
+        second = total_blocks(back_kept, back_other, sizes_of)
+        second_near = (move(second[2], row=-1), move(second[3], row=1))
+        second_got = move(second[5], hi=1)
+        first_far = move(add(first[4], first_got), row=2)
+        second_got, _ = lax.optimization_barrier((second_got, second_near))
+        second_far = move(add(second[4], second_got), row=2)
+        results = []
+        for total, near, straight in (
+            (first, first_near, first_far),
+            (second, second_near, second_far),
+        ):
+            across = move(add(total[1], near[0][r:], near[1][r:]), hi=1)
+            results.append((total[0], *near, across, straight))
+        return results
 
     sent, core = dispatch_rows(
         lax.axis_index("tp"), tokens, expert_ids, combine_weights, cotangent, experts, capacity
@@ -288,21 +353,25 @@
     (routed_rows, routed_grad), gate, down = gather(
         (arrived[:, :half_width], grad_block), (gate, down)
     )
-    pre, out_kept, out_given = expert_call(forward_kernel, core, *routed_rows, gate, down)
-    back_kept, back_given = expert_call(backward_kernel, core, *routed_grad, down, gate, pre)
-    out_block = scatter(out_kept, out_given)
+    token_rows, token_other = routed_rows
+    grad_rows, grad_other = routed_grad
+    token_partial, grad_partial = expert_call(
+        first_kernel, ["units", "units"], (core, token_rows, grad_rows, gate, down), 2
+    )
+    pre, out_kept, out_given = expert_call(
+        forward_kernel, ["units", "half", "half"], (core, token_partial, token_other, gate, down), 3
+    )
+    back_kept, back_given = expert_call(
+        backward_kernel, ["half", "half"], (core, grad_partial, grad_other, down, gate, pre), 3
+    )
+    out_parts, back_parts = scatter_all((out_kept, out_given), (back_kept, back_given))
+    out_block = add(*[part[:member_rows] for part in out_parts])
     pair_half = jnp.sum(
         out_block.astype(jnp.float32) * grad_block.astype(jnp.float32), 1, keepdims=True
     )
-    pair_value = pair_half + move(pair_half, core=1)
-    pieces = []
-    for _ in range(3):
-        piece = pair_value.astype(jnp.bfloat16)
-        pieces.append(piece)
-        pair_value = pair_value - piece.astype(jnp.float32)
-    back_block = scatter(back_kept, back_given)
-    extra = jnp.concatenate(pieces + [jnp.zeros((member_rows, 125), jnp.bfloat16)], 1)
-    returned = exchange(jnp.concatenate([out_block, back_block, extra], 1))
+    returned = exchange(
+        return_payload(out_block, back_parts, pair_half, move(pair_half, core=1))
+    )
 
     return combine_rows(expert_ids, combine_weights, returned, half_width, capacity)
 

time: 128 us -> 125 us (0.977)
  the two profiles are of different devices: /device:TPU:4 before, /device:TPU:8 now
where the time goes in v3:
time: 125 us
  blocking collectives  40.4 us (32%)
  starting transfers between devices  33.9 us (27%)
  waiting for transfers between devices  28.6 us (23%)
  Pallas kernels  19.3 us (15%)
    all_to_all x2, blocking collectives, exchange(): got = lax.all_to_all(sent, 'exp', split_axis=0, concat_axis=0, tiled=True)  40.4 us
    ppermute x22, starting transfers between devices, move(): return lax.ppermute(value, AXES, shift_pairs(sizes, **shift))  33.9 us
    ppermute x22, waiting for transfers between devices, move(): return lax.ppermute(value, AXES, shift_pairs(sizes, **shift))  28.6 us
    pallas_call x3, Pallas kernels, expert_call(): pl.pallas_call(kernel, out_shape=tuple((shapes[name] for name in outs)),...  9.4 us
    pallas_call x2, Pallas kernels, load_weights(): pl.pallas_call(load_kernel, out_shape=jax.ShapeDtypeStruct(weight.shape,...  5.53 us
  transfers between devices with their start and end apart: 22, of which 10 were waited for; matrix products, arithmetic and copies ran while one was open for 1% of the time, Pallas kernels for 13%

profile of v3, /device:TPU:8, one launch (start us, length us, event | category | flops | bytes accessed | tf_op | source)
XLA Modules:
  0.0 124.6 jit_solution(10304157318099159438)
XLA Ops:
  0.6 2.0 %shard_map.85 = (bf16[16,2,6144]{2,1,0:T(2,128)(2,1)}, s32[1]{0:T(128)}) custom-call(s32[1]{0:T(128)} %bitcast.core_ref, s32[4,4]{1,0:T(4,128)} %ids_ref.3, f32[4,4]{1,0:T(4,128)} %weights_ref.3, bf16[4,3072]{1,0:T(4,128)(2,1)} %tokens_ref.1, bf16[4,3072]{1,0:T(4,128)(2,1)} %cotangent_ref.1), custom_call_target="tpu_custom_call" | custom-call | tf_op jit(solution)/shard_map/pallas_call | solution.py:221
  2.6 22.1 %all_to_all.10 = bf16[16,2,6144]{2,1,0:T(2,128)(2,1)S(1)} all-to-all(bf16[16,2,6144]{2,1,0:T(2,128)(2,1)} %get-tuple-element.33), channel_id=1, replica_groups=mesh['ctx'=8,'exp'=16,'tp'=2] {'exp'}, dimensions={0} | all-to-all | bytes 786432 | tf_op jit(solution)/shard_map/all_to_all | solution.py:300
  25.0 2.8 %collective-permute-start = (bf16[64,3072]{1,0:T(8,128)(2,1)S(1)}, bf16[64,3072]{1,0:T(8,128)(2,1)S(1)}, u32[]{:S(2)}, u32[]{:S(2)}) collective-permute-start(bf16[64,3072]{1,0:T(8,128)(2,1)S(1)} %pad_maximum_fusion.1), channel_id=1, source_target_pairs={{0,128},{1,129},{2,130},{3,131},{4,132},{5,133},{6,134},{7,135},{8... | collective-permute-start | bytes 1179656 | tf_op jit(solution)/shard_map/ppermute | solution.py:296
  27.8 2.3 %collective-permute-start.1 = (bf16[64,3072]{1,0:T(8,128)(2,1)S(1)}, bf16[64,3072]{1,0:T(8,128)(2,1)S(1)}, u32[]{:S(2)}, u32[]{:S(2)}) collective-permute-start(bf16[64,3072]{1,0:T(8,128)(2,1)S(1)} %pad_maximum_fusion.1), channel_id=1, source_target_pairs={{0,64},{1,65},{2,66},{3,67},{4,68},{5,69},{6,70},{7,71},{8,72},{9,... | collective-permute-start | bytes 1179656 | tf_op jit(solution)/shard_map/ppermute | solution.py:296
  30.1 2.8 %shard_map.86.gate_ref = bf16[504,6144]{1,0:T(8,128)(2,1)S(1)} custom-call(bf16[504,6144]{1,0:T(8,128)(2,1)} %bitcast.6), custom_call_target="tpu_custom_call" | custom-call | tf_op jit(solution)/shard_map/pallas_call | solution.py:114
  32.9 2.8 %shard_map.87.down_ref = bf16[504,6144]{1,0:T(8,128)(2,1)S(1)} custom-call(bf16[504,6144]{1,0:T(8,128)(2,1)} %bitcast.7), custom_call_target="tpu_custom_call" | custom-call | tf_op jit(solution)/shard_map/pallas_call | solution.py:114
  35.7 2.3 %collective-permute-done.1 = bf16[64,3072]{1,0:T(8,128)(2,1)S(1)} collective-permute-done((bf16[64,3072]{1,0:T(8,128)(2,1)S(1)}, bf16[64,3072]{1,0:T(8,128)(2,1)S(1)}, u32[]{:S(2)}, u32[]{:S(2)}) %collective-permute-start.1) | collective-permute-done | bytes 393248 | tf_op jit(solution)/shard_map/ppermute | solution.py:296
  38.1 2.2 %collective-permute-start.5 = (bf16[64,3072]{1,0:T(8,128)(2,1)S(1)}, bf16[64,3072]{1,0:T(8,128)(2,1)S(1)}, u32[]{:S(2)}, u32[]{:S(2)}) collective-permute-start(bf16[64,3072]{1,0:T(8,128)(2,1)S(1)} %pad_maximum_fusion.2), channel_id=1, source_target_pairs={{0,32},{1,33},{2,34},{3,35},{4,36},{5,37},{6,38},{7,39},{8,40},{9,... | collective-permute-start | bytes 1179656 | tf_op jit(solution)/shard_map/ppermute | solution.py:296
  40.3 2.1 %collective-permute-start.2 = (bf16[64,3072]{1,0:T(8,128)(2,1)S(1)}, bf16[64,3072]{1,0:T(8,128)(2,1)S(1)}, u32[]{:S(2)}, u32[]{:S(2)}) collective-permute-start(bf16[64,3072]{1,0:T(8,128)(2,1)S(1)} %pad_maximum_fusion), channel_id=1, source_target_pairs={{0,32},{1,33},{2,34},{3,35},{4,36},{5,37},{6,38},{7,39},{8,40},{9,... | collective-permute-start | bytes 1179656 | tf_op jit(solution)/shard_map/ppermute | solution.py:296
  42.4 0.8 collective-permute-start.4
  43.2 7.0 %collective-permute-done.5 = bf16[64,3072]{1,0:T(8,128)(2,1)S(1)} collective-permute-done((bf16[64,3072]{1,0:T(8,128)(2,1)S(1)}, bf16[64,3072]{1,0:T(8,128)(2,1)S(1)}, u32[]{:S(2)}, u32[]{:S(2)}) %collective-permute-start.5) | collective-permute-done | bytes 393248 | tf_op jit(solution)/shard_map/ppermute | solution.py:296
  50.3 1.2 collective-permute-done.6
  51.5 3.5 %collective-permute-done.2 = bf16[64,3072]{1,0:T(8,128)(2,1)S(1)} collective-permute-done((bf16[64,3072]{1,0:T(8,128)(2,1)S(1)}, bf16[64,3072]{1,0:T(8,128)(2,1)S(1)}, u32[]{:S(2)}, u32[]{:S(2)}) %collective-permute-start.2) | collective-permute-done | bytes 393248 | tf_op jit(solution)/shard_map/ppermute | solution.py:296
  55.0 0.7 collective-permute-done.3
  56.4 2.5 %shard_map.88 = (f32[256,504]{1,0:T(8,128)S(1)}, f32[256,504]{1,0:T(8,128)S(1)}) custom-call(s32[1]{0:T(128)} %get-tuple-element.32.core_ref, bf16[256,3072]{1,0:T(8,128)(2,1)S(1)} %get-tuple-element.64.rows_ref, bf16[256,3072]{1,0:T(8,128)(2,1)S(1)} %get-tuple-element.63.grads_ref, bf16[504,6144]{1,0:T(8,128)(2,1)S(1)} %shard_map.86.gate_ref, ...), custom_call_target="tpu_custom_call" | custom-call | flops 1585446912 | bytes 3096576 | tf_op jit(solution)/shard_map/pallas_call | solution.py:92
  59.3 3.5 %shard_map.89 = (f32[256,504]{1,0:T(8,128)S(1)}, bf16[256,3072]{1,0:T(8,128)(2,1)S(1)}, bf16[256,3072]{1,0:T(8,128)(2,1)S(1)}) custom-call(s32[1]{0:T(128)} %get-tuple-element.32.core_ref, f32[256,504]{1,0:T(8,128)S(1)} %get-tuple-element.41.partial_ref, bf16[256,3072]{1,0:T(8,128)(2,1)S(1)} %collective-permute-done.7.other_ref, ...), custom_call_target="tpu_custom_call" | custom-call | flops 2378170368 | bytes 4644864 | tf_op jit(solution)/shard_map/pallas_call | solution.py:92
  63.2 3.5 %shard_map.91 = (bf16[256,3072]{1,0:T(8,128)(2,1)S(1)}, bf16[256,3072]{1,0:T(8,128)(2,1)S(1)}) custom-call(s32[1]{0:T(128)} %get-tuple-element.32.core_ref, f32[256,504]{1,0:T(8,128)S(1)} %get-tuple-element.50.partial_ref, bf16[256,3072]{1,0:T(8,128)(2,1)S(1)} %collective-permute-done.14.other_ref, bf16[504,6144]{1,0:T(8,128)(2,1)S(1)} %shard_map.87.down_ref, ...), custom_call_target="tpu_custom_call" | custom-call | flops 2378170368 | bytes 4644864 | tf_op jit(solution)/shard_map/pallas_call | solution.py:92
  67.5 0.9 collective-permute-start.12
  68.4 1.3 %collective-permute-start.10 = (bf16[64,3072]{1,0:T(8,128)(2,1)S(1)}, bf16[64,3072]{1,0:T(8,128)(2,1)S(1)}, u32[]{:S(2)}, u32[]{:S(2)}) collective-permute-start(bf16[64,3072]{1,0:T(8,128)(2,1)S(1)} %get-tuple-element.46), channel_id=1, source_target_pairs={{0,32},{1,33},{2,34},{3,35},{4,36},{5,37},{6,38},{7,39},{8,40},{9,... | collective-permute-start | bytes 1179656 | tf_op jit(solution)/shard_map/ppermute | solution.py:296
  69.7 0.7 collective-permute-start.9
  70.8 1.7 %collective-permute-start.16 = (bf16[64,3072]{1,0:T(8,128)(2,1)S(1)}, bf16[64,3072]{1,0:T(8,128)(2,1)S(1)}, u32[]{:S(2)}, u32[]{:S(2)}) collective-permute-start(bf16[64,3072]{1,0:T(8,128)(2,1)S(1)} %get-tuple-element.55), channel_id=1, source_target_pairs={{0,96},{1,97},{2,98},{3,99},{4,100},{5,101},{6,102},{7,103},{8,104... | collective-permute-start | bytes 1179656 | tf_op jit(solution)/shard_map/ppermute | solution.py:296
  72.9 3.1 %collective-permute-done.12 = bf16[32,3072]{1,0:T(8,128)(2,1)S(1)} collective-permute-done((bf16[32,3072]{1,0:T(8,128)(2,1)S(1)}, bf16[32,3072]{1,0:T(8,128)(2,1)S(1)}, u32[]{:S(2)}, u32[]{:S(2)}) %collective-permute-start.12) | collective-permute-done | bytes 196640 | tf_op jit(solution)/shard_map/ppermute | solution.py:296
  76.0 0.8 collective-permute-start.19
  76.9 3.5 %collective-permute-done.10 = bf16[64,3072]{1,0:T(8,128)(2,1)S(1)} collective-permute-done((bf16[64,3072]{1,0:T(8,128)(2,1)S(1)}, bf16[64,3072]{1,0:T(8,128)(2,1)S(1)}, u32[]{:S(2)}, u32[]{:S(2)}) %collective-permute-start.10) | collective-permute-done | bytes 393248 | tf_op jit(solution)/shard_map/ppermute | solution.py:296
  80.4 2.3 %collective-permute-start.13 = (bf16[32,3072]{1,0:T(8,128)(2,1)S(1)}, bf16[32,3072]{1,0:T(8,128)(2,1)S(1)}, u32[]{:S(2)}, u32[]{:S(2)}) collective-permute-start(bf16[32,3072]{1,0:T(8,128)(2,1)S(1)} %add_convert_fusion.3), channel_id=1, source_target_pairs={{0,64},{1,65},{2,66},{3,67},{4,68},{5,69},{6,70},{7,71},{8,72},{9,... | collective-permute-start | bytes 589832 | tf_op jit(solution)/shard_map/ppermute | solution.py:296
  82.8 2.8 %collective-permute-start.11 = (bf16[32,3072]{1,0:T(8,128)(2,1)S(1)}, bf16[32,3072]{1,0:T(8,128)(2,1)S(1)}, u32[]{:S(2)}, u32[]{:S(2)}) collective-permute-start(bf16[32,3072]{1,0:T(8,128)(2,1)S(1)} %add_convert_fusion.4), channel_id=1, source_target_pairs={{0,128},{1,129},{2,130},{3,131},{4,132},{5,133},{6,134},{7,135},{8... | collective-permute-start | bytes 589832 | tf_op jit(solution)/shard_map/ppermute | solution.py:296
  85.6 3.5 %collective-permute-done.16.below = bf16[64,3072]{1,0:T(8,128)(2,1)S(1)} collective-permute-done((bf16[64,3072]{1,0:T(8,128)(2,1)S(1)}, bf16[64,3072]{1,0:T(8,128)(2,1)S(1)}, u32[]{:S(2)}, u32[]{:S(2)}) %collective-permute-start.16) | collective-permute-done | bytes 393248 | tf_op jit(solution)/shard_map/ppermute | solution.py:296
  89.2 2.8 %collective-permute-start.18 = (bf16[32,3072]{1,0:T(8,128)(2,1)S(1)}, bf16[32,3072]{1,0:T(8,128)(2,1)S(1)}, u32[]{:S(2)}, u32[]{:S(2)}) collective-permute-start(bf16[32,3072]{1,0:T(8,128)(2,1)S(1)} %add_convert_fusion.1), channel_id=1, source_target_pairs={{0,128},{1,129},{2,130},{3,131},{4,132},{5,133},{6,134},{7,135},{8... | collective-permute-start | bytes 589832 | tf_op jit(solution)/shard_map/ppermute | solution.py:296
  92.1 8.5 %collective-permute-start.20 = (bf16[32,3072]{1,0:T(8,128)(2,1)S(1)}, bf16[32,3072]{1,0:T(8,128)(2,1)S(1)}, u32[]{:S(2)}, u32[]{:S(2)}) collective-permute-start(bf16[32,3072]{1,0:T(8,128)(2,1)S(1)} %add_convert_fusion), channel_id=1, source_target_pairs={{0,64},{1,65},{2,66},{3,67},{4,68},{5,69},{6,70},{7,71},{8,72},{9,... | collective-permute-start | bytes 589832 | tf_op jit(solution)/shard_map/ppermute | solution.py:296
  101.0 3.2 %collective-permute-done.20.straight = bf16[32,3072]{1,0:T(8,128)(2,1)S(1)} collective-permute-done((bf16[32,3072]{1,0:T(8,128)(2,1)S(1)}, bf16[32,3072]{1,0:T(8,128)(2,1)S(1)}, u32[]{:S(2)}, u32[]{:S(2)}) %collective-permute-start.20) | collective-permute-done | bytes 196640 | tf_op jit(solution)/shard_map/ppermute | solution.py:296
  104.5 18.3 %all_to_all.11 = bf16[16,2,6272]{2,1,0:T(2,128)(2,1)S(1)} all-to-all(bf16[16,2,6272]{2,1,0:T(2,128)(2,1)S(1)} %reshape.20), channel_id=1, replica_groups=mesh['ctx'=8,'exp'=16,'tp'=2] {'exp'}, dimensions={0} | all-to-all | bytes 802816 | tf_op jit(solution)/shard_map/all_to_all | solution.py:300
  123.0 1.6 %shard_map.94 = (bf16[4,3072]{1,0:T(4,128)(2,1)}, bf16[4,3072]{1,0:T(4,128)(2,1)}, f32[4,4]{1,0:T(4,128)}) custom-call(s32[4,4]{1,0:T(4,128)S(1)} %copy-done, f32[4,4]{1,0:T(4,128)S(1)} %copy-done.1, bf16[32,6272]{1,0:T(8,128)(2,1)S(1)} %reshape.21.returned_ref), custom_call_target="tpu_custom_call" | custom-call | tf_op jit(solution)/shard_map/pallas_call | solution.py:278
  (48 shorter events, 4.6 us)
Async XLA Ops:
  25.0 10.7 %collective-permute-start = (bf16[64,3072]{1,0:T(8,128)(2,1)S(1)}, bf16[64,3072]{1,0:T(8,128)(2,1)S(1)}, u32[]{:S(2)}, u32[]{:S(2)}) collective-permute-start(bf16[64,3072]{1,0:T(8,128)(2,1)S(1)} %pad_maximum_fusion.1), channel_id=1, source_target_pairs={{0,128},{1,129},{2,130},{3,131},{4,132},{5,133},{6,134},{7,135},{8... | collective-permute-start | bytes 1179656 | tf_op jit(solution)/shard_map/ppermute | solution.py:296
  27.8 10.2 %collective-permute-start.1 = (bf16[64,3072]{1,0:T(8,128)(2,1)S(1)}, bf16[64,3072]{1,0:T(8,128)(2,1)S(1)}, u32[]{:S(2)}, u32[]{:S(2)}) collective-permute-start(bf16[64,3072]{1,0:T(8,128)(2,1)S(1)} %pad_maximum_fusion.1), channel_id=1, source_target_pairs={{0,64},{1,65},{2,66},{3,67},{4,68},{5,69},{6,70},{7,71},{8,72},{9,... | collective-permute-start | bytes 1179656 | tf_op jit(solution)/shard_map/ppermute | solution.py:296
  38.1 12.1 %collective-permute-start.5 = (bf16[64,3072]{1,0:T(8,128)(2,1)S(1)}, bf16[64,3072]{1,0:T(8,128)(2,1)S(1)}, u32[]{:S(2)}, u32[]{:S(2)}) collective-permute-start(bf16[64,3072]{1,0:T(8,128)(2,1)S(1)} %pad_maximum_fusion.2), channel_id=1, source_target_pairs={{0,32},{1,33},{2,34},{3,35},{4,36},{5,37},{6,38},{7,39},{8,40},{9,... | collective-permute-start | bytes 1179656 | tf_op jit(solution)/shard_map/ppermute | solution.py:296
  40.3 11.2 %collective-permute-start.6 = (bf16[64,3072]{1,0:T(8,128)(2,1)S(1)}, bf16[64,3072]{1,0:T(8,128)(2,1)S(1)}, u32[]{:S(2)}, u32[]{:S(2)}) collective-permute-start(bf16[64,3072]{1,0:T(8,128)(2,1)S(1)} %pad_maximum_fusion.2), channel_id=1, source_target_pairs={{0,96},{1,97},{2,98},{3,99},{4,100},{5,101},{6,102},{7,103},{8,104... | collective-permute-start | bytes 1179656 | tf_op jit(solution)/shard_map/ppermute | solution.py:296
  40.3 14.7 %collective-permute-start.2 = (bf16[64,3072]{1,0:T(8,128)(2,1)S(1)}, bf16[64,3072]{1,0:T(8,128)(2,1)S(1)}, u32[]{:S(2)}, u32[]{:S(2)}) collective-permute-start(bf16[64,3072]{1,0:T(8,128)(2,1)S(1)} %pad_maximum_fusion), channel_id=1, source_target_pairs={{0,32},{1,33},{2,34},{3,35},{4,36},{5,37},{6,38},{7,39},{8,40},{9,... | collective-permute-start | bytes 1179656 | tf_op jit(solution)/shard_map/ppermute | solution.py:296
  42.4 13.3 %collective-permute-start.3 = (bf16[64,3072]{1,0:T(8,128)(2,1)S(1)}, bf16[64,3072]{1,0:T(8,128)(2,1)S(1)}, u32[]{:S(2)}, u32[]{:S(2)}) collective-permute-start(bf16[64,3072]{1,0:T(8,128)(2,1)S(1)} %pad_maximum_fusion), channel_id=1, source_target_pairs={{0,96},{1,97},{2,98},{3,99},{4,100},{5,101},{6,102},{7,103},{8,104... | collective-permute-start | bytes 1179656 | tf_op jit(solution)/shard_map/ppermute | solution.py:296
  42.4 13.4 %collective-permute-start.4 = (bf16[64,3072]{1,0:T(8,128)(2,1)S(1)}, bf16[64,3072]{1,0:T(8,128)(2,1)S(1)}, u32[]{:S(2)}, u32[]{:S(2)}) collective-permute-start(bf16[64,3072]{1,0:T(8,128)(2,1)S(1)} %collective-permute-done.1), channel_id=1, source_target_pairs={{0,128},{1,129},{2,130},{3,131},{4,132},{5,133},{6,134},{7,135},{8... | collective-permute-start | bytes 1179656 | tf_op jit(solution)/shard_map/ppermute | solution.py:296
  55.8 3.5 %collective-permute-start.7 = (bf16[256,3072]{1,0:T(8,128)(2,1)S(1)}, bf16[256,3072]{1,0:T(8,128)(2,1)S(1)}, u32[]{:S(2)}, u32[]{:S(2)}) collective-permute-start(bf16[256,3072]{1,0:T(8,128)(2,1)S(1)} %get-tuple-element.64.rows_ref), channel_id=1, source_target_pairs={{0,1},{1,0},{2,3},{3,2},{4,5},{5,4},{6,7},{7,6},{8,9},{9,8},{10,11... | collective-permute-start | bytes 4718600 | tf_op jit(solution)/shard_map/ppermute | solution.py:296
  55.9 7.3 %collective-permute-start.14 = (bf16[256,3072]{1,0:T(8,128)(2,1)S(1)}, bf16[256,3072]{1,0:T(8,128)(2,1)S(1)}, u32[]{:S(2)}, u32[]{:S(2)}) collective-permute-start(bf16[256,3072]{1,0:T(8,128)(2,1)S(1)} %get-tuple-element.63.grads_ref), channel_id=1, source_target_pairs={{0,1},{1,0},{2,3},{3,2},{4,5},{5,4},{6,7},{7,6},{8,9},{9,8},{10,11... | collective-permute-start | bytes 4718600 | tf_op jit(solution)/shard_map/ppermute | solution.py:296
  62.8 4.3 %collective-permute-start.8 = (bf16[256,3072]{1,0:T(8,128)(2,1)S(1)}, bf16[256,3072]{1,0:T(8,128)(2,1)S(1)}, u32[]{:S(2)}, u32[]{:S(2)}) collective-permute-start(bf16[256,3072]{1,0:T(8,128)(2,1)S(1)} %get-tuple-element.43), channel_id=1, source_target_pairs={{0,1},{1,0},{2,3},{3,2},{4,5},{5,4},{6,7},{7,6},{8,9},{9,8},{10,11... | collective-permute-start | bytes 4718600 | tf_op jit(solution)/shard_map/ppermute | solution.py:296
  66.7 3.8 %collective-permute-start.15 = (bf16[256,3072]{1,0:T(8,128)(2,1)S(1)}, bf16[256,3072]{1,0:T(8,128)(2,1)S(1)}, u32[]{:S(2)}, u32[]{:S(2)}) collective-permute-start(bf16[256,3072]{1,0:T(8,128)(2,1)S(1)} %get-tuple-element.53), channel_id=1, source_target_pairs={{0,1},{1,0},{2,3},{3,2},{4,5},{5,4},{6,7},{7,6},{8,9},{9,8},{10,11... | collective-permute-start | bytes 4718600 | tf_op jit(solution)/shard_map/ppermute | solution.py:296
  67.5 8.5 %collective-permute-start.12 = (bf16[32,3072]{1,0:T(8,128)(2,1)S(1)}, bf16[32,3072]{1,0:T(8,128)(2,1)S(1)}, u32[]{:S(2)}, u32[]{:S(2)}) collective-permute-start(bf16[32,3072]{1,0:T(8,128)(2,1)S(1)} %get-tuple-element.49), channel_id=1, source_target_pairs={{0,128},{1,129},{2,130},{3,131},{4,132},{5,133},{6,134},{7,135},{8... | collective-permute-start | bytes 589832 | tf_op jit(solution)/shard_map/ppermute | solution.py:296
  68.4 12.0 %collective-permute-start.10 = (bf16[64,3072]{1,0:T(8,128)(2,1)S(1)}, bf16[64,3072]{1,0:T(8,128)(2,1)S(1)}, u32[]{:S(2)}, u32[]{:S(2)}) collective-permute-start(bf16[64,3072]{1,0:T(8,128)(2,1)S(1)} %get-tuple-element.46), channel_id=1, source_target_pairs={{0,32},{1,33},{2,34},{3,35},{4,36},{5,37},{6,38},{7,39},{8,40},{9,... | collective-permute-start | bytes 1179656 | tf_op jit(solution)/shard_map/ppermute | solution.py:296
  69.7 13.0 %collective-permute-start.9 = (bf16[64,3072]{1,0:T(8,128)(2,1)S(1)}, bf16[64,3072]{1,0:T(8,128)(2,1)S(1)}, u32[]{:S(2)}, u32[]{:S(2)}) collective-permute-start(bf16[64,3072]{1,0:T(8,128)(2,1)S(1)} %get-tuple-element.45), channel_id=1, source_target_pairs={{0,96},{1,97},{2,98},{3,99},{4,100},{5,101},{6,102},{7,103},{8,104... | collective-permute-start | bytes 1179656 | tf_op jit(solution)/shard_map/ppermute | solution.py:296
  70.8 18.3 %collective-permute-start.16 = (bf16[64,3072]{1,0:T(8,128)(2,1)S(1)}, bf16[64,3072]{1,0:T(8,128)(2,1)S(1)}, u32[]{:S(2)}, u32[]{:S(2)}) collective-permute-start(bf16[64,3072]{1,0:T(8,128)(2,1)S(1)} %get-tuple-element.55), channel_id=1, source_target_pairs={{0,96},{1,97},{2,98},{3,99},{4,100},{5,101},{6,102},{7,103},{8,104... | collective-permute-start | bytes 1179656 | tf_op jit(solution)/shard_map/ppermute | solution.py:296
  72.5 16.6 %collective-permute-start.17 = (bf16[64,3072]{1,0:T(8,128)(2,1)S(1)}, bf16[64,3072]{1,0:T(8,128)(2,1)S(1)}, u32[]{:S(2)}, u32[]{:S(2)}) collective-permute-start(bf16[64,3072]{1,0:T(8,128)(2,1)S(1)} %get-tuple-element.56), channel_id=1, source_target_pairs={{0,32},{1,33},{2,34},{3,35},{4,36},{5,37},{6,38},{7,39},{8,40},{9,... | collective-permute-start | bytes 1179656 | tf_op jit(solution)/shard_map/ppermute | solution.py:296
  76.0 16.0 %collective-permute-start.19 = (bf16[32,3072]{1,0:T(8,128)(2,1)S(1)}, bf16[32,3072]{1,0:T(8,128)(2,1)S(1)}, u32[]{:S(2)}, u32[]{:S(2)}) collective-permute-start(bf16[32,3072]{1,0:T(8,128)(2,1)S(1)} %get-tuple-element.59), channel_id=1, source_target_pairs={{0,128},{1,129},{2,130},{3,131},{4,132},{5,133},{6,134},{7,135},{8... | collective-permute-start | bytes 589832 | tf_op jit(solution)/shard_map/ppermute | solution.py:296
  80.4 20.2 %collective-permute-start.13 = (bf16[32,3072]{1,0:T(8,128)(2,1)S(1)}, bf16[32,3072]{1,0:T(8,128)(2,1)S(1)}, u32[]{:S(2)}, u32[]{:S(2)}) collective-permute-start(bf16[32,3072]{1,0:T(8,128)(2,1)S(1)} %add_convert_fusion.3), channel_id=1, source_target_pairs={{0,64},{1,65},{2,66},{3,67},{4,68},{5,69},{6,70},{7,71},{8,72},{9,... | collective-permute-start | bytes 589832 | tf_op jit(solution)/shard_map/ppermute | solution.py:296
  82.8 17.8 %collective-permute-start.11 = (bf16[32,3072]{1,0:T(8,128)(2,1)S(1)}, bf16[32,3072]{1,0:T(8,128)(2,1)S(1)}, u32[]{:S(2)}, u32[]{:S(2)}) collective-permute-start(bf16[32,3072]{1,0:T(8,128)(2,1)S(1)} %add_convert_fusion.4), channel_id=1, source_target_pairs={{0,128},{1,129},{2,130},{3,131},{4,132},{5,133},{6,134},{7,135},{8... | collective-permute-start | bytes 589832 | tf_op jit(solution)/shard_map/ppermute | solution.py:296
  89.2 11.8 %collective-permute-start.18 = (bf16[32,3072]{1,0:T(8,128)(2,1)S(1)}, bf16[32,3072]{1,0:T(8,128)(2,1)S(1)}, u32[]{:S(2)}, u32[]{:S(2)}) collective-permute-start(bf16[32,3072]{1,0:T(8,128)(2,1)S(1)} %add_convert_fusion.1), channel_id=1, source_target_pairs={{0,128},{1,129},{2,130},{3,131},{4,132},{5,133},{6,134},{7,135},{8... | collective-permute-start | bytes 589832 | tf_op jit(solution)/shard_map/ppermute | solution.py:296
  92.1 12.1 %collective-permute-start.20 = (bf16[32,3072]{1,0:T(8,128)(2,1)S(1)}, bf16[32,3072]{1,0:T(8,128)(2,1)S(1)}, u32[]{:S(2)}, u32[]{:S(2)}) collective-permute-start(bf16[32,3072]{1,0:T(8,128)(2,1)S(1)} %add_convert_fusion), channel_id=1, source_target_pairs={{0,64},{1,65},{2,66},{3,67},{4,68},{5,69},{6,70},{7,71},{8,72},{9,... | collective-permute-start | bytes 589832 | tf_op jit(solution)/shard_map/ppermute | solution.py:296
  100.9 3.3 %collective-permute-start.21 = (f32[32,1]{1,0:T(8,128)S(1)}, f32[32,1]{1,0:T(8,128)S(1)}, u32[]{:S(2)}, u32[]{:S(2)}) collective-permute-start(f32[32,1]{1,0:T(8,128)S(1)} %copy.10.pair_ref), channel_id=1, source_target_pairs={{0,1},{1,0},{2,3},{3,2},{4,5},{5,4},{6,7},{7,6},{8,9},{9,8},{10,11... | collective-permute-start | bytes 392 | tf_op jit(solution)/shard_map/ppermute | solution.py:296
  104.4 18.7 %copy-start = (s32[4,4]{1,0:T(4,128)S(1)}, s32[4,4]{1,0:T(4,128)}, u32[]{:S(2)}) copy-start(s32[4,4]{1,0:T(4,128)} %ids_ref.3) | copy-start | bytes 196
  104.4 18.7 %copy-start.1 = (f32[4,4]{1,0:T(4,128)S(1)}, f32[4,4]{1,0:T(4,128)}, u32[]{:S(2)}) copy-start(f32[4,4]{1,0:T(4,128)} %weights_ref.3) | copy-start | bytes 196

commit v4 on v3

--- a/solution.py
+++ b/solution.py
@@ -31,96 +31,123 @@
 WHOLE = pl.BlockSpec(memory_space=pltpu.VMEM)
 
 
-def half_columns(core, width, start, size):
-    return pl.ds(pl.multiple_of(core * width + start, TILE), size)
-
-
-def wide_product(core, rows_ref, weight_ref):
+def wide_product(rows_ref, weight_ref, half):
     width = rows_ref.shape[1]
     return lax.dot_general(
         rows_ref[...],
-        weight_ref[:, half_columns(core, width, 0, width)],
+        weight_ref[:, half * width : (half + 1) * width],
         NT,
         preferred_element_type=jnp.float32,
     )
 
 
-def deep_product(core, left, weight_ref, kept_ref, given_ref):
+def deep_product(left, weight_ref, given_ref, kept_ref):
     width = kept_ref.shape[1]
-    for side, out_ref in ((1 - core, given_ref), (core, kept_ref)):
+    for half, out_ref in ((1, given_ref), (0, kept_ref)):
         for start in range(0, width, TILE):
+            at = half * width + start
             out_ref[:, start : start + TILE] = jnp.dot(
-                left,
-                weight_ref[:, half_columns(side, width, start, TILE)],
-                preferred_element_type=jnp.float32,
+                left, weight_ref[:, at : at + TILE], preferred_element_type=jnp.float32
             ).astype(jnp.bfloat16)
 
 
-def first_kernel(core_ref, rows_ref, grads_ref, gate_ref, down_ref, pre_ref, grad_ref):
-    pre_ref[...] = wide_product(core_ref[0], rows_ref, gate_ref)
-    grad_ref[...] = wide_product(core_ref[0], grads_ref, down_ref)
-
-
-def forward_kernel(
-    core_ref, partial_ref, other_ref, gate_ref, down_ref, pre_ref, kept_ref, given_ref
-):
-    core = core_ref[0]
-    pre = partial_ref[...] + wide_product(1 - core, other_ref, gate_ref)
+def first_kernel(rows_ref, weight_ref, partial_ref):
+    partial_ref[...] = wide_product(rows_ref, weight_ref, 0)
+
+
+def forward_kernel(partial_ref, other_ref, gate_ref, down_ref, pre_ref, given_ref, kept_ref):
+    pre = partial_ref[...] + wide_product(other_ref, gate_ref, 1)
     pre_ref[...] = pre
     hidden = (pre / (1.0 + jnp.exp(-pre))).astype(jnp.bfloat16)
-    deep_product(core, hidden, down_ref, kept_ref, given_ref)
+    deep_product(hidden, down_ref, given_ref, kept_ref)
 
 
 def backward_kernel(
-    core_ref, partial_ref, other_ref, down_ref, gate_ref, pre_ref, kept_ref, given_ref
+    mine_ref, other_ref, down_ref, gate_ref, pre_ref, given_ref, kept_ref
 ):
-    core = core_ref[0]
-    grad = partial_ref[...] + wide_product(1 - core, other_ref, down_ref)
+    grad = wide_product(mine_ref, down_ref, 0) + wide_product(other_ref, down_ref, 1)
     pre = pre_ref[...]
     sigma = 1.0 / (1.0 + jnp.exp(-pre))
     pre_grad = (grad * (sigma * (1.0 + pre * (1.0 - sigma)))).astype(jnp.bfloat16)
-    deep_product(core, pre_grad, gate_ref, kept_ref, given_ref)
-
-
-def expert_call(kernel, outs, args, products):
-    rows, width = args[2].shape
-    units = args[3].shape[0]
+    deep_product(pre_grad, gate_ref, given_ref, kept_ref)
+
+
+def expert_call(kernel, outs, rows, units, args, products):
+    count, width = rows.shape
     shapes = {
-        "units": jax.ShapeDtypeStruct((rows, units), jnp.float32),
-        "half": jax.ShapeDtypeStruct((rows, width), jnp.bfloat16),
+        "units": jax.ShapeDtypeStruct((count, units), jnp.float32),
+        "half": jax.ShapeDtypeStruct((count, width), jnp.bfloat16),
     }
     return pl.pallas_call(
         kernel,
         out_shape=tuple(shapes[name] for name in outs),
-        in_specs=[pl.BlockSpec(memory_space=pltpu.SMEM)] + [WHOLE] * (len(args) - 1),
+        in_specs=[WHOLE] * len(args),
         out_specs=tuple([WHOLE] * len(outs)),
         compiler_params=pltpu.CompilerParams(vmem_limit_bytes=24 * 1024 * 1024),
         cost_estimate=pl.CostEstimate(
-            flops=2 * products * rows * width * units,
+            flops=2 * products * count * width * units,
             bytes_accessed=products * units * width,
             transcendentals=0,
         ),
     )(*args)
 
 
-def load_kernel(source, target, sem):
-    copy = pltpu.make_async_copy(source, target, sem)
-    copy.start()
-    copy.wait()
-
-
-def load_weights(*weights):
+def load_kernel(core_ref, source, target, sems):
+    core = core_ref[0]
+    width = target.shape[1] // 2
+    copies = []
+    for half in range(2):
+        side = core if half == 0 else 1 - core
+        start = pl.multiple_of(side * width, width)
+        copies.append(
+            pltpu.make_async_copy(
+                source.at[:, pl.ds(start, width)],
+                target.at[:, pl.ds(half * width, width)],
+                sems.at[half],
+            )
+        )
+    for copy in copies:
+        copy.start()
+    for copy in copies:
+        copy.wait()
+
+
+def load_weights(core, *weights):
     return [
         pl.pallas_call(
             load_kernel,
             out_shape=jax.ShapeDtypeStruct(weight.shape, weight.dtype),
-            in_specs=[pl.BlockSpec(memory_space=pl.ANY)],
+            in_specs=[pl.BlockSpec(memory_space=pltpu.SMEM), pl.BlockSpec(memory_space=pl.ANY)],
             out_specs=WHOLE,
-            scratch_shapes=[pltpu.SemaphoreType.DMA],
+            scratch_shapes=[pltpu.SemaphoreType.DMA((2,))],
             compiler_params=pltpu.CompilerParams(vmem_limit_bytes=44 * 1024 * 1024),
-        )(weight)
+        )(core, weight)
         for weight in weights
     ]
+
+
+def join_kernel(layout, *refs):
+    sources, targets = refs[: len(refs) - len(layout)], refs[len(refs) - len(layout) :]
+    for target, pieces in zip(targets, layout):
+        at = 0
+        for source, start, size in pieces:
+            target[at : at + size, :] = sources[source][start : start + size, :]
+            at = at + size
+
+
+def join_rows(layout, *sources, after=()):
+    width = sources[0].shape[1]
+    return pl.pallas_call(
+        functools.partial(join_kernel, layout),
+        out_shape=tuple(
+            jax.ShapeDtypeStruct((sum(piece[2] for piece in pieces), width), jnp.bfloat16)
+            for pieces in layout
+        ),
+        in_specs=[WHOLE] * len(sources) + [pl.BlockSpec(memory_space=pl.ANY)] * len(after),
+        out_specs=tuple([WHOLE] * len(layout)),
+        compiler_params=pltpu.CompilerParams(vmem_limit_bytes=10 * 1024 * 1024),
+        cost_estimate=pl.CostEstimate(flops=0, bytes_accessed=1 << 20, transcendentals=0),
+    )(*sources, *after)
 
 
 def total_kernel(kept_ref, got_ref, *out_refs):
@@ -255,14 +282,13 @@
     low = (rest - middle.astype(jnp.float32)).astype(jnp.bfloat16)
     terms = jnp.concatenate([high, middle, low], 0)
     plain = chosen.astype(jnp.bfloat16)
-    for start in range(0, width, 512):
-        values = returned_ref[:, start : start + 512]
-        total = jnp.dot(terms, values, preferred_element_type=jnp.float32)
-        total = total[0:8] + total[8:16] + total[16:24]
-        out_ref[:, start : start + 512] = total[:tok_count].astype(jnp.bfloat16)
-        values = returned_ref[:, width + start : width + start + 512]
-        total = jnp.dot(plain, values, preferred_element_type=jnp.float32)
-        back_ref[:, start : start + 512] = total[:tok_count].astype(jnp.bfloat16)
+    total = jnp.dot(terms, returned_ref[:, :width], preferred_element_type=jnp.float32)
+    total = total[0:8] + total[8:16] + total[16:24]
+    out_ref[...] = total[:tok_count].astype(jnp.bfloat16)
+    total = jnp.dot(
+        plain, returned_ref[:, width : 2 * width], preferred_element_type=jnp.float32
+    )
+    back_ref[...] = total[:tok_count].astype(jnp.bfloat16)
     extra = returned_ref[:, 2 * width : 2 * width + 128].astype(jnp.float32)
     row_values = jnp.sum(extra, 1, keepdims=True)
     match = lax.broadcasted_iota(jnp.int32, (rows, 128), 0) == pair_place
@@ -347,22 +373,41 @@
         lax.axis_index("tp"), tokens, expert_ids, combine_weights, cotangent, experts, capacity
     )
     arrived = exchange(sent)
-    arrived, gate, down = lax.optimization_barrier((arrived, gate, down))
-    gate, down = load_weights(gate, down)
+    r = member_rows
     grad_block = arrived[:, half_width:]
-    (routed_rows, routed_grad), gate, down = gather(
-        (arrived[:, :half_width], grad_block), (gate, down)
-    )
-    token_rows, token_other = routed_rows
-    grad_rows, grad_other = routed_grad
-    token_partial, grad_partial = expert_call(
-        first_kernel, ["units", "units"], (core, token_rows, grad_rows, gate, down), 2
-    )
-    pre, out_kept, out_given = expert_call(
-        forward_kernel, ["units", "half", "half"], (core, token_partial, token_other, gate, down), 3
-    )
-    back_kept, back_given = expert_call(
-        backward_kernel, ["half", "half"], (core, grad_partial, grad_other, down, gate, pre), 3
+    stacked = jnp.concatenate([arrived[:, :half_width], grad_block], 0)
+    stacked, gate, down = lax.optimization_barrier((stacked, gate, down))
+    across, far = move(stacked, hi=1), move(stacked, row=2)
+    across, far, gate, down = lax.optimization_barrier((across, far, *load_weights(core, gate, down)))
+    pairs = join_rows([[(0, i, r), (1, i, r)] for i in (0, r)], stacked, across)
+    token_pair, grad_pair = pairs
+    below, above = zip(*[(move(pair, row=1), move(pair, row=-1)) for pair in pairs])
+    across_far = move(far, hi=1)
+
+    def join_mine(i, after=()):
+        layout = [(0, 0, 2 * r), (1, 0, 2 * r), (2, 0, 2 * r), (3, i * r, r), (4, i * r, r)]
+        return join_rows(
+            [layout], pairs[i], below[i], above[i], far, across_far, after=after
+        )[0]
+
+    token_rows = join_mine(0)
+    token_other = move(token_rows, core=1)
+    units = down.shape[0]
+    (token_partial,) = expert_call(
+        first_kernel, ["units"], token_rows, units, (token_rows, gate), 1
+    )
+    grad_rows = join_mine(1, (token_partial,))
+    grad_other = move(grad_rows, core=1)
+    pre, out_given, out_kept = expert_call(
+        forward_kernel,
+        ["units", "half", "half"],
+        token_rows,
+        units,
+        (token_partial, token_other, gate, down),
+        3,
+    )
+    back_given, back_kept = expert_call(
+        backward_kernel, ["half", "half"], grad_rows, units, (grad_rows, grad_other, down, gate, pre), 4
     )
     out_parts, back_parts = scatter_all((out_kept, out_given), (back_kept, back_given))
     out_block = add(*[part[:member_rows] for part in out_parts])

time: 125 us -> 120 us (0.960)
  waiting for transfers between devices: 28.6 us -> 25.3 us
  starting transfers between devices: 33.9 us -> 32.5 us
    ppermute x22, waiting for transfers between devices: 28.6 us -> 25.3 us  [move(): return lax.ppermute(value, AXES, shift_pairs(sizes, **shift))]
    pallas_call x3, Pallas kernels: 9.4 us -> 7.4 us  [expert_call(): pl.pallas_call(kernel, out_shape=tuple((shapes[name] for name in outs)),...]
    pallas_call x2, Pallas kernels: 5.53 us -> 6.96 us  [load_weights(): pl.pallas_call(load_kernel, out_shape=jax.ShapeDtypeStruct(weight.shape,...]
    ppermute x22, starting transfers between devices: 33.9 us -> 32.5 us  [move(): return lax.ppermute(value, AXES, shift_pairs(sizes, **shift))]
where the time goes in v4:
time: 120 us; the launch traced here: 119 us
  blocking collectives  40.3 us (34%)
  starting transfers between devices  32.5 us (27%)
  waiting for transfers between devices  25.3 us (21%)
  Pallas kernels  19 us (16%)
    all_to_all x2, blocking collectives, exchange(): got = lax.all_to_all(sent, 'exp', split_axis=0, concat_axis=0, tiled=True)  40.3 us
    ppermute x22, starting transfers between devices, move(): return lax.ppermute(value, AXES, shift_pairs(sizes, **shift))  32.5 us
    ppermute x22, waiting for transfers between devices, move(): return lax.ppermute(value, AXES, shift_pairs(sizes, **shift))  25.3 us
    pallas_call x3, Pallas kernels, expert_call(): pl.pallas_call(kernel, out_shape=tuple((shapes[name] for name in outs)),...  7.4 us
    pallas_call x2, Pallas kernels, load_weights(): pl.pallas_call(load_kernel, out_shape=jax.ShapeDtypeStruct(weight.shape,...  6.96 us
  transfers between devices with their start and end apart: 22, of which 10 were waited for; matrix products, arithmetic and copies ran while one was open for 1% of the time, Pallas kernels for 13%

profile of v4, /device:TPU:8, one launch (start us, length us, event | category | flops | bytes accessed | tf_op | source)
XLA Modules:
  0.0 119.2 jit_solution(15369626833914352778)
XLA Ops:
  0.6 2.0 %shard_map.85 = (bf16[16,2,6144]{2,1,0:T(2,128)(2,1)}, s32[1]{0:T(128)}) custom-call(s32[1]{0:T(128)} %bitcast.core_ref, s32[4,4]{1,0:T(4,128)} %ids_ref.3, f32[4,4]{1,0:T(4,128)} %weights_ref.3, bf16[4,3072]{1,0:T(4,128)(2,1)} %tokens_ref.1, bf16[4,3072]{1,0:T(4,128)(2,1)} %cotangent_ref.1), custom_call_target="tpu_custom_call" | custom-call | tf_op jit(solution)/shard_map/pallas_call | solution.py:248
  2.6 22.1 %all_to_all.10 = bf16[16,2,6144]{2,1,0:T(2,128)(2,1)S(1)} all-to-all(bf16[16,2,6144]{2,1,0:T(2,128)(2,1)} %get-tuple-element.32), channel_id=1, replica_groups=mesh['ctx'=8,'exp'=16,'tp'=2] {'exp'}, dimensions={0} | all-to-all | bytes 786432 | tf_op jit(solution)/shard_map/all_to_all | solution.py:326
  24.9 2.8 %collective-permute-start = (bf16[64,3072]{1,0:T(8,128)(2,1)S(1)}, bf16[64,3072]{1,0:T(8,128)(2,1)S(1)}, u32[]{:S(2)}, u32[]{:S(2)}) collective-permute-start(bf16[64,3072]{1,0:T(8,128)(2,1)S(1)} %pad_maximum_fusion.refs_0_), channel_id=1, source_target_pairs={{0,128},{1,129},{2,130},{3,131},{4,132},{5,133},{6,134},{7,135},{8... | collective-permute-start | bytes 1179656 | tf_op jit(solution)/shard_map/ppermute | solution.py:322
  27.8 2.3 %collective-permute-start.1 = (bf16[64,3072]{1,0:T(8,128)(2,1)S(1)}, bf16[64,3072]{1,0:T(8,128)(2,1)S(1)}, u32[]{:S(2)}, u32[]{:S(2)}) collective-permute-start(bf16[64,3072]{1,0:T(8,128)(2,1)S(1)} %pad_maximum_fusion.refs_0_), channel_id=1, source_target_pairs={{0,64},{1,65},{2,66},{3,67},{4,68},{5,69},{6,70},{7,71},{8,72},{9,... | collective-permute-start | bytes 1179656 | tf_op jit(solution)/shard_map/ppermute | solution.py:322
  30.1 3.5 %shard_map.86.weight_ref.gate_ref = bf16[504,6144]{1,0:T(8,128)(2,1)S(1)} custom-call(s32[1]{0:T(128)} %get-tuple-element.34.core_ref, bf16[504,6144]{1,0:T(8,128)(2,1)} %bitcast.6), custom_call_target="tpu_custom_call" | custom-call | tf_op jit(solution)/shard_map/pallas_call | solution.py:117
  33.5 3.5 %shard_map.87.down_ref = bf16[504,6144]{1,0:T(8,128)(2,1)S(1)} custom-call(s32[1]{0:T(128)} %get-tuple-element.34.core_ref, bf16[504,6144]{1,0:T(8,128)(2,1)} %bitcast.7), custom_call_target="tpu_custom_call" | custom-call | tf_op jit(solution)/shard_map/pallas_call | solution.py:117
  37.0 0.9 collective-permute-done.1.refs_3_
  38.0 2.2 %collective-permute-start.2 = (bf16[64,3072]{1,0:T(8,128)(2,1)S(1)}, bf16[64,3072]{1,0:T(8,128)(2,1)S(1)}, u32[]{:S(2)}, u32[]{:S(2)}) collective-permute-start(bf16[64,3072]{1,0:T(8,128)(2,1)S(1)} %get-tuple-element.38.refs_0_), channel_id=1, source_target_pairs={{0,32},{1,33},{2,34},{3,35},{4,36},{5,37},{6,38},{7,39},{8,40},{9,... | collective-permute-start | bytes 1179656 | tf_op jit(solution)/shard_map/ppermute | solution.py:322
  40.2 0.8 collective-permute-start.4
  41.0 2.0 %collective-permute-start.12 = (bf16[64,3072]{1,0:T(8,128)(2,1)S(1)}, bf16[64,3072]{1,0:T(8,128)(2,1)S(1)}, u32[]{:S(2)}, u32[]{:S(2)}) collective-permute-start(bf16[64,3072]{1,0:T(8,128)(2,1)S(1)} %get-tuple-element.50.refs_0_), channel_id=1, source_target_pairs={{0,32},{1,33},{2,34},{3,35},{4,36},{5,37},{6,38},{7,39},{8,40},{9,... | collective-permute-start | bytes 1179656 | tf_op jit(solution)/shard_map/ppermute | solution.py:322
  43.1 7.1 %collective-permute-done.2.refs_1_ = bf16[64,3072]{1,0:T(8,128)(2,1)S(1)} collective-permute-done((bf16[64,3072]{1,0:T(8,128)(2,1)S(1)}, bf16[64,3072]{1,0:T(8,128)(2,1)S(1)}, u32[]{:S(2)}, u32[]{:S(2)}) %collective-permute-start.2) | collective-permute-done | bytes 393248 | tf_op jit(solution)/shard_map/ppermute | solution.py:322
  50.1 1.2 %collective-permute-done.3.refs_2_ = bf16[64,3072]{1,0:T(8,128)(2,1)S(1)} collective-permute-done((bf16[64,3072]{1,0:T(8,128)(2,1)S(1)}, bf16[64,3072]{1,0:T(8,128)(2,1)S(1)}, u32[]{:S(2)}, u32[]{:S(2)}) %collective-permute-start.3) | collective-permute-done | bytes 393248 | tf_op jit(solution)/shard_map/ppermute | solution.py:322
  51.6 1.0 shard_map.90.partial_ref.refs_5_
  52.6 2.3 %collective-permute-done.12.refs_1_ = bf16[64,3072]{1,0:T(8,128)(2,1)S(1)} collective-permute-done((bf16[64,3072]{1,0:T(8,128)(2,1)S(1)}, bf16[64,3072]{1,0:T(8,128)(2,1)S(1)}, u32[]{:S(2)}, u32[]{:S(2)}) %collective-permute-start.12) | collective-permute-done | bytes 393248 | tf_op jit(solution)/shard_map/ppermute | solution.py:322
  55.8 2.8 %shard_map.91 = (f32[256,504]{1,0:T(8,128)S(1)}, bf16[256,3072]{1,0:T(8,128)(2,1)S(1)}, bf16[256,3072]{1,0:T(8,128)(2,1)S(1)}) custom-call(f32[256,504]{1,0:T(8,128)S(1)} %shard_map.90.partial_ref.refs_5_, bf16[256,3072]{1,0:T(8,128)(2,1)S(1)} %collective-permute-done.5.other_ref, bf16[504,6144]{1,0:T(8,128)(2,1)S(1)} %shard_map.86.weight_ref.gate_ref, ...), custom_call_target="tpu_custom_call" | custom-call | flops 2378170368 | bytes 4644864 | tf_op jit(solution)/shard_map/pallas_call | solution.py:81
  58.6 0.8 collective-permute-start.6
  59.4 3.6 %shard_map.94 = (bf16[256,3072]{1,0:T(8,128)(2,1)S(1)}, bf16[256,3072]{1,0:T(8,128)(2,1)S(1)}) custom-call(bf16[256,3072]{1,0:T(8,128)(2,1)S(1)} %shard_map.93.mine_ref, bf16[256,3072]{1,0:T(8,128)(2,1)S(1)} %collective-permute-done.14.other_ref, bf16[504,6144]{1,0:T(8,128)(2,1)S(1)} %shard_map.87.down_ref, ...), custom_call_target="tpu_custom_call" | custom-call | flops 3170893824 | bytes 6193152 | tf_op jit(solution)/shard_map/pallas_call | solution.py:81
  63.5 0.9 collective-permute-start.10
  64.4 1.3 %collective-permute-start.8 = (bf16[64,3072]{1,0:T(8,128)(2,1)S(1)}, bf16[64,3072]{1,0:T(8,128)(2,1)S(1)}, u32[]{:S(2)}, u32[]{:S(2)}) collective-permute-start(bf16[64,3072]{1,0:T(8,128)(2,1)S(1)} %get-tuple-element.46), channel_id=1, source_target_pairs={{0,32},{1,33},{2,34},{3,35},{4,36},{5,37},{6,38},{7,39},{8,40},{9,... | collective-permute-start | bytes 1179656 | tf_op jit(solution)/shard_map/ppermute | solution.py:322
  65.7 0.7 collective-permute-start.7
  66.8 2.2 %collective-permute-start.16 = (bf16[64,3072]{1,0:T(8,128)(2,1)S(1)}, bf16[64,3072]{1,0:T(8,128)(2,1)S(1)}, u32[]{:S(2)}, u32[]{:S(2)}) collective-permute-start(bf16[64,3072]{1,0:T(8,128)(2,1)S(1)} %get-tuple-element.55), channel_id=1, source_target_pairs={{0,96},{1,97},{2,98},{3,99},{4,100},{5,101},{6,102},{7,103},{8,104... | collective-permute-start | bytes 1179656 | tf_op jit(solution)/shard_map/ppermute | solution.py:322
  69.0 3.3 %collective-permute-done.10 = bf16[32,3072]{1,0:T(8,128)(2,1)S(1)} collective-permute-done((bf16[32,3072]{1,0:T(8,128)(2,1)S(1)}, bf16[32,3072]{1,0:T(8,128)(2,1)S(1)}, u32[]{:S(2)}, u32[]{:S(2)}) %collective-permute-start.10) | collective-permute-done | bytes 196640 | tf_op jit(solution)/shard_map/ppermute | solution.py:322
  72.3 0.8 collective-permute-start.19
  73.2 3.1 %collective-permute-done.8 = bf16[64,3072]{1,0:T(8,128)(2,1)S(1)} collective-permute-done((bf16[64,3072]{1,0:T(8,128)(2,1)S(1)}, bf16[64,3072]{1,0:T(8,128)(2,1)S(1)}, u32[]{:S(2)}, u32[]{:S(2)}) %collective-permute-start.8) | collective-permute-done | bytes 393248 | tf_op jit(solution)/shard_map/ppermute | solution.py:322
  76.3 2.8 %collective-permute-start.11 = (bf16[32,3072]{1,0:T(8,128)(2,1)S(1)}, bf16[32,3072]{1,0:T(8,128)(2,1)S(1)}, u32[]{:S(2)}, u32[]{:S(2)}) collective-permute-start(bf16[32,3072]{1,0:T(8,128)(2,1)S(1)} %add_convert_fusion.3), channel_id=1, source_target_pairs={{0,64},{1,65},{2,66},{3,67},{4,68},{5,69},{6,70},{7,71},{8,72},{9,... | collective-permute-start | bytes 589832 | tf_op jit(solution)/shard_map/ppermute | solution.py:322
  79.2 2.8 %collective-permute-start.9 = (bf16[32,3072]{1,0:T(8,128)(2,1)S(1)}, bf16[32,3072]{1,0:T(8,128)(2,1)S(1)}, u32[]{:S(2)}, u32[]{:S(2)}) collective-permute-start(bf16[32,3072]{1,0:T(8,128)(2,1)S(1)} %add_convert_fusion.4), channel_id=1, source_target_pairs={{0,128},{1,129},{2,130},{3,131},{4,132},{5,133},{6,134},{7,135},{8... | collective-permute-start | bytes 589832 | tf_op jit(solution)/shard_map/ppermute | solution.py:322
  82.0 3.3 %collective-permute-done.16.below = bf16[64,3072]{1,0:T(8,128)(2,1)S(1)} collective-permute-done((bf16[64,3072]{1,0:T(8,128)(2,1)S(1)}, bf16[64,3072]{1,0:T(8,128)(2,1)S(1)}, u32[]{:S(2)}, u32[]{:S(2)}) %collective-permute-start.16) | collective-permute-done | bytes 393248 | tf_op jit(solution)/shard_map/ppermute | solution.py:322
  85.4 2.8 %collective-permute-start.18 = (bf16[32,3072]{1,0:T(8,128)(2,1)S(1)}, bf16[32,3072]{1,0:T(8,128)(2,1)S(1)}, u32[]{:S(2)}, u32[]{:S(2)}) collective-permute-start(bf16[32,3072]{1,0:T(8,128)(2,1)S(1)} %add_convert_fusion.1), channel_id=1, source_target_pairs={{0,128},{1,129},{2,130},{3,131},{4,132},{5,133},{6,134},{7,135},{8... | collective-permute-start | bytes 589832 | tf_op jit(solution)/shard_map/ppermute | solution.py:322
  88.3 7.0 %collective-permute-start.20 = (bf16[32,3072]{1,0:T(8,128)(2,1)S(1)}, bf16[32,3072]{1,0:T(8,128)(2,1)S(1)}, u32[]{:S(2)}, u32[]{:S(2)}) collective-permute-start(bf16[32,3072]{1,0:T(8,128)(2,1)S(1)} %add_convert_fusion), channel_id=1, source_target_pairs={{0,64},{1,65},{2,66},{3,67},{4,68},{5,69},{6,70},{7,71},{8,72},{9,... | collective-permute-start | bytes 589832 | tf_op jit(solution)/shard_map/ppermute | solution.py:322
  95.7 3.2 %collective-permute-done.20.straight = bf16[32,3072]{1,0:T(8,128)(2,1)S(1)} collective-permute-done((bf16[32,3072]{1,0:T(8,128)(2,1)S(1)}, bf16[32,3072]{1,0:T(8,128)(2,1)S(1)}, u32[]{:S(2)}, u32[]{:S(2)}) %collective-permute-start.20) | collective-permute-done | bytes 196640 | tf_op jit(solution)/shard_map/ppermute | solution.py:322
  99.2 18.2 %all_to_all.11 = bf16[16,2,6272]{2,1,0:T(2,128)(2,1)S(1)} all-to-all(bf16[16,2,6272]{2,1,0:T(2,128)(2,1)S(1)} %reshape.20), channel_id=1, replica_groups=mesh['ctx'=8,'exp'=16,'tp'=2] {'exp'}, dimensions={0} | all-to-all | bytes 802816 | tf_op jit(solution)/shard_map/all_to_all | solution.py:326
  117.6 1.6 %shard_map.97 = (bf16[4,3072]{1,0:T(4,128)(2,1)}, bf16[4,3072]{1,0:T(4,128)(2,1)}, f32[4,4]{1,0:T(4,128)}) custom-call(s32[4,4]{1,0:T(4,128)S(1)} %copy-done, f32[4,4]{1,0:T(4,128)S(1)} %copy-done.1, bf16[32,6272]{1,0:T(8,128)(2,1)S(1)} %reshape.21.returned_ref), custom_call_target="tpu_custom_call" | custom-call | tf_op jit(solution)/shard_map/pallas_call | solution.py:304
  (42 shorter events, 3.3 us)
Async XLA Ops:
  24.9 12.1 %collective-permute-start = (bf16[64,3072]{1,0:T(8,128)(2,1)S(1)}, bf16[64,3072]{1,0:T(8,128)(2,1)S(1)}, u32[]{:S(2)}, u32[]{:S(2)}) collective-permute-start(bf16[64,3072]{1,0:T(8,128)(2,1)S(1)} %pad_maximum_fusion.refs_0_), channel_id=1, source_target_pairs={{0,128},{1,129},{2,130},{3,131},{4,132},{5,133},{6,134},{7,135},{8... | collective-permute-start | bytes 1179656 | tf_op jit(solution)/shard_map/ppermute | solution.py:322
  27.8 10.2 %collective-permute-start.1 = (bf16[64,3072]{1,0:T(8,128)(2,1)S(1)}, bf16[64,3072]{1,0:T(8,128)(2,1)S(1)}, u32[]{:S(2)}, u32[]{:S(2)}) collective-permute-start(bf16[64,3072]{1,0:T(8,128)(2,1)S(1)} %pad_maximum_fusion.refs_0_), channel_id=1, source_target_pairs={{0,64},{1,65},{2,66},{3,67},{4,68},{5,69},{6,70},{7,71},{8,72},{9,... | collective-permute-start | bytes 1179656 | tf_op jit(solution)/shard_map/ppermute | solution.py:322
  38.0 12.1 %collective-permute-start.2 = (bf16[64,3072]{1,0:T(8,128)(2,1)S(1)}, bf16[64,3072]{1,0:T(8,128)(2,1)S(1)}, u32[]{:S(2)}, u32[]{:S(2)}) collective-permute-start(bf16[64,3072]{1,0:T(8,128)(2,1)S(1)} %get-tuple-element.38.refs_0_), channel_id=1, source_target_pairs={{0,32},{1,33},{2,34},{3,35},{4,36},{5,37},{6,38},{7,39},{8,40},{9,... | collective-permute-start | bytes 1179656 | tf_op jit(solution)/shard_map/ppermute | solution.py:322
  40.2 11.2 %collective-permute-start.3 = (bf16[64,3072]{1,0:T(8,128)(2,1)S(1)}, bf16[64,3072]{1,0:T(8,128)(2,1)S(1)}, u32[]{:S(2)}, u32[]{:S(2)}) collective-permute-start(bf16[64,3072]{1,0:T(8,128)(2,1)S(1)} %get-tuple-element.38.refs_0_), channel_id=1, source_target_pairs={{0,96},{1,97},{2,98},{3,99},{4,100},{5,101},{6,102},{7,103},{8,104... | collective-permute-start | bytes 1179656 | tf_op jit(solution)/shard_map/ppermute | solution.py:322
  40.2 11.2 %collective-permute-start.4 = (bf16[64,3072]{1,0:T(8,128)(2,1)S(1)}, bf16[64,3072]{1,0:T(8,128)(2,1)S(1)}, u32[]{:S(2)}, u32[]{:S(2)}) collective-permute-start(bf16[64,3072]{1,0:T(8,128)(2,1)S(1)} %collective-permute-done.1.refs_3_), channel_id=1, source_target_pairs={{0,128},{1,129},{2,130},{3,131},{4,132},{5,133},{6,134},{7,135},{8... | collective-permute-start | bytes 1179656 | tf_op jit(solution)/shard_map/ppermute | solution.py:322
  41.0 13.9 %collective-permute-start.12 = (bf16[64,3072]{1,0:T(8,128)(2,1)S(1)}, bf16[64,3072]{1,0:T(8,128)(2,1)S(1)}, u32[]{:S(2)}, u32[]{:S(2)}) collective-permute-start(bf16[64,3072]{1,0:T(8,128)(2,1)S(1)} %get-tuple-element.50.refs_0_), channel_id=1, source_target_pairs={{0,32},{1,33},{2,34},{3,35},{4,36},{5,37},{6,38},{7,39},{8,40},{9,... | collective-permute-start | bytes 1179656 | tf_op jit(solution)/shard_map/ppermute | solution.py:322
  43.1 12.5 %collective-permute-start.13 = (bf16[64,3072]{1,0:T(8,128)(2,1)S(1)}, bf16[64,3072]{1,0:T(8,128)(2,1)S(1)}, u32[]{:S(2)}, u32[]{:S(2)}) collective-permute-start(bf16[64,3072]{1,0:T(8,128)(2,1)S(1)} %get-tuple-element.50.refs_0_), channel_id=1, source_target_pairs={{0,96},{1,97},{2,98},{3,99},{4,100},{5,101},{6,102},{7,103},{8,104... | collective-permute-start | bytes 1179656 | tf_op jit(solution)/shard_map/ppermute | solution.py:322
  51.5 4.3 %collective-permute-start.5 = (bf16[256,3072]{1,0:T(8,128)(2,1)S(1)}, bf16[256,3072]{1,0:T(8,128)(2,1)S(1)}, u32[]{:S(2)}, u32[]{:S(2)}) collective-permute-start(bf16[256,3072]{1,0:T(8,128)(2,1)S(1)} %shard_map.89.rows_ref), channel_id=1, source_target_pairs={{0,1},{1,0},{2,3},{3,2},{4,5},{5,4},{6,7},{7,6},{8,9},{9,8},{10,11... | collective-permute-start | bytes 4718600 | tf_op jit(solution)/shard_map/ppermute | solution.py:322
  55.7 3.7 %collective-permute-start.14 = (bf16[256,3072]{1,0:T(8,128)(2,1)S(1)}, bf16[256,3072]{1,0:T(8,128)(2,1)S(1)}, u32[]{:S(2)}, u32[]{:S(2)}) collective-permute-start(bf16[256,3072]{1,0:T(8,128)(2,1)S(1)} %shard_map.93.mine_ref), channel_id=1, source_target_pairs={{0,1},{1,0},{2,3},{3,2},{4,5},{5,4},{6,7},{7,6},{8,9},{9,8},{10,11... | collective-permute-start | bytes 4718600 | tf_op jit(solution)/shard_map/ppermute | solution.py:322
  58.6 4.5 %collective-permute-start.6 = (bf16[256,3072]{1,0:T(8,128)(2,1)S(1)}, bf16[256,3072]{1,0:T(8,128)(2,1)S(1)}, u32[]{:S(2)}, u32[]{:S(2)}) collective-permute-start(bf16[256,3072]{1,0:T(8,128)(2,1)S(1)} %get-tuple-element.43), channel_id=1, source_target_pairs={{0,1},{1,0},{2,3},{3,2},{4,5},{5,4},{6,7},{7,6},{8,9},{9,8},{10,11... | collective-permute-start | bytes 4718600 | tf_op jit(solution)/shard_map/ppermute | solution.py:322
  63.0 3.5 %collective-permute-start.15 = (bf16[256,3072]{1,0:T(8,128)(2,1)S(1)}, bf16[256,3072]{1,0:T(8,128)(2,1)S(1)}, u32[]{:S(2)}, u32[]{:S(2)}) collective-permute-start(bf16[256,3072]{1,0:T(8,128)(2,1)S(1)} %get-tuple-element.53), channel_id=1, source_target_pairs={{0,1},{1,0},{2,3},{3,2},{4,5},{5,4},{6,7},{7,6},{8,9},{9,8},{10,11... | collective-permute-start | bytes 4718600 | tf_op jit(solution)/shard_map/ppermute | solution.py:322
  63.5 8.9 %collective-permute-start.10 = (bf16[32,3072]{1,0:T(8,128)(2,1)S(1)}, bf16[32,3072]{1,0:T(8,128)(2,1)S(1)}, u32[]{:S(2)}, u32[]{:S(2)}) collective-permute-start(bf16[32,3072]{1,0:T(8,128)(2,1)S(1)} %get-tuple-element.49), channel_id=1, source_target_pairs={{0,128},{1,129},{2,130},{3,131},{4,132},{5,133},{6,134},{7,135},{8... | collective-permute-start | bytes 589832 | tf_op jit(solution)/shard_map/ppermute | solution.py:322
  64.4 12.0 %collective-permute-start.8 = (bf16[64,3072]{1,0:T(8,128)(2,1)S(1)}, bf16[64,3072]{1,0:T(8,128)(2,1)S(1)}, u32[]{:S(2)}, u32[]{:S(2)}) collective-permute-start(bf16[64,3072]{1,0:T(8,128)(2,1)S(1)} %get-tuple-element.46), channel_id=1, source_target_pairs={{0,32},{1,33},{2,34},{3,35},{4,36},{5,37},{6,38},{7,39},{8,40},{9,... | collective-permute-start | bytes 1179656 | tf_op jit(solution)/shard_map/ppermute | solution.py:322
  65.7 13.4 %collective-permute-start.7 = (bf16[64,3072]{1,0:T(8,128)(2,1)S(1)}, bf16[64,3072]{1,0:T(8,128)(2,1)S(1)}, u32[]{:S(2)}, u32[]{:S(2)}) collective-permute-start(bf16[64,3072]{1,0:T(8,128)(2,1)S(1)} %get-tuple-element.45), channel_id=1, source_target_pairs={{0,96},{1,97},{2,98},{3,99},{4,100},{5,101},{6,102},{7,103},{8,104... | collective-permute-start | bytes 1179656 | tf_op jit(solution)/shard_map/ppermute | solution.py:322
  66.8 18.5 %collective-permute-start.16 = (bf16[64,3072]{1,0:T(8,128)(2,1)S(1)}, bf16[64,3072]{1,0:T(8,128)(2,1)S(1)}, u32[]{:S(2)}, u32[]{:S(2)}) collective-permute-start(bf16[64,3072]{1,0:T(8,128)(2,1)S(1)} %get-tuple-element.55), channel_id=1, source_target_pairs={{0,96},{1,97},{2,98},{3,99},{4,100},{5,101},{6,102},{7,103},{8,104... | collective-permute-start | bytes 1179656 | tf_op jit(solution)/shard_map/ppermute | solution.py:322
  69.0 16.3 %collective-permute-start.17 = (bf16[64,3072]{1,0:T(8,128)(2,1)S(1)}, bf16[64,3072]{1,0:T(8,128)(2,1)S(1)}, u32[]{:S(2)}, u32[]{:S(2)}) collective-permute-start(bf16[64,3072]{1,0:T(8,128)(2,1)S(1)} %get-tuple-element.56), channel_id=1, source_target_pairs={{0,32},{1,33},{2,34},{3,35},{4,36},{5,37},{6,38},{7,39},{8,40},{9,... | collective-permute-start | bytes 1179656 | tf_op jit(solution)/shard_map/ppermute | solution.py:322
  72.3 15.9 %collective-permute-start.19 = (bf16[32,3072]{1,0:T(8,128)(2,1)S(1)}, bf16[32,3072]{1,0:T(8,128)(2,1)S(1)}, u32[]{:S(2)}, u32[]{:S(2)}) collective-permute-start(bf16[32,3072]{1,0:T(8,128)(2,1)S(1)} %get-tuple-element.59), channel_id=1, source_target_pairs={{0,128},{1,129},{2,130},{3,131},{4,132},{5,133},{6,134},{7,135},{8... | collective-permute-start | bytes 589832 | tf_op jit(solution)/shard_map/ppermute | solution.py:322
  76.3 19.0 %collective-permute-start.11 = (bf16[32,3072]{1,0:T(8,128)(2,1)S(1)}, bf16[32,3072]{1,0:T(8,128)(2,1)S(1)}, u32[]{:S(2)}, u32[]{:S(2)}) collective-permute-start(bf16[32,3072]{1,0:T(8,128)(2,1)S(1)} %add_convert_fusion.3), channel_id=1, source_target_pairs={{0,64},{1,65},{2,66},{3,67},{4,68},{5,69},{6,70},{7,71},{8,72},{9,... | collective-permute-start | bytes 589832 | tf_op jit(solution)/shard_map/ppermute | solution.py:322
  79.2 16.1 %collective-permute-start.9 = (bf16[32,3072]{1,0:T(8,128)(2,1)S(1)}, bf16[32,3072]{1,0:T(8,128)(2,1)S(1)}, u32[]{:S(2)}, u32[]{:S(2)}) collective-permute-start(bf16[32,3072]{1,0:T(8,128)(2,1)S(1)} %add_convert_fusion.4), channel_id=1, source_target_pairs={{0,128},{1,129},{2,130},{3,131},{4,132},{5,133},{6,134},{7,135},{8... | collective-permute-start | bytes 589832 | tf_op jit(solution)/shard_map/ppermute | solution.py:322
  85.4 10.2 %collective-permute-start.18 = (bf16[32,3072]{1,0:T(8,128)(2,1)S(1)}, bf16[32,3072]{1,0:T(8,128)(2,1)S(1)}, u32[]{:S(2)}, u32[]{:S(2)}) collective-permute-start(bf16[32,3072]{1,0:T(8,128)(2,1)S(1)} %add_convert_fusion.1), channel_id=1, source_target_pairs={{0,128},{1,129},{2,130},{3,131},{4,132},{5,133},{6,134},{7,135},{8... | collective-permute-start | bytes 589832 | tf_op jit(solution)/shard_map/ppermute | solution.py:322
  88.3 10.6 %collective-permute-start.20 = (bf16[32,3072]{1,0:T(8,128)(2,1)S(1)}, bf16[32,3072]{1,0:T(8,128)(2,1)S(1)}, u32[]{:S(2)}, u32[]{:S(2)}) collective-permute-start(bf16[32,3072]{1,0:T(8,128)(2,1)S(1)} %add_convert_fusion), channel_id=1, source_target_pairs={{0,64},{1,65},{2,66},{3,67},{4,68},{5,69},{6,70},{7,71},{8,72},{9,... | collective-permute-start | bytes 589832 | tf_op jit(solution)/shard_map/ppermute | solution.py:322
  95.6 3.3 %collective-permute-start.21 = (f32[32,1]{1,0:T(8,128)S(1)}, f32[32,1]{1,0:T(8,128)S(1)}, u32[]{:S(2)}, u32[]{:S(2)}) collective-permute-start(f32[32,1]{1,0:T(8,128)S(1)} %copy.10.pair_ref), channel_id=1, source_target_pairs={{0,1},{1,0},{2,3},{3,2},{4,5},{5,4},{6,7},{7,6},{8,9},{9,8},{10,11... | collective-permute-start | bytes 392 | tf_op jit(solution)/shard_map/ppermute | solution.py:322
  99.1 18.5 %copy-start = (s32[4,4]{1,0:T(4,128)S(1)}, s32[4,4]{1,0:T(4,128)}, u32[]{:S(2)}) copy-start(s32[4,4]{1,0:T(4,128)} %ids_ref.3) | copy-start | bytes 196
  99.1 18.5 %copy-start.1 = (f32[4,4]{1,0:T(4,128)S(1)}, f32[4,4]{1,0:T(4,128)}, u32[]{:S(2)}) copy-start(f32[4,4]{1,0:T(4,128)} %weights_ref.3) | copy-start | bytes 196

commit v5 on v4

--- a/solution.py
+++ b/solution.py
@@ -358,16 +358,14 @@
         second_near = (move(second[2], row=-1), move(second[3], row=1))
         second_got = move(second[5], hi=1)
         first_far = move(add(first[4], first_got), row=2)
-        second_got, _ = lax.optimization_barrier((second_got, second_near))
+        first_across = move(add(first[1], first_near[0][r:], first_near[1][r:]), hi=1)
+        second_got, _ = lax.optimization_barrier((second_got, first_across))
         second_far = move(add(second[4], second_got), row=2)
-        results = []
-        for total, near, straight in (
-            (first, first_near, first_far),
-            (second, second_near, second_far),
-        ):
-            across = move(add(total[1], near[0][r:], near[1][r:]), hi=1)
-            results.append((total[0], *near, across, straight))
-        return results
+        second_across = move(add(second[1], second_near[0][r:], second_near[1][r:]), hi=1)
+        return [
+            (first[0], *first_near, first_across, first_far),
+            (second[0], *second_near, second_across, second_far),
+        ]
 
     sent, core = dispatch_rows(
         lax.axis_index("tp"), tokens, expert_ids, combine_weights, cotangent, experts, capacity
@@ -381,7 +379,7 @@
     across, far, gate, down = lax.optimization_barrier((across, far, *load_weights(core, gate, down)))
     pairs = join_rows([[(0, i, r), (1, i, r)] for i in (0, r)], stacked, across)
     token_pair, grad_pair = pairs
-    below, above = zip(*[(move(pair, row=1), move(pair, row=-1)) for pair in pairs])
+    above, below = zip(*[(move(pair, row=-1), move(pair, row=1)) for pair in pairs])
     across_far = move(far, hi=1)
 
     def join_mine(i, after=()):

time: 120 us -> 120 us (level)
  transfers between devices with their start and end apart: 22 -> 22, of which waited for: 10 -> 11; matrix products, arithmetic and copies ran while one was open for 1% -> 1% of each run, Pallas kernels for 13% -> 13%
where the time goes in v5:
time: 120 us; the launch traced here: 119 us
  blocking collectives  40.3 us (34%)
  starting transfers between devices  32.5 us (27%)
  waiting for transfers between devices  25.3 us (21%)
  Pallas kernels  19 us (16%)
    all_to_all x2, blocking collectives, exchange(): got = lax.all_to_all(sent, 'exp', split_axis=0, concat_axis=0, tiled=True)  40.3 us
    ppermute x22, starting transfers between devices, move(): return lax.ppermute(value, AXES, shift_pairs(sizes, **shift))  32.5 us
    ppermute x22, waiting for transfers between devices, move(): return lax.ppermute(value, AXES, shift_pairs(sizes, **shift))  25.3 us
    pallas_call x3, Pallas kernels, expert_call(): pl.pallas_call(kernel, out_shape=tuple((shapes[name] for name in outs)),...  7.4 us
    pallas_call x2, Pallas kernels, load_weights(): pl.pallas_call(load_kernel, out_shape=jax.ShapeDtypeStruct(weight.shape,...  6.96 us
  transfers between devices with their start and end apart: 22, of which 11 were waited for; matrix products, arithmetic and copies ran while one was open for 1% of the time, Pallas kernels for 13%

profile of v5, /device:TPU:8, one launch (start us, length us, event | category | flops | bytes accessed | tf_op | source)
XLA Modules:
  0.0 119.2 jit_solution(3624288258534732967)
XLA Ops:
  0.6 2.0 %shard_map.85 = (bf16[16,2,6144]{2,1,0:T(2,128)(2,1)}, s32[1]{0:T(128)}) custom-call(s32[1]{0:T(128)} %bitcast.core_ref, s32[4,4]{1,0:T(4,128)} %ids_ref.3, f32[4,4]{1,0:T(4,128)} %weights_ref.3, bf16[4,3072]{1,0:T(4,128)(2,1)} %tokens_ref.1, bf16[4,3072]{1,0:T(4,128)(2,1)} %cotangent_ref.1), custom_call_target="tpu_custom_call" | custom-call | tf_op jit(solution)/shard_map/pallas_call | solution.py:248
  2.6 22.1 %all_to_all.10 = bf16[16,2,6144]{2,1,0:T(2,128)(2,1)S(1)} all-to-all(bf16[16,2,6144]{2,1,0:T(2,128)(2,1)} %get-tuple-element.32), channel_id=1, replica_groups=mesh['ctx'=8,'exp'=16,'tp'=2] {'exp'}, dimensions={0} | all-to-all | bytes 786432 | tf_op jit(solution)/shard_map/all_to_all | solution.py:326
  24.9 2.8 %collective-permute-start = (bf16[64,3072]{1,0:T(8,128)(2,1)S(1)}, bf16[64,3072]{1,0:T(8,128)(2,1)S(1)}, u32[]{:S(2)}, u32[]{:S(2)}) collective-permute-start(bf16[64,3072]{1,0:T(8,128)(2,1)S(1)} %pad_maximum_fusion.refs_0_), channel_id=1, source_target_pairs={{0,128},{1,129},{2,130},{3,131},{4,132},{5,133},{6,134},{7,135},{8... | collective-permute-start | bytes 1179656 | tf_op jit(solution)/shard_map/ppermute | solution.py:322
  27.8 2.3 %collective-permute-start.1 = (bf16[64,3072]{1,0:T(8,128)(2,1)S(1)}, bf16[64,3072]{1,0:T(8,128)(2,1)S(1)}, u32[]{:S(2)}, u32[]{:S(2)}) collective-permute-start(bf16[64,3072]{1,0:T(8,128)(2,1)S(1)} %pad_maximum_fusion.refs_0_), channel_id=1, source_target_pairs={{0,64},{1,65},{2,66},{3,67},{4,68},{5,69},{6,70},{7,71},{8,72},{9,... | collective-permute-start | bytes 1179656 | tf_op jit(solution)/shard_map/ppermute | solution.py:322
  30.1 3.5 %shard_map.86.weight_ref.gate_ref = bf16[504,6144]{1,0:T(8,128)(2,1)S(1)} custom-call(s32[1]{0:T(128)} %get-tuple-element.34.core_ref, bf16[504,6144]{1,0:T(8,128)(2,1)} %bitcast.6), custom_call_target="tpu_custom_call" | custom-call | tf_op jit(solution)/shard_map/pallas_call | solution.py:117
  33.5 3.5 %shard_map.87.down_ref = bf16[504,6144]{1,0:T(8,128)(2,1)S(1)} custom-call(s32[1]{0:T(128)} %get-tuple-element.34.core_ref, bf16[504,6144]{1,0:T(8,128)(2,1)} %bitcast.7), custom_call_target="tpu_custom_call" | custom-call | tf_op jit(solution)/shard_map/pallas_call | solution.py:117
  37.0 0.9 collective-permute-done.1.refs_3_
  38.0 2.2 %collective-permute-start.2 = (bf16[64,3072]{1,0:T(8,128)(2,1)S(1)}, bf16[64,3072]{1,0:T(8,128)(2,1)S(1)}, u32[]{:S(2)}, u32[]{:S(2)}) collective-permute-start(bf16[64,3072]{1,0:T(8,128)(2,1)S(1)} %get-tuple-element.38.refs_0_), channel_id=1, source_target_pairs={{0,32},{1,33},{2,34},{3,35},{4,36},{5,37},{6,38},{7,39},{8,40},{9,... | collective-permute-start | bytes 1179656 | tf_op jit(solution)/shard_map/ppermute | solution.py:322
  40.2 0.8 collective-permute-start.4
  41.0 2.0 %collective-permute-start.12 = (bf16[64,3072]{1,0:T(8,128)(2,1)S(1)}, bf16[64,3072]{1,0:T(8,128)(2,1)S(1)}, u32[]{:S(2)}, u32[]{:S(2)}) collective-permute-start(bf16[64,3072]{1,0:T(8,128)(2,1)S(1)} %get-tuple-element.50.refs_0_), channel_id=1, source_target_pairs={{0,32},{1,33},{2,34},{3,35},{4,36},{5,37},{6,38},{7,39},{8,40},{9,... | collective-permute-start | bytes 1179656 | tf_op jit(solution)/shard_map/ppermute | solution.py:322
  43.1 7.1 %collective-permute-done.2.refs_1_ = bf16[64,3072]{1,0:T(8,128)(2,1)S(1)} collective-permute-done((bf16[64,3072]{1,0:T(8,128)(2,1)S(1)}, bf16[64,3072]{1,0:T(8,128)(2,1)S(1)}, u32[]{:S(2)}, u32[]{:S(2)}) %collective-permute-start.2) | collective-permute-done | bytes 393248 | tf_op jit(solution)/shard_map/ppermute | solution.py:322
  50.1 1.2 %collective-permute-done.3.refs_2_ = bf16[64,3072]{1,0:T(8,128)(2,1)S(1)} collective-permute-done((bf16[64,3072]{1,0:T(8,128)(2,1)S(1)}, bf16[64,3072]{1,0:T(8,128)(2,1)S(1)}, u32[]{:S(2)}, u32[]{:S(2)}) %collective-permute-start.3) | collective-permute-done | bytes 393248 | tf_op jit(solution)/shard_map/ppermute | solution.py:322
  51.6 1.0 shard_map.90.partial_ref.refs_5_
  52.6 2.3 %collective-permute-done.12.refs_1_ = bf16[64,3072]{1,0:T(8,128)(2,1)S(1)} collective-permute-done((bf16[64,3072]{1,0:T(8,128)(2,1)S(1)}, bf16[64,3072]{1,0:T(8,128)(2,1)S(1)}, u32[]{:S(2)}, u32[]{:S(2)}) %collective-permute-start.12) | collective-permute-done | bytes 393248 | tf_op jit(solution)/shard_map/ppermute | solution.py:322
  55.8 2.8 %shard_map.91 = (f32[256,504]{1,0:T(8,128)S(1)}, bf16[256,3072]{1,0:T(8,128)(2,1)S(1)}, bf16[256,3072]{1,0:T(8,128)(2,1)S(1)}) custom-call(f32[256,504]{1,0:T(8,128)S(1)} %shard_map.90.partial_ref.refs_5_, bf16[256,3072]{1,0:T(8,128)(2,1)S(1)} %collective-permute-done.5.other_ref, bf16[504,6144]{1,0:T(8,128)(2,1)S(1)} %shard_map.86.weight_ref.gate_ref, ...), custom_call_target="tpu_custom_call" | custom-call | flops 2378170368 | bytes 4644864 | tf_op jit(solution)/shard_map/pallas_call | solution.py:81
  58.6 0.8 collective-permute-start.6
  59.4 3.6 %shard_map.94 = (bf16[256,3072]{1,0:T(8,128)(2,1)S(1)}, bf16[256,3072]{1,0:T(8,128)(2,1)S(1)}) custom-call(bf16[256,3072]{1,0:T(8,128)(2,1)S(1)} %shard_map.93.mine_ref, bf16[256,3072]{1,0:T(8,128)(2,1)S(1)} %collective-permute-done.14.other_ref, bf16[504,6144]{1,0:T(8,128)(2,1)S(1)} %shard_map.87.down_ref, ...), custom_call_target="tpu_custom_call" | custom-call | flops 3170893824 | bytes 6193152 | tf_op jit(solution)/shard_map/pallas_call | solution.py:81
  63.5 0.9 collective-permute-start.10
  64.4 1.3 %collective-permute-start.8 = (bf16[64,3072]{1,0:T(8,128)(2,1)S(1)}, bf16[64,3072]{1,0:T(8,128)(2,1)S(1)}, u32[]{:S(2)}, u32[]{:S(2)}) collective-permute-start(bf16[64,3072]{1,0:T(8,128)(2,1)S(1)} %get-tuple-element.46), channel_id=1, source_target_pairs={{0,32},{1,33},{2,34},{3,35},{4,36},{5,37},{6,38},{7,39},{8,40},{9,... | collective-permute-start | bytes 1179656 | tf_op jit(solution)/shard_map/ppermute | solution.py:322
  66.8 2.2 %collective-permute-start.16 = (bf16[64,3072]{1,0:T(8,128)(2,1)S(1)}, bf16[64,3072]{1,0:T(8,128)(2,1)S(1)}, u32[]{:S(2)}, u32[]{:S(2)}) collective-permute-start(bf16[64,3072]{1,0:T(8,128)(2,1)S(1)} %get-tuple-element.55), channel_id=1, source_target_pairs={{0,96},{1,97},{2,98},{3,99},{4,100},{5,101},{6,102},{7,103},{8,104... | collective-permute-start | bytes 1179656 | tf_op jit(solution)/shard_map/ppermute | solution.py:322
  69.0 3.3 %collective-permute-done.10 = bf16[32,3072]{1,0:T(8,128)(2,1)S(1)} collective-permute-done((bf16[32,3072]{1,0:T(8,128)(2,1)S(1)}, bf16[32,3072]{1,0:T(8,128)(2,1)S(1)}, u32[]{:S(2)}, u32[]{:S(2)}) %collective-permute-start.10) | collective-permute-done | bytes 196640 | tf_op jit(solution)/shard_map/ppermute | solution.py:322
  72.3 0.8 collective-permute-start.19
  73.2 3.1 %collective-permute-done.8 = bf16[64,3072]{1,0:T(8,128)(2,1)S(1)} collective-permute-done((bf16[64,3072]{1,0:T(8,128)(2,1)S(1)}, bf16[64,3072]{1,0:T(8,128)(2,1)S(1)}, u32[]{:S(2)}, u32[]{:S(2)}) %collective-permute-start.8) | collective-permute-done | bytes 393248 | tf_op jit(solution)/shard_map/ppermute | solution.py:322
  76.3 2.8 %collective-permute-start.11 = (bf16[32,3072]{1,0:T(8,128)(2,1)S(1)}, bf16[32,3072]{1,0:T(8,128)(2,1)S(1)}, u32[]{:S(2)}, u32[]{:S(2)}) collective-permute-start(bf16[32,3072]{1,0:T(8,128)(2,1)S(1)} %add_convert_fusion.3), channel_id=1, source_target_pairs={{0,64},{1,65},{2,66},{3,67},{4,68},{5,69},{6,70},{7,71},{8,72},{9,... | collective-permute-start | bytes 589832 | tf_op jit(solution)/shard_map/ppermute | solution.py:322
  79.2 2.8 %collective-permute-start.9 = (bf16[32,3072]{1,0:T(8,128)(2,1)S(1)}, bf16[32,3072]{1,0:T(8,128)(2,1)S(1)}, u32[]{:S(2)}, u32[]{:S(2)}) collective-permute-start(bf16[32,3072]{1,0:T(8,128)(2,1)S(1)} %add_convert_fusion.4), channel_id=1, source_target_pairs={{0,128},{1,129},{2,130},{3,131},{4,132},{5,133},{6,134},{7,135},{8... | collective-permute-start | bytes 589832 | tf_op jit(solution)/shard_map/ppermute | solution.py:322
  82.0 3.3 %collective-permute-done.16.below = bf16[64,3072]{1,0:T(8,128)(2,1)S(1)} collective-permute-done((bf16[64,3072]{1,0:T(8,128)(2,1)S(1)}, bf16[64,3072]{1,0:T(8,128)(2,1)S(1)}, u32[]{:S(2)}, u32[]{:S(2)}) %collective-permute-start.16) | collective-permute-done | bytes 393248 | tf_op jit(solution)/shard_map/ppermute | solution.py:322
  85.4 2.8 %collective-permute-start.18 = (bf16[32,3072]{1,0:T(8,128)(2,1)S(1)}, bf16[32,3072]{1,0:T(8,128)(2,1)S(1)}, u32[]{:S(2)}, u32[]{:S(2)}) collective-permute-start(bf16[32,3072]{1,0:T(8,128)(2,1)S(1)} %add_convert_fusion.1), channel_id=1, source_target_pairs={{0,128},{1,129},{2,130},{3,131},{4,132},{5,133},{6,134},{7,135},{8... | collective-permute-start | bytes 589832 | tf_op jit(solution)/shard_map/ppermute | solution.py:322
  88.3 7.0 %collective-permute-start.20 = (bf16[32,3072]{1,0:T(8,128)(2,1)S(1)}, bf16[32,3072]{1,0:T(8,128)(2,1)S(1)}, u32[]{:S(2)}, u32[]{:S(2)}) collective-permute-start(bf16[32,3072]{1,0:T(8,128)(2,1)S(1)} %add_convert_fusion), channel_id=1, source_target_pairs={{0,64},{1,65},{2,66},{3,67},{4,68},{5,69},{6,70},{7,71},{8,72},{9,... | collective-permute-start | bytes 589832 | tf_op jit(solution)/shard_map/ppermute | solution.py:322
  95.7 1.2 collective-permute-done.21.moved_ref
  96.8 2.1 %collective-permute-done.20.straight = bf16[32,3072]{1,0:T(8,128)(2,1)S(1)} collective-permute-done((bf16[32,3072]{1,0:T(8,128)(2,1)S(1)}, bf16[32,3072]{1,0:T(8,128)(2,1)S(1)}, u32[]{:S(2)}, u32[]{:S(2)}) %collective-permute-start.20) | collective-permute-done | bytes 196640 | tf_op jit(solution)/shard_map/ppermute | solution.py:322
  99.2 18.2 %all_to_all.11 = bf16[16,2,6272]{2,1,0:T(2,128)(2,1)S(1)} all-to-all(bf16[16,2,6272]{2,1,0:T(2,128)(2,1)S(1)} %reshape.20), channel_id=1, replica_groups=mesh['ctx'=8,'exp'=16,'tp'=2] {'exp'}, dimensions={0} | all-to-all | bytes 802816 | tf_op jit(solution)/shard_map/all_to_all | solution.py:326
  117.6 1.6 %shard_map.97 = (bf16[4,3072]{1,0:T(4,128)(2,1)}, bf16[4,3072]{1,0:T(4,128)(2,1)}, f32[4,4]{1,0:T(4,128)}) custom-call(s32[4,4]{1,0:T(4,128)S(1)} %copy-done, f32[4,4]{1,0:T(4,128)S(1)} %copy-done.1, bf16[32,6272]{1,0:T(8,128)(2,1)S(1)} %reshape.21.returned_ref), custom_call_target="tpu_custom_call" | custom-call | tf_op jit(solution)/shard_map/pallas_call | solution.py:304
  (42 shorter events, 4.0 us)
Async XLA Ops:
  24.9 12.1 %collective-permute-start = (bf16[64,3072]{1,0:T(8,128)(2,1)S(1)}, bf16[64,3072]{1,0:T(8,128)(2,1)S(1)}, u32[]{:S(2)}, u32[]{:S(2)}) collective-permute-start(bf16[64,3072]{1,0:T(8,128)(2,1)S(1)} %pad_maximum_fusion.refs_0_), channel_id=1, source_target_pairs={{0,128},{1,129},{2,130},{3,131},{4,132},{5,133},{6,134},{7,135},{8... | collective-permute-start | bytes 1179656 | tf_op jit(solution)/shard_map/ppermute | solution.py:322
  27.8 10.2 %collective-permute-start.1 = (bf16[64,3072]{1,0:T(8,128)(2,1)S(1)}, bf16[64,3072]{1,0:T(8,128)(2,1)S(1)}, u32[]{:S(2)}, u32[]{:S(2)}) collective-permute-start(bf16[64,3072]{1,0:T(8,128)(2,1)S(1)} %pad_maximum_fusion.refs_0_), channel_id=1, source_target_pairs={{0,64},{1,65},{2,66},{3,67},{4,68},{5,69},{6,70},{7,71},{8,72},{9,... | collective-permute-start | bytes 1179656 | tf_op jit(solution)/shard_map/ppermute | solution.py:322
  38.0 12.1 %collective-permute-start.2 = (bf16[64,3072]{1,0:T(8,128)(2,1)S(1)}, bf16[64,3072]{1,0:T(8,128)(2,1)S(1)}, u32[]{:S(2)}, u32[]{:S(2)}) collective-permute-start(bf16[64,3072]{1,0:T(8,128)(2,1)S(1)} %get-tuple-element.38.refs_0_), channel_id=1, source_target_pairs={{0,32},{1,33},{2,34},{3,35},{4,36},{5,37},{6,38},{7,39},{8,40},{9,... | collective-permute-start | bytes 1179656 | tf_op jit(solution)/shard_map/ppermute | solution.py:322
  40.2 11.2 %collective-permute-start.3 = (bf16[64,3072]{1,0:T(8,128)(2,1)S(1)}, bf16[64,3072]{1,0:T(8,128)(2,1)S(1)}, u32[]{:S(2)}, u32[]{:S(2)}) collective-permute-start(bf16[64,3072]{1,0:T(8,128)(2,1)S(1)} %get-tuple-element.38.refs_0_), channel_id=1, source_target_pairs={{0,96},{1,97},{2,98},{3,99},{4,100},{5,101},{6,102},{7,103},{8,104... | collective-permute-start | bytes 1179656 | tf_op jit(solution)/shard_map/ppermute | solution.py:322
  40.2 11.2 %collective-permute-start.4 = (bf16[64,3072]{1,0:T(8,128)(2,1)S(1)}, bf16[64,3072]{1,0:T(8,128)(2,1)S(1)}, u32[]{:S(2)}, u32[]{:S(2)}) collective-permute-start(bf16[64,3072]{1,0:T(8,128)(2,1)S(1)} %collective-permute-done.1.refs_3_), channel_id=1, source_target_pairs={{0,128},{1,129},{2,130},{3,131},{4,132},{5,133},{6,134},{7,135},{8... | collective-permute-start | bytes 1179656 | tf_op jit(solution)/shard_map/ppermute | solution.py:322
  41.0 13.9 %collective-permute-start.12 = (bf16[64,3072]{1,0:T(8,128)(2,1)S(1)}, bf16[64,3072]{1,0:T(8,128)(2,1)S(1)}, u32[]{:S(2)}, u32[]{:S(2)}) collective-permute-start(bf16[64,3072]{1,0:T(8,128)(2,1)S(1)} %get-tuple-element.50.refs_0_), channel_id=1, source_target_pairs={{0,32},{1,33},{2,34},{3,35},{4,36},{5,37},{6,38},{7,39},{8,40},{9,... | collective-permute-start | bytes 1179656 | tf_op jit(solution)/shard_map/ppermute | solution.py:322
  43.1 12.5 %collective-permute-start.13 = (bf16[64,3072]{1,0:T(8,128)(2,1)S(1)}, bf16[64,3072]{1,0:T(8,128)(2,1)S(1)}, u32[]{:S(2)}, u32[]{:S(2)}) collective-permute-start(bf16[64,3072]{1,0:T(8,128)(2,1)S(1)} %get-tuple-element.50.refs_0_), channel_id=1, source_target_pairs={{0,96},{1,97},{2,98},{3,99},{4,100},{5,101},{6,102},{7,103},{8,104... | collective-permute-start | bytes 1179656 | tf_op jit(solution)/shard_map/ppermute | solution.py:322
  51.5 4.3 %collective-permute-start.5 = (bf16[256,3072]{1,0:T(8,128)(2,1)S(1)}, bf16[256,3072]{1,0:T(8,128)(2,1)S(1)}, u32[]{:S(2)}, u32[]{:S(2)}) collective-permute-start(bf16[256,3072]{1,0:T(8,128)(2,1)S(1)} %shard_map.89.rows_ref), channel_id=1, source_target_pairs={{0,1},{1,0},{2,3},{3,2},{4,5},{5,4},{6,7},{7,6},{8,9},{9,8},{10,11... | collective-permute-start | bytes 4718600 | tf_op jit(solution)/shard_map/ppermute | solution.py:322
  55.7 3.7 %collective-permute-start.14 = (bf16[256,3072]{1,0:T(8,128)(2,1)S(1)}, bf16[256,3072]{1,0:T(8,128)(2,1)S(1)}, u32[]{:S(2)}, u32[]{:S(2)}) collective-permute-start(bf16[256,3072]{1,0:T(8,128)(2,1)S(1)} %shard_map.93.mine_ref), channel_id=1, source_target_pairs={{0,1},{1,0},{2,3},{3,2},{4,5},{5,4},{6,7},{7,6},{8,9},{9,8},{10,11... | collective-permute-start | bytes 4718600 | tf_op jit(solution)/shard_map/ppermute | solution.py:322
  58.6 4.5 %collective-permute-start.6 = (bf16[256,3072]{1,0:T(8,128)(2,1)S(1)}, bf16[256,3072]{1,0:T(8,128)(2,1)S(1)}, u32[]{:S(2)}, u32[]{:S(2)}) collective-permute-start(bf16[256,3072]{1,0:T(8,128)(2,1)S(1)} %get-tuple-element.43), channel_id=1, source_target_pairs={{0,1},{1,0},{2,3},{3,2},{4,5},{5,4},{6,7},{7,6},{8,9},{9,8},{10,11... | collective-permute-start | bytes 4718600 | tf_op jit(solution)/shard_map/ppermute | solution.py:322
  63.0 3.5 %collective-permute-start.15 = (bf16[256,3072]{1,0:T(8,128)(2,1)S(1)}, bf16[256,3072]{1,0:T(8,128)(2,1)S(1)}, u32[]{:S(2)}, u32[]{:S(2)}) collective-permute-start(bf16[256,3072]{1,0:T(8,128)(2,1)S(1)} %get-tuple-element.53), channel_id=1, source_target_pairs={{0,1},{1,0},{2,3},{3,2},{4,5},{5,4},{6,7},{7,6},{8,9},{9,8},{10,11... | collective-permute-start | bytes 4718600 | tf_op jit(solution)/shard_map/ppermute | solution.py:322
  63.5 8.9 %collective-permute-start.10 = (bf16[32,3072]{1,0:T(8,128)(2,1)S(1)}, bf16[32,3072]{1,0:T(8,128)(2,1)S(1)}, u32[]{:S(2)}, u32[]{:S(2)}) collective-permute-start(bf16[32,3072]{1,0:T(8,128)(2,1)S(1)} %get-tuple-element.49), channel_id=1, source_target_pairs={{0,128},{1,129},{2,130},{3,131},{4,132},{5,133},{6,134},{7,135},{8... | collective-permute-start | bytes 589832 | tf_op jit(solution)/shard_map/ppermute | solution.py:322
  64.4 12.0 %collective-permute-start.8 = (bf16[64,3072]{1,0:T(8,128)(2,1)S(1)}, bf16[64,3072]{1,0:T(8,128)(2,1)S(1)}, u32[]{:S(2)}, u32[]{:S(2)}) collective-permute-start(bf16[64,3072]{1,0:T(8,128)(2,1)S(1)} %get-tuple-element.46), channel_id=1, source_target_pairs={{0,32},{1,33},{2,34},{3,35},{4,36},{5,37},{6,38},{7,39},{8,40},{9,... | collective-permute-start | bytes 1179656 | tf_op jit(solution)/shard_map/ppermute | solution.py:322
  65.7 13.4 %collective-permute-start.7 = (bf16[64,3072]{1,0:T(8,128)(2,1)S(1)}, bf16[64,3072]{1,0:T(8,128)(2,1)S(1)}, u32[]{:S(2)}, u32[]{:S(2)}) collective-permute-start(bf16[64,3072]{1,0:T(8,128)(2,1)S(1)} %get-tuple-element.45), channel_id=1, source_target_pairs={{0,96},{1,97},{2,98},{3,99},{4,100},{5,101},{6,102},{7,103},{8,104... | collective-permute-start | bytes 1179656 | tf_op jit(solution)/shard_map/ppermute | solution.py:322
  66.8 18.5 %collective-permute-start.16 = (bf16[64,3072]{1,0:T(8,128)(2,1)S(1)}, bf16[64,3072]{1,0:T(8,128)(2,1)S(1)}, u32[]{:S(2)}, u32[]{:S(2)}) collective-permute-start(bf16[64,3072]{1,0:T(8,128)(2,1)S(1)} %get-tuple-element.55), channel_id=1, source_target_pairs={{0,96},{1,97},{2,98},{3,99},{4,100},{5,101},{6,102},{7,103},{8,104... | collective-permute-start | bytes 1179656 | tf_op jit(solution)/shard_map/ppermute | solution.py:322
  69.0 16.3 %collective-permute-start.17 = (bf16[64,3072]{1,0:T(8,128)(2,1)S(1)}, bf16[64,3072]{1,0:T(8,128)(2,1)S(1)}, u32[]{:S(2)}, u32[]{:S(2)}) collective-permute-start(bf16[64,3072]{1,0:T(8,128)(2,1)S(1)} %get-tuple-element.56), channel_id=1, source_target_pairs={{0,32},{1,33},{2,34},{3,35},{4,36},{5,37},{6,38},{7,39},{8,40},{9,... | collective-permute-start | bytes 1179656 | tf_op jit(solution)/shard_map/ppermute | solution.py:322
  72.3 15.9 %collective-permute-start.19 = (bf16[32,3072]{1,0:T(8,128)(2,1)S(1)}, bf16[32,3072]{1,0:T(8,128)(2,1)S(1)}, u32[]{:S(2)}, u32[]{:S(2)}) collective-permute-start(bf16[32,3072]{1,0:T(8,128)(2,1)S(1)} %get-tuple-element.59), channel_id=1, source_target_pairs={{0,128},{1,129},{2,130},{3,131},{4,132},{5,133},{6,134},{7,135},{8... | collective-permute-start | bytes 589832 | tf_op jit(solution)/shard_map/ppermute | solution.py:322
  76.3 19.0 %collective-permute-start.11 = (bf16[32,3072]{1,0:T(8,128)(2,1)S(1)}, bf16[32,3072]{1,0:T(8,128)(2,1)S(1)}, u32[]{:S(2)}, u32[]{:S(2)}) collective-permute-start(bf16[32,3072]{1,0:T(8,128)(2,1)S(1)} %add_convert_fusion.3), channel_id=1, source_target_pairs={{0,64},{1,65},{2,66},{3,67},{4,68},{5,69},{6,70},{7,71},{8,72},{9,... | collective-permute-start | bytes 589832 | tf_op jit(solution)/shard_map/ppermute | solution.py:322
  79.2 9.1 %collective-permute-start.9 = (bf16[32,3072]{1,0:T(8,128)(2,1)S(1)}, bf16[32,3072]{1,0:T(8,128)(2,1)S(1)}, u32[]{:S(2)}, u32[]{:S(2)}) collective-permute-start(bf16[32,3072]{1,0:T(8,128)(2,1)S(1)} %add_convert_fusion.4), channel_id=1, source_target_pairs={{0,128},{1,129},{2,130},{3,131},{4,132},{5,133},{6,134},{7,135},{8... | collective-permute-start | bytes 589832 | tf_op jit(solution)/shard_map/ppermute | solution.py:322
  85.4 10.2 %collective-permute-start.18 = (bf16[32,3072]{1,0:T(8,128)(2,1)S(1)}, bf16[32,3072]{1,0:T(8,128)(2,1)S(1)}, u32[]{:S(2)}, u32[]{:S(2)}) collective-permute-start(bf16[32,3072]{1,0:T(8,128)(2,1)S(1)} %add_convert_fusion.1), channel_id=1, source_target_pairs={{0,128},{1,129},{2,130},{3,131},{4,132},{5,133},{6,134},{7,135},{8... | collective-permute-start | bytes 589832 | tf_op jit(solution)/shard_map/ppermute | solution.py:322
  88.3 10.6 %collective-permute-start.20 = (bf16[32,3072]{1,0:T(8,128)(2,1)S(1)}, bf16[32,3072]{1,0:T(8,128)(2,1)S(1)}, u32[]{:S(2)}, u32[]{:S(2)}) collective-permute-start(bf16[32,3072]{1,0:T(8,128)(2,1)S(1)} %add_convert_fusion), channel_id=1, source_target_pairs={{0,64},{1,65},{2,66},{3,67},{4,68},{5,69},{6,70},{7,71},{8,72},{9,... | collective-permute-start | bytes 589832 | tf_op jit(solution)/shard_map/ppermute | solution.py:322
  95.6 1.2 collective-permute-start.21
  99.1 18.6 %copy-start = (s32[4,4]{1,0:T(4,128)S(1)}, s32[4,4]{1,0:T(4,128)}, u32[]{:S(2)}) copy-start(s32[4,4]{1,0:T(4,128)} %ids_ref.3) | copy-start | bytes 196
  99.1 18.5 %copy-start.1 = (f32[4,4]{1,0:T(4,128)S(1)}, f32[4,4]{1,0:T(4,128)}, u32[]{:S(2)}) copy-start(f32[4,4]{1,0:T(4,128)} %weights_ref.3) | copy-start | bytes 196
